TPU v7x, 256 devices: a whole 4x4x8 slice. The times are simulated.
256 devices in a mesh: ctx: 64 (over x, z, core), tp: 4 (over y).
Axes of the slice: x: 4, y: 4, z: 8, core: 2. Of those that a mesh axis runs over, the one named last changes fastest.
Arguments:
- tokens: bfloat16 [24576, 5120], P('ctx', 'tp'), may hold values from -6 to 6
- input_gain: float32 [5120], replicated, may hold values from 0.5 to 1.5
- w_query: bfloat16 [5120, 2560], P('ctx', 'tp'), may hold values from -0.078125 to 0.078125
- w_key: bfloat16 [5120, 512], P('ctx', 'tp'), may hold values from -0.078125 to 0.078125
- w_value: bfloat16 [5120, 512], P('ctx', 'tp'), may hold values from -0.078125 to 0.078125
- query_bias: float32 [2560], P('tp'), may hold values from -8 to 8
- key_bias: float32 [512], P('tp'), may hold values from -8 to 8
- value_bias: float32 [512], P('tp'), may hold values from -3 to 3
- w_out: bfloat16 [2560, 5120], P('tp', 'ctx'), may hold values from -0.125 to 0.125
- final_gain: float32 [5120], P('tp'), may hold values from 0.5 to 1.5
- critic_head: float32 [5120], P('tp'), may hold values from -0.078125 to 0.078125
- critic_bias: float32 [1], replicated, may hold values from -1 to 1
- rewards: int32 [24576], P('ctx'), may hold values from -4 to 4
- turn_ends: int32 [24576], P('ctx'), may hold values 0 or 1
- episode_done: int32 [24576], P('ctx'), may hold values 0 or 1
Outputs:
- residual_stream: bfloat16 [24576, 5120], P('ctx', 'tp')
- values: float32 [24576], P('ctx')
- advantages: float32 [24576], P('ctx')
All inputs are finite; a program needn't handle non-finite values. No bound on the sum of `turn_ends` or of `episode_done` on one device may be relied on, other than what follows from the above.
Results may differ from a plain program's by a relative error of at most 0.013.
The roundings to bfloat16 on the way count: a program that leaves them out, or rounds other values in their place, can miss the bound.
Values may be sent and summed in bfloat16 or wider, within the bound.
No kernel may reach another device: no remote copies, remote signals or barrier semaphores. Data moves between devices by JAX's collectives and lax.ppermute only.
A program may use at most 64 MiB of HBM per device.

v0:
```python
import jax
import jax.numpy as jnp
from jax import lax
from jax.sharding import PartitionSpec as P

D = 5120
HD = 128


EPS = 1e-06
GAMMA = 0.99
LAMBDA = 0.95
ROPE_BASE = 1000000.0
REWARD_SCALE = 0.25


def from_root(x, axis, root):
    mine = lax.axis_index(axis) == root
    return lax.psum(jnp.where(mine, x, jnp.zeros_like(x)), axis)


def passed_along(block, axis, distance):
    devices = range(lax.axis_size(axis))
    route = [(i - distance, i) for i in devices if i - distance in devices]
    return lax.ppermute(block, axis, route)


def prefix(x, axis, combine, identity):
    length, here = (lax.axis_size(axis), lax.axis_index(axis))
    everything = jax.tree.map(lambda part: lax.all_gather(part, axis), x)
    start = jax.tree.map(
        lambda part, zero: jnp.broadcast_to(jnp.asarray(zero, part.dtype), part.shape), x, identity
    )

    def lap(k, before):
        at = length - 1 - k
        reached = at > here
        new = combine(before, jax.tree.map(lambda part: part[at], everything))
        return jax.tree.map(lambda a, b: jnp.where(reached, a, b), new, before)

    return lax.fori_loop(0, length, lap, start)


def rotary(values, positions):
    half = values.shape[-1] // 2
    steps = jnp.arange(half).astype(jnp.float32)
    inverse = 1.0 / ROPE_BASE ** (steps * 2.0 / values.shape[-1])
    angle = positions.astype(jnp.float32)[:, None] * inverse[None, :]
    cosine = jnp.cos(angle)[:, None, :]
    sine = jnp.sin(angle)[:, None, :]
    first = values[..., :half]
    second = values[..., half:]
    return jnp.concatenate(
        [first * cosine - second * sine, second * cosine + first * sine], axis=-1
    )


def compose(earlier, later):
    return (later[0] * earlier[0], later[1] + later[0] * earlier[1])


def on_device(
    tokens,
    input_gain,
    w_query,
    w_key,
    w_value,
    query_bias,
    key_bias,
    value_bias,
    w_out,
    final_gain,
    critic_head,
    critic_bias,
    rewards,
    turn_ends,
    episode_done,
):
    index = lax.axis_index("ctx")
    whole = lax.all_gather(tokens, "tp", axis=1, tiled=True)
    rows = whole.shape[0]
    xfull = whole.astype(jnp.float32)
    normed = (
        xfull * lax.rsqrt(jnp.mean(xfull * xfull, axis=-1, keepdims=True) + EPS) * input_gain
    ).astype(jnp.bfloat16)

    def add_rows(piece):
        return jnp.dot(normed, piece, preferred_element_type=jnp.float32)

    query = add_rows(lax.all_gather(w_query, "ctx", axis=0, tiled=True))
    keys = add_rows(lax.all_gather(w_key, "ctx", axis=0, tiled=True))
    vals = add_rows(lax.all_gather(w_value, "ctx", axis=0, tiled=True))
    q_heads = query.shape[1] // HD
    kv_heads = keys.shape[1] // HD
    group = q_heads // kv_heads
    positions = index * rows + jnp.arange(rows)
    query = (
        rotary((query + query_bias).reshape(rows, q_heads, HD), positions)
        .astype(jnp.bfloat16)
        .reshape(rows, kv_heads, group, HD)
    )
    keys = rotary((keys + key_bias).reshape(rows, kv_heads, HD), positions).astype(jnp.bfloat16)
    vals = (vals + value_bias).astype(jnp.bfloat16).reshape(rows, kv_heads, HD)
    anchor_keys, anchor_vals = (from_root(keys, "ctx", 0), from_root(vals, "ctx", 0))
    scale = HD ** (-0.5)
    causal = jnp.arange(rows)[:, None] >= jnp.arange(rows)[None, :]
    s_anchor = (
        jnp.einsum("tkgd,skd->kgts", query, anchor_keys, preferred_element_type=jnp.float32) * scale
    )
    s_anchor = jnp.where(index > 0, s_anchor, -jnp.inf)
    s_local = jnp.einsum("tkgd,skd->kgts", query, keys, preferred_element_type=jnp.float32) * scale
    s_local = jnp.where(causal, s_local, -jnp.inf)
    peak = jnp.maximum(jnp.max(s_anchor, axis=-1), jnp.max(s_local, axis=-1))
    p_anchor = jnp.exp(s_anchor - peak[..., None])
    p_local = jnp.exp(s_local - peak[..., None])
    total = jnp.sum(p_anchor, axis=-1) + jnp.sum(p_local, axis=-1)
    mixed = jnp.einsum(
        "kgts,skd->tkgd",
        p_anchor.astype(jnp.bfloat16),
        anchor_vals,
        preferred_element_type=jnp.float32,
    )
    mixed = mixed + jnp.einsum(
        "kgts,skd->tkgd", p_local.astype(jnp.bfloat16), vals, preferred_element_type=jnp.float32
    )
    mixed = mixed / jnp.transpose(total, (2, 0, 1))[..., None]
    attended = mixed.astype(jnp.bfloat16).reshape(rows, q_heads * HD)
    partial_sums = jnp.dot(
        attended,
        lax.all_gather(w_out, "ctx", axis=1, tiled=True),
        preferred_element_type=jnp.float32,
    )
    shared = lax.psum_scatter(
        partial_sums.astype(jnp.bfloat16), "tp", scatter_dimension=1, tiled=True
    ).astype(jnp.float32)
    resid = tokens.astype(jnp.float32) + shared
    residual_stream = resid.astype(jnp.bfloat16)
    squares, products = lax.psum(
        (jnp.sum(resid * resid, axis=-1), jnp.sum(resid * final_gain * critic_head, axis=-1)), "tp"
    )
    values = products * lax.rsqrt(squares / D + EPS) + critic_bias[0]
    following = passed_along(values[:1], "ctx", -1)
    next_values = jnp.concatenate([values[1:], following])
    ends = jnp.maximum(turn_ends, episode_done)
    discount = jnp.where(ends > 0, GAMMA, 1.0).astype(jnp.float32)
    keep = (1 - episode_done).astype(jnp.float32)
    reward = REWARD_SCALE * (rewards * ends).astype(jnp.float32)
    delta = reward + discount * keep * next_values - values
    decaying = ends * (1 - episode_done)
    zero_int = jnp.zeros((1,), jnp.int32)
    decay_count = jnp.concatenate([zero_int, jnp.cumsum(decaying)])
    done_count = jnp.concatenate([zero_int, jnp.cumsum(episode_done)])
    rate = GAMMA * LAMBDA
    later = jnp.arange(rows)[None, :] >= jnp.arange(rows)[:, None]
    same_episode = done_count[None, :rows] == done_count[:rows, None]
    powers = (decay_count[None, :rows] - decay_count[:rows, None]).astype(jnp.float32)
    matrix = jnp.where(later & same_episode, jnp.power(rate, powers), 0.0)
    local_adv = jnp.dot(matrix, delta, precision=lax.Precision.HIGHEST)
    tail_powers = (decay_count[rows] - decay_count[:rows]).astype(jnp.float32)
    tail = jnp.where(done_count[rows] == done_count[:rows], jnp.power(rate, tail_powers), 0.0)
    identity = (jnp.ones((1,), jnp.float32), jnp.zeros((1,), jnp.float32))
    decays, carry = prefix((tail[:1], local_adv[:1]), "ctx", compose, identity)
    advantages = local_adv + tail * carry
    return (residual_stream, values, advantages)


def solution(mesh):
    in_specs = (
        P("ctx", "tp"),
        P(),
        P("ctx", "tp"),
        P("ctx", "tp"),
        P("ctx", "tp"),
        P("tp"),
        P("tp"),
        P("tp"),
        P("tp", "ctx"),
        P("tp"),
        P("tp"),
        P(),
        P("ctx"),
        P("ctx"),
        P("ctx"),
    )
    out_specs = (P("ctx", "tp"), P("ctx"), P("ctx"))
    return jax.shard_map(
        on_device, mesh=mesh, in_specs=in_specs, out_specs=out_specs, check_vma=False
    )
```

profile of v0, /device:TPU:1, one launch (start us, length us, event | category | flops | bytes accessed | tf_op | source)
XLA Modules:
  0.0 886.9 jit_solution(8594790156812096538)
XLA Ops:
  7.2 0.7 all-gather.8.cloned.1.call-update
  8.0 0.7 all-gather.12.cloned.1.call-update
  10.1 52.2 %all-gather.8.cloned.1.call-done = bf16[384,5120]{1,0:T(8,128)(2,1)} async-done(((bf16[384,1280]{1,0:T(8,128)(2,1)}), bf16[384,5120]{1,0:T(8,128)(2,1)}) %all-gather.8.cloned.1.call-update) | async-done | bytes 3932176 | tf_op jit(solution)/shard_map/all_gather | solution.py:80
  62.3 3.0 fusion
  65.3 77.1 %all-gather.12.cloned.1.call-done = bf16[5120,128]{1,0:T(8,128)(2,1)} async-done(((bf16[80,128]{1,0:T(8,128)(2,1)}), bf16[5120,128]{1,0:T(8,128)(2,1)}) %all-gather.12.cloned.1.call-update) | async-done | bytes 1310736 | tf_op jit(solution)/shard_map/all_gather | solution.py:91
  142.4 4.0 fusion.30
  148.2 71.4 %all-gather.10.cloned.1.call-done = bf16[5120,128]{1,0:T(8,128)(2,1)} async-done(((bf16[80,128]{1,0:T(8,128)(2,1)}), bf16[5120,128]{1,0:T(8,128)(2,1)}) %all-gather.10.cloned.1.call-update) | async-done | bytes 1310736 | tf_op jit(solution)/shard_map/all_gather | solution.py:92
  219.5 4.5 broadcast_select_fusion
  224.8 0.7 iota_compare_fusion.1
  225.5 0.8 multiply_cosine_fusion
  226.3 75.0 %all-gather.14.cloned.1.call-done = bf16[5120,640]{1,0:T(8,128)(2,1)} async-done(((bf16[80,640]{1,0:T(8,128)(2,1)}), bf16[5120,640]{1,0:T(8,128)(2,1)}) %all-gather.14.cloned.1.call-update) | async-done | bytes 6553616 | tf_op jit(solution)/shard_map/all_gather | solution.py:90
  301.3 7.3 convolution_add_fusion
  310.0 167.8 %all-reduce.7.cloned.1.call-done = (bf16[384,128]{0,1:T(8,128)(2,1)}, bf16[384,128]{1,0:T(8,128)(2,1)}) async-done(((bf16[384,128]{0,1:T(8,128)(2,1)}, bf16[384,128]{1,0:T(8,128)(2,1)}), (bf16[384,128]{0,1:T(8,128)(2,1)}, bf16[384,128]{1,0:T(8,128)(2,1)})) %all-reduce.7.cloned.1.call-update) | async-done | bytes 196624 | tf_op jit(solution)/shard_map/psum | solution.py:19
  477.7 1.6 bitcast_reduce_fusion
  479.4 0.9 fusion.8
  480.3 1.2 fusion.4
  481.5 0.8 fusion.11
  482.4 0.9 divide_convert_fusion
  483.3 79.0 %all-gather.16.cloned.1.call-done = bf16[640,5120]{0,1:T(8,128)(2,1)} async-done(((bf16[640,80]{0,1:T(8,128)(2,1)}), bf16[640,5120]{0,1:T(8,128)(2,1)}) %all-gather.16.cloned.1.call-update) | async-done | bytes 6553616 | tf_op jit(solution)/shard_map/all_gather | solution.py:130
  562.3 8.2 convolution_convert_fusion
  574.5 1.3 power_select_fusion
  575.8 0.7 slice_dynamic-update-slice_fusion
  576.5 37.7 %reduce-scatter.2.cloned.1.call-done = bf16[384,1280]{1,0:T(8,128)(2,1)} async-done(((bf16[384,5120]{1,0:T(8,128)(2,1)}), bf16[384,1280]{1,0:T(8,128)(2,1)}) %reduce-scatter.2.cloned.1.call-update) | async-done | bytes 983056 | tf_op jit(solution)/shard_map/reduce_scatter | solution.py:133
  614.2 2.7 multiply_reduce_fusion
  616.9 6.5 all-reduce.3
  624.1 4.5 collective-permute-start
  628.6 2.7 collective-permute-done
  631.3 0.7 fusion.64
  632.0 0.7 convolution_reduce_fusion
  632.7 0.7 slice_dynamic-update-slice_fusion.1
  633.5 122.7 %all-reduce.2 = (f32[64]{0:T(128)S(1)}, f32[64]{0:T(128)S(1)}) all-reduce(f32[64]{0:T(128)S(1)} %slice_dynamic-update-slice_fusion.1, f32[64]{0:T(128)S(1)} %slice_dynamic-update-slice_fusion), channel_id=2, replica_groups=mesh['ctx'=64,'tp'=4] {'ctx'}, use_global_device_ids=true, to_apply=%add | all-reduce | flops 128 | bytes 1024
  756.1 123.3 %while.15 = (s32[]{:T(128)}, f32[1]{0:T(128)}, s32[]{:T(128)}, f32[64,1]{0,1:T(1,128)S(1)}, f32[64,1]{0,1:T(1,128)S(1)}, /*index=5*/s32[]{:T(128)}, s32[]{:T(128)}, s32[]{:T(128)}, s32[]{:T(128)}) while((s32[]{:T(128)}, f32[1]{0:T(128)}, s32[]{:T(128)}, f32[64,1]{0,1:T(1,128)S(1)}, f32[64,1]{0,1:T(1,128)S(1)}, /*index=5*/s32[]{:T(128)}, ...), condition=%wide.region_17.18_spmd, body=%wide.region_16.17_spmd.sunk | while | flops 10 | bytes 213 | solution.py:41
  (144 shorter events, 51.4 us)
Async XLA Ops:
  7.2 135.2 %copy-start.11 = (f32[5120]{0:T(1024)S(1)}, f32[5120]{0:T(1024)}, u32[]{:S(2)}) copy-start(f32[5120]{0:T(1024)} %param.18) | copy-start | bytes 61444
  7.2 135.2 %copy-start.13 = (f32[128]{0:T(128)S(1)}, f32[128]{0:T(128)}, u32[]{:S(2)}) copy-start(f32[128]{0:T(128)} %param.23) | copy-start | bytes 1540
  7.2 55.1 %all-gather.8.cloned.1.call-start = ((), (), s32[]{:S(2)}) async-start(), calls=%async_computation.1 | async-start | bytes 4915200 | tf_op jit(solution)/shard_map/all_gather | solution.py:80
  7.9 134.5 %all-gather.12.cloned.1.call-start = ((), (), s32[]{:S(2)}) async-start(), calls=%async_computation.3 | async-start | bytes 1331200 | tf_op jit(solution)/shard_map/all_gather | solution.py:91
  8.7 210.9 %all-gather.10.cloned.1.call-start = ((), (), s32[]{:S(2)}) async-start(), calls=%async_computation.2 | async-start | bytes 1331200 | tf_op jit(solution)/shard_map/all_gather | solution.py:92
  9.4 291.9 %all-gather.14.cloned.1.call-start = ((), (), s32[]{:S(2)}) async-start(), calls=%async_computation.4 | async-start | bytes 6656000 | tf_op jit(solution)/shard_map/all_gather | solution.py:90
  10.0 467.7 %all-reduce.7.cloned.1.call-start = ((), (), s32[]{:S(2)}) async-start(), calls=%async_computation.7 | async-start | bytes 393216 | tf_op jit(solution)/shard_map/psum | solution.py:19
  65.3 154.3 %copy-start.14 = (f32[128]{0:T(128)S(1)}, f32[128]{0:T(128)}, u32[]{:S(2)}) copy-start(f32[128]{0:T(128)} %param.24) | copy-start | bytes 1540
  146.9 0.6 copy-start.2
  148.1 153.1 %copy-start.12 = (f32[640]{0:T(1024)S(1)}, f32[640]{0:T(1024)}, u32[]{:S(2)}) copy-start(f32[640]{0:T(1024)} %param.22) | copy-start | bytes 7684
  224.0 338.3 %all-gather.16.cloned.1.call-start = ((), (), s32[]{:S(2)}) async-start(), calls=%async_computation.5 | async-start | bytes 6656000 | tf_op jit(solution)/shard_map/all_gather | solution.py:130
  224.6 389.6 %reduce-scatter.2.cloned.1.call-start = ((), (), s32[]{:S(2)}) async-start(), calls=%async_computation.6 | async-start | bytes 4915200 | tf_op jit(solution)/shard_map/reduce_scatter | solution.py:133
  309.7 169.7 %copy-start.1 = (pred[384,384]{0,1:T(8,128)(4,1)S(1)}, pred[384,384]{0,1:T(8,128)(4,1)}, u32[]{:S(2)}) copy-start(pred[384,384]{0,1:T(8,128)(4,1)} %iota_compare_fusion.1) | copy-start | bytes 442372
  310.0 169.4 %copy-start.3 = (bf16[384,1,64]{0,2,1:T(8,128)(2,1)S(1)}, bf16[384,1,64]{0,2,1:T(8,128)(2,1)}, u32[]{:S(2)}) copy-start(bf16[384,1,64]{0,2,1:T(8,128)(2,1)} %copy-done.2) | copy-start | bytes 147460
  480.2 1.2 copy-start.4
  481.5 0.9 copy-start.16
  570.5 0.8 copy-start.5
  570.5 0.8 copy-start.9
  570.5 3.3 copy-start.15
  570.5 43.7 %copy-start = (bf16[384,1280]{1,0:T(8,128)(2,1)S(1)}, bf16[384,1280]{1,0:T(8,128)(2,1)}, u32[]{:S(2)}) copy-start(bf16[384,1280]{1,0:T(8,128)(2,1)} %param.17) | copy-start | bytes 2949124
  570.5 43.7 %copy-start.7 = (f32[1280]{0:T(1024)S(1)}, f32[1280]{0:T(1024)}, u32[]{:S(2)}) copy-start(f32[1280]{0:T(1024)} %param.27) | copy-start | bytes 15364
  570.6 43.7 %copy-start.8 = (f32[1280]{0:T(1024)S(1)}, f32[1280]{0:T(1024)}, u32[]{:S(2)}) copy-start(f32[1280]{0:T(1024)} %param.26) | copy-start | bytes 15364
  570.6 60.7 %copy-start.10 = (s32[384]{0:T(512)S(1)}, s32[384]{0:T(512)}, u32[]{:S(2)}) copy-start(s32[384]{0:T(512)} %param.29) | copy-start | bytes 4612
  623.4 256.6 %copy-start.6 = (f32[384]{0:T(512)}, f32[384]{0:T(512)S(1)}, u32[]{:S(2)}) copy-start(f32[384]{0:T(512)S(1)} %multiply_add_fusion.1) | copy-start | bytes 4612
  624.1 7.2 collective-permute-start
Sparse Core Ops, SparseCore 0:
  9.8 52.4 all-gather.7
  65.0 77.3 all-gather.11
  145.1 74.3 all-gather.9
  222.1 79.1 all-gather.13
  304.6 173.0 all-reduce.6
  480.3 82.0 all-gather.15
  570.7 43.4 reduce-scatter.1
where the time goes:
time: 892 us; the launch traced here: 887 us
  waiting for transfers between devices  566 us (63%)
  blocking collectives  129 us (14%)
  loops' own time  81.6 us (9%)
  local copies, waits for them, and re-layouts  47.7 us (5%)
  matrix products  29 us (3%)
  between operations  15.2 us (2%)
  other arithmetic  13.2 us (1%)
    psum x1, waiting for transfers between devices, from_root(): return lax.psum(jnp.where(mine, x, jnp.zeros_like(x)), axis)  168 us
    unnamed x1, blocking collectives  123 us
    another operation x1, loops' own time, prefix(): return lax.fori_loop(0, length, lap, start)  81.6 us
    all_gather x1, waiting for transfers between devices, on_device(): lax.all_gather(w_out, 'ctx', axis=1, tiled=True)  79 us
    all_gather x1, waiting for transfers between devices, on_device(): keys = add_rows(lax.all_gather(w_key, 'ctx', axis=0, tiled=True))  77.1 us
    all_gather x1, waiting for transfers between devices, on_device(): query = add_rows(lax.all_gather(w_query, 'ctx', axis=0, tiled=True))  75 us
    all_gather x1, waiting for transfers between devices, on_device(): vals = add_rows(lax.all_gather(w_value, 'ctx', axis=0, tiled=True))  71.4 us
    all_gather x1, waiting for transfers between devices, on_device(): whole = lax.all_gather(tokens, 'tp', axis=1, tiled=True)  52.2 us
  transfers between devices with their start and end apart: 8, of which 8 were waited for; matrix products, arithmetic and copies ran while one was open for 4% of the time, Pallas kernels for 0%

commit v1 on v0

v1 whole, which is shorter than its diff:
```python
import jax
import jax.numpy as jnp
from jax import lax
from jax.experimental import pallas as pl
from jax.experimental.pallas import tpu as pltpu
from jax.sharding import PartitionSpec as P

D = 5120
HD = 128
HALF = HD // 2
GROUP = 5
QW = GROUP * HD

EPS = 1e-06
GAMMA = 0.99
LAMBDA = 0.95
ROPE_BASE = 1000000.0
REWARD_SCALE = 0.25

X, Z, C, T = 4, 8, 2, 4
ROWS = 384
PIECE = D // T
MIB = 1 << 20

F32 = jnp.float32
BF16 = jnp.bfloat16


def place(x, z, c):
    return (x * Z + z) * C + c


def shift_tp(block, distance):
    return lax.ppermute(block, "tp", [(i, (i + distance) % T) for i in range(T)])


def ring_tp(block):
    half = block.shape[0] // 2
    below = shift_tp(block, 1)
    above = shift_tp(block, -1)
    first = shift_tp(below[:half], 1)
    second = shift_tp(above[half:], -1)
    return block, below, above, first, second


def params(mib=40):
    return pltpu.CompilerParams(vmem_limit_bytes=mib * MIB)


def project_kernel(
    order, own, below, above, first, second, gain, w_q, w_kv, bias, cosine, sine, q_out, kv_out, scale, acc
):
    step = pl.program_id(0)
    half = first.shape[0]

    @pl.when(step == 0)
    def _():
        def squares(ref):
            x = ref[...].astype(F32)
            return jnp.sum(x * x, axis=-1, keepdims=True)

        far = jnp.concatenate([squares(first), squares(second)], axis=0)
        mean = (squares(own) + squares(below) + squares(above) + far) / D
        scale[...] = lax.rsqrt(mean + EPS)
        acc[...] = jnp.zeros_like(acc)

    def add(x, rows):
        normed = (x.astype(F32) * scale[rows, :] * gain[0]).astype(BF16)
        acc[rows, :QW] += jnp.dot(normed, w_q[...], preferred_element_type=F32)
        acc[rows, QW:] += jnp.dot(normed, w_kv[...], preferred_element_type=F32)

    everything = pl.ds(0, ROWS)
    for at, ref in enumerate((own, below, above)):

        @pl.when(step == at)
        def _(ref=ref):
            add(ref[...], everything)

    @pl.when(step == T - 1)
    def _():
        add(first[...], pl.ds(0, half))
        add(second[...], pl.ds(half, half))

        def rotary(u):
            return u * cosine[...] + pltpu.roll(u, HALF, 1) * sine[...]

        for head in range(GROUP):
            span = slice(head * HD, (head + 1) * HD)
            q_out[:, span] = rotary(acc[:, span] + bias[:, span]).astype(BF16)
        span = slice(QW, QW + HD)
        kv_out[:, :HD] = rotary(acc[:, span] + bias[:, span]).astype(BF16)
        span = slice(QW + HD, QW + 2 * HD)
        kv_out[:, HD:] = (acc[:, span] + bias[:, span]).astype(BF16)


def project(order, pieces, gain, weights, bias, cosine, sine):
    whole = lambda *shape: pl.BlockSpec(shape, lambda k, order: (0,) * len(shape))
    wide = QW + 2 * HD
    grid = pltpu.PrefetchScalarGridSpec(
        num_scalar_prefetch=1,
        grid=(T,),
        in_specs=[
            whole(ROWS, PIECE),
            whole(ROWS, PIECE),
            whole(ROWS, PIECE),
            whole(ROWS // 2, PIECE),
            whole(ROWS // 2, PIECE),
            pl.BlockSpec((1, 1, PIECE), lambda k, order: (order[k], 0, 0)),
            pl.BlockSpec((PIECE, QW), lambda k, order: (order[k], 1)),
            pl.BlockSpec((PIECE, 2 * HD), lambda k, order: (order[k], 5)),
            whole(1, wide),
            whole(ROWS, HD),
            whole(ROWS, HD),
        ],
        out_specs=[whole(ROWS, QW), whole(ROWS, 2 * HD)],
        scratch_shapes=[pltpu.VMEM((ROWS, 1), F32), pltpu.VMEM((ROWS, wide), F32)],
    )
    return pl.pallas_call(
        project_kernel,
        grid_spec=grid,
        out_shape=[
            jax.ShapeDtypeStruct((ROWS, QW), BF16),
            jax.ShapeDtypeStruct((ROWS, 2 * HD), BF16),
        ],
        compiler_params=params(),
        cost_estimate=pl.CostEstimate(
            flops=2 * ROWS * D * wide, bytes_accessed=2 * D * (wide + ROWS), transcendentals=0
        ),
        name="project",
    )(order, *pieces, gain, weights, weights, bias, cosine, sine)


def attend_kernel(index, q, kv, anchor, out, bias):
    keep_anchor = jnp.full((ROWS, ROWS), index[0], jnp.int32) > 0
    row = lax.broadcasted_iota(jnp.int32, (ROWS, ROWS), 0)
    col = lax.broadcasted_iota(jnp.int32, (ROWS, ROWS), 1)
    bias[:, :ROWS] = jnp.where(keep_anchor, 0.0, -jnp.inf)
    bias[:, ROWS:] = jnp.where(row >= col, 0.0, -jnp.inf)
    keys = jnp.concatenate([anchor[:, :HD], kv[:, :HD]], axis=0)
    vals = jnp.concatenate([anchor[:, HD:], kv[:, HD:]], axis=0)
    for head in range(GROUP):
        span = slice(head * HD, (head + 1) * HD)
        scores = lax.dot_general(q[:, span], keys, (((1,), (1,)), ((), ())), preferred_element_type=F32)
        scores = scores * (HD**-0.5) + bias[...]
        peak = jnp.max(scores, axis=-1, keepdims=True)
        weights = jnp.exp(scores - peak)
        total = jnp.sum(weights, axis=-1, keepdims=True)
        mixed = jnp.dot(weights.astype(BF16), vals, preferred_element_type=F32)
        out[:, span] = (mixed / total).astype(BF16)


def attend(index, q, kv, anchor):
    vmem = pl.BlockSpec(memory_space=pltpu.VMEM)
    return pl.pallas_call(
        attend_kernel,
        in_specs=[pl.BlockSpec(memory_space=pltpu.SMEM), vmem, vmem, vmem],
        out_specs=vmem,
        out_shape=jax.ShapeDtypeStruct((ROWS, QW), BF16),
        scratch_shapes=[pltpu.VMEM((ROWS, 2 * ROWS), F32)],
        compiler_params=params(),
        cost_estimate=pl.CostEstimate(
            flops=4 * ROWS * 2 * ROWS * QW, bytes_accessed=4 * ROWS * QW, transcendentals=ROWS * 2 * ROWS * GROUP
        ),
        name="attend",
    )(index, q, kv, anchor)


def times(a, w):
    return lax.dot_general(a, w, (((1,), (1,)), ((), ())), preferred_element_type=F32)


def out_own_kernel(order, tokens, att, w, out):
    out[...] = tokens[...].astype(F32) + times(att[...], w[...])


def out_next_kernel(order, total, below, above, w_below, w_above, out):
    out[...] = total[...] + times(below[...], w_below[...]) + times(above[...], w_above[...])


def out_last_kernel(order, total, first, second, w, gain, head, resid_out, stats_out):
    half = first.shape[0]
    lane = lax.broadcasted_iota(jnp.int32, (half, HD), 1)
    for at, ref in enumerate((first, second)):
        rows = pl.ds(at * half, half)
        resid = total[rows, :] + times(ref[...], w[...])
        resid_out[rows, :] = resid.astype(BF16)
        squares = jnp.sum(resid * resid, axis=-1, keepdims=True)
        products = jnp.sum(resid * gain[...] * head[...], axis=-1, keepdims=True)
        both = jnp.where(lane == 0, squares, products)
        stats_out[at] = both.T[:8, :]


def out_call(kernel, order, operands, weights, extra, out_shape, name, flops):
    vmem = lambda shape: pl.BlockSpec(shape, lambda i, order: (0,) * len(shape))
    w_spec = lambda at: pl.BlockSpec((PIECE, QW), lambda i, order, at=at: (order[at], 0))
    grid = pltpu.PrefetchScalarGridSpec(
        num_scalar_prefetch=1,
        grid=(1,),
        in_specs=[vmem(o.shape) for o in operands] + [w_spec(at) for _, at in weights] + [vmem(e.shape) for e in extra],
        out_specs=jax.tree.map(lambda s: vmem(s.shape), out_shape),
    )
    return pl.pallas_call(
        kernel,
        grid_spec=grid,
        out_shape=out_shape,
        compiler_params=params(),
        cost_estimate=pl.CostEstimate(flops=flops, bytes_accessed=6 * MIB, transcendentals=0),
        name=name,
    )(order, *operands, *(w for w, _ in weights), *extra)


def broadcast_anchor(block):
    here = lax.axis_index("ctx")
    holders = [(0, 0, 0)]
    for dx, dz, dc in ((0, 0, 1), (2, 0, 0), (0, 4, 0), (1, 0, 0), (0, 2, 0), (0, 1, 0)):
        fresh = [((x + dx) % X, (z + dz) % Z, (c + dc) % C) for x, z, c in holders]
        sent = lax.ppermute(block, "ctx", [(place(*a), place(*b)) for a, b in zip(holders, fresh)])
        table = jnp.zeros((X * Z * C,), jnp.bool_).at[jnp.array([place(*b) for b in fresh])].set(True)
        block = jnp.where(table[here], sent, block)
        holders = holders + fresh
    return block


def on_device(
    tokens,
    input_gain,
    w_query,
    w_key,
    w_value,
    query_bias,
    key_bias,
    value_bias,
    w_out,
    final_gain,
    critic_head,
    critic_bias,
    rewards,
    turn_ends,
    episode_done,
):
    index = lax.axis_index("ctx")
    mine = lax.axis_index("tp")
    order = jnp.stack([mine, (mine + 3) % T, (mine + 1) % T, (mine + 2) % T]).astype(jnp.int32)

    corner = [
        (place(x, z, c) * T + y, place(y, z, c) * T + x) for x in range(X) for z in range(Z) for c in range(C) for y in range(T)
    ]
    out_block = lax.ppermute(w_out.T, ("ctx", "tp"), corner)
    weights = lax.all_gather(
        jnp.concatenate([out_block, w_query, w_key, w_value], axis=1), "ctx", axis=0, tiled=True
    )

    pieces = ring_tp(tokens)
    positions = (index * ROWS + jnp.arange(ROWS)).astype(F32)
    steps = jnp.arange(HALF).astype(F32)
    inverse = 1.0 / ROPE_BASE ** (steps * 2.0 / HD)
    angle = positions[:, None] * inverse[None, :]
    cosine, sine = jnp.cos(angle), jnp.sin(angle)
    cosine = jnp.concatenate([cosine, cosine], axis=1)
    sine = jnp.concatenate([-sine, sine], axis=1)
    bias = jnp.concatenate([query_bias, key_bias, value_bias])[None, :]
    query, kv = project(order, pieces, input_gain.reshape(T, 1, PIECE), weights, bias, cosine, sine)

    anchor = broadcast_anchor(kv)
    att = attend(index.astype(jnp.int32)[None], query, kv, anchor)

    own, below, above, first, second = ring_tp(att)
    flops = 2 * ROWS * QW * PIECE
    wide = jax.ShapeDtypeStruct((ROWS, PIECE), F32)
    total = out_call(out_own_kernel, order, [tokens, own], [(weights, 0)], [], wide, "out_own", flops)
    total = out_call(
        out_next_kernel, order, [total, below, above], [(weights, 1), (weights, 2)], [], wide, "out_next", 2 * flops
    )
    residual_stream, stats = out_call(
        out_last_kernel,
        order,
        [total, first, second],
        [(weights, 3)],
        [final_gain[None, :], critic_head[None, :]],
        [jax.ShapeDtypeStruct((ROWS, PIECE), BF16), jax.ShapeDtypeStruct((2, 8, ROWS // 2), F32)],
        "out_last",
        flops,
    )
    stats = lax.psum(jnp.concatenate([stats[0, :2], stats[1, :2]], axis=1), "tp")
    values = stats[1] * lax.rsqrt(stats[0] / D + EPS) + critic_bias[0]

    ends = jnp.maximum(turn_ends, episode_done)
    discount = jnp.where(ends > 0, GAMMA, 1.0).astype(F32) * (1 - episode_done).astype(F32)
    reward = REWARD_SCALE * (rewards * ends).astype(F32)
    decaying = ends * (1 - episode_done)
    zero_int = jnp.zeros((1,), jnp.int32)
    decay_count = jnp.concatenate([zero_int, jnp.cumsum(decaying)])
    done_count = jnp.concatenate([zero_int, jnp.cumsum(episode_done)])
    rate = GAMMA * LAMBDA
    later = jnp.arange(ROWS)[None, :] >= jnp.arange(ROWS)[:, None]
    same_episode = done_count[None, :ROWS] == done_count[:ROWS, None]
    powers = (decay_count[None, :ROWS] - decay_count[:ROWS, None]).astype(F32)
    matrix = jnp.where(later & same_episode, jnp.power(rate, powers), 0.0)
    tail_powers = (decay_count[ROWS] - decay_count[:ROWS]).astype(F32)
    tail = jnp.where(done_count[ROWS] == done_count[:ROWS], jnp.power(rate, tail_powers), 0.0)
    edge = matrix[:, ROWS - 1] * discount[ROWS - 1]

    next_values = jnp.concatenate([values[1:], jnp.zeros((1,), F32)])
    delta = reward + discount * next_values - values
    local = jnp.dot(matrix, delta, precision=lax.Precision.HIGHEST)
    record = jnp.stack([values[0], local[0], tail[0], edge[0]])
    n = lax.axis_size("ctx")
    records = jnp.broadcast_to(jnp.concatenate([record, jnp.zeros((HD - 4,), F32)])[None, :], (n, HD))
    records = lax.all_to_all(records, "ctx", 0, 0, tiled=True)
    after_values = jnp.concatenate([records[1:, 0], jnp.zeros((1,), F32)])
    terms = records[:, 1] + records[:, 3] * after_values
    block = jnp.arange(n)
    between = (block[None, :] > index) & (block[None, :] < block[:, None])
    reach = jnp.prod(jnp.where(between, records[None, :, 2], 1.0), axis=1)
    carry = jnp.sum(jnp.where(block > index, reach * terms, 0.0))
    following = jnp.sum(jnp.where(block == index, after_values, 0.0))
    advantages = local + edge * following + tail * carry
    return (residual_stream, values, advantages)


def solution(mesh):
    in_specs = (
        P("ctx", "tp"),
        P(),
        P("ctx", "tp"),
        P("ctx", "tp"),
        P("ctx", "tp"),
        P("tp"),
        P("tp"),
        P("tp"),
        P("tp", "ctx"),
        P("tp"),
        P("tp"),
        P(),
        P("ctx"),
        P("ctx"),
        P("ctx"),
    )
    out_specs = (P("ctx", "tp"), P("ctx"), P("ctx"))
    return jax.shard_map(
        on_device, mesh=mesh, in_specs=in_specs, out_specs=out_specs, check_vma=False
    )
```

time: 892 us -> 247 us (0.28)
  waiting for transfers between devices: 566 us -> 116 us
  blocking collectives: 129 us -> 6.06 us
  loops' own time: 81.6 us -> 0 us
  starting transfers between devices: 4.99 us -> 55.3 us
  local copies, waits for them, and re-layouts: 47.7 us -> 16.1 us
  matrix products: 29 us -> 0.59 us
  Pallas kernels: 0 us -> 22.8 us
    all_gather x5 -> x1, waiting for transfers between devices: 355 us -> 60.6 us  [on_device(): lax.all_gather(jnp.concatenate([out_block, w_query, w_key, w_value], axis...]
    psum x1 -> x0, waiting for transfers between devices: 168 us -> none  [from_root(): return lax.psum(jnp.where(mine, x, jnp.zeros_like(x)), axis)]
    unnamed x1 -> x0, blocking collectives: 123 us -> none
    another operation x1 -> x0, loops' own time: 81.6 us -> none  [prefix(): return lax.fori_loop(0, length, lap, start)]
    ppermute x1 -> x15, waiting for transfers between devices: 2.68 us -> 46.1 us  [the longest x8 35.6 us: shift_tp(): lax.ppermute(block, 'tp', [(i, (i + distance) % T) for i in range(T)])]
    reduce_scatter x1 -> x0, waiting for transfers between devices: 37.7 us -> none  [on_device(): lax.psum_scatter(partial_sums.astype(jnp.bfloat16), 'tp', scatter_dimensi...]
    dynamic_slice x64 -> x6, local copies, waits for them, and re-layouts: 41.7 us -> 4.85 us  [broadcast_anchor(): block = jnp.where(table[here], sent, block)]
    dot_general x9 -> x1, matrix products: 29 us -> 0.59 us  [on_device(): local = jnp.dot(matrix, delta, precision=lax.Precision.HIGHEST)]
  transfers between devices with their start and end apart: 8 -> 17, of which waited for: 8 -> 11; matrix products, arithmetic and copies ran while one was open for 4% -> 5% of each run, Pallas kernels for 0% -> 3%
where the time goes in v1:
time: 247 us; the launch traced here: 246 us
  waiting for transfers between devices  116 us (47%)
  starting transfers between devices  55.3 us (22%)
  Pallas kernels  22.8 us (9%)
  local copies, waits for them, and re-layouts  16.1 us (7%)
  between operations  15.1 us (6%)
  other arithmetic  14 us (6%)
  blocking collectives  6.06 us (2%)
    all_gather x1, waiting for transfers between devices, on_device(): lax.all_gather(jnp.concatenate([out_block, w_query, w_key, w_value], axis...  60.6 us
    ppermute x8, waiting for transfers between devices, shift_tp(): lax.ppermute(block, 'tp', [(i, (i + distance) % T) for i in range(T)])  35.6 us
    all_to_all x1, starting transfers between devices, on_device(): records = lax.all_to_all(records, 'ctx', 0, 0, tiled=True)  22.9 us
    ppermute x8, starting transfers between devices, shift_tp(): lax.ppermute(block, 'tp', [(i, (i + distance) % T) for i in range(T)])  22.3 us
    pallas_call x3, Pallas kernels, out_call(): pl.pallas_call(kernel, grid_spec=grid, out_shape=out_shape, compiler_para...  11.4 us
    ppermute x6, waiting for transfers between devices, broadcast_anchor(): lax.ppermute(block, 'ctx', [(place(*a), place(*b)) for a, b in zip(holder...  10.6 us
    all_to_all x1, waiting for transfers between devices, on_device(): records = lax.all_to_all(records, 'ctx', 0, 0, tiled=True)  9.27 us
    pallas_call x1, Pallas kernels, project(): pl.pallas_call(project_kernel, grid_spec=grid, out_shape=[jax.ShapeDtypeS...  8.92 us
  transfers between devices with their start and end apart: 17, of which 11 were waited for; matrix products, arithmetic and copies ran while one was open for 5% of the time, Pallas kernels for 3%

profile of v1, /device:TPU:1, one launch (start us, length us, event | category | flops | bytes accessed | tf_op | source)
XLA Modules:
  0.0 246.0 jit_solution(4004936843681881249)
XLA Ops:
  7.2 1.6 collective-permute-start.4
  8.8 1.7 pad_maximum_fusion
  10.5 7.2 %collective-permute-start = (bf16[384,1280]{1,0:T(8,128)(2,1)}, bf16[384,1280]{1,0:T(8,128)(2,1)S(1)}, u32[]{:S(2)}, u32[]{:S(2)}) collective-permute-start(bf16[384,1280]{1,0:T(8,128)(2,1)} %tokens.1), channel_id=1, source_target_pairs={{0,1},{1,2},{2,3},{3,0},{4,5},{5,6},{6,7},{7,4},{8,9},{9,10},{10,1... | collective-permute-start | bytes 2949128 | tf_op jit(solution)/shard_map/ppermute | solution.py:34
  17.6 6.9 %collective-permute-start.1 = (bf16[384,1280]{1,0:T(8,128)(2,1)}, bf16[384,1280]{1,0:T(8,128)(2,1)S(1)}, u32[]{:S(2)}, u32[]{:S(2)}) collective-permute-start(bf16[384,1280]{1,0:T(8,128)(2,1)} %tokens.1), channel_id=1, source_target_pairs={{0,3},{1,0},{2,1},{3,2},{4,7},{5,4},{6,5},{7,6},{8,11},{9,8},{10,9... | collective-permute-start | bytes 2949128 | tf_op jit(solution)/shard_map/ppermute | solution.py:34
  25.3 20.6 %collective-permute-done.below = bf16[384,1280]{1,0:T(8,128)(2,1)S(1)} collective-permute-done((bf16[384,1280]{1,0:T(8,128)(2,1)}, bf16[384,1280]{1,0:T(8,128)(2,1)S(1)}, u32[]{:S(2)}, u32[]{:S(2)}) %collective-permute-start) | collective-permute-done | bytes 983072 | tf_op jit(solution)/shard_map/ppermute | solution.py:34
  47.5 2.7 %collective-permute-start.3 = (bf16[192,1280]{1,0:T(8,128)(2,1)}, bf16[192,1280]{1,0:T(8,128)(2,1)}, u32[]{:S(2)}, u32[]{:S(2)}) collective-permute-start(bf16[192,1280]{1,0:T(8,128)(2,1)} %slice.130), channel_id=1, source_target_pairs={{0,3},{1,0},{2,1},{3,2},{4,7},{5,4},{6,5},{7,6},{8,11},{9,8},{10,9... | collective-permute-start | bytes 1474568 | tf_op jit(solution)/shard_map/ppermute | solution.py:34
  51.3 8.2 %collective-permute-done.2.first = bf16[192,1280]{1,0:T(8,128)(2,1)} collective-permute-done((bf16[192,1280]{1,0:T(8,128)(2,1)}, bf16[192,1280]{1,0:T(8,128)(2,1)}, u32[]{:S(2)}, u32[]{:S(2)}) %collective-permute-start.2) | collective-permute-done | bytes 491552 | tf_op jit(solution)/shard_map/ppermute | solution.py:34
  59.5 60.6 %all-gather.2.cloned.1.call-done.w_q.w_kv.w.w_below.w_above = bf16[5120,1536]{1,0:T(8,128)(2,1)} async-done(((bf16[80,1536]{1,0:T(8,128)(2,1)}), bf16[5120,1536]{1,0:T(8,128)(2,1)}) %all-gather.2.cloned.1.call-update) | async-done | bytes 15728656 | tf_op jit(solution)/shard_map/all_gather | solution.py:249
  120.8 8.9 %project.1 = (bf16[384,640]{1,0:T(8,128)(2,1)S(1)}, bf16[384,256]{1,0:T(8,128)(2,1)S(1)}) custom-call(s32[4]{0:T(128)S(1)} %pad_add_fusion.2.order, bf16[384,1280]{1,0:T(8,128)(2,1)S(1)} %copy-done, bf16[384,1280]{1,0:T(8,128)(2,1)S(1)} %collective-permute-done.below, bf16[384,1280]{1,0:T(8,128)(2,1)S(1)} %collective-permute-done.1.above, ...), custom_call_target="tpu_custom_call" | custom-call | flops 3523215360 | bytes 13107200 | tf_op jit(solution)/shard_map/project/pallas_call | solution.py:118
  130.5 1.4 collective-permute-start.5
  134.7 1.7 collective-permute-start.6
  137.6 2.8 %collective-permute-done.6 = bf16[384,256]{1,0:T(8,128)(2,1)S(1)} collective-permute-done((bf16[384,256]{1,0:T(8,128)(2,1)S(1)}, bf16[384,256]{1,0:T(8,128)(2,1)S(1)}, u32[]{:S(2)}, u32[]{:S(2)}) %collective-permute-start.6) | collective-permute-done | bytes 196640 | tf_op jit(solution)/shard_map/ppermute | solution.py:217
  141.1 1.3 collective-permute-start.7
  143.0 2.8 %collective-permute-done.7 = bf16[384,256]{1,0:T(8,128)(2,1)S(1)} collective-permute-done((bf16[384,256]{1,0:T(8,128)(2,1)S(1)}, bf16[384,256]{1,0:T(8,128)(2,1)S(1)}, u32[]{:S(2)}, u32[]{:S(2)}) %collective-permute-start.7) | collective-permute-done | bytes 196640 | tf_op jit(solution)/shard_map/ppermute | solution.py:217
  146.5 1.3 collective-permute-start.8
  148.4 2.0 collective-permute-done.8
  151.0 1.3 collective-permute-start.9
  153.5 1.4 collective-permute-done.9
  155.6 1.5 collective-permute-start.10
  160.4 2.5 %attend.1.att = bf16[384,640]{1,0:T(8,128)(2,1)S(1)} custom-call(s32[1]{0:T(128)} %bitcast.4.index, bf16[384,640]{1,0:T(8,128)(2,1)S(1)} %copy-done.3, bf16[384,256]{1,0:T(8,128)(2,1)S(1)} %get-tuple-element.20.kv, bf16[384,256]{1,0:T(8,128)(2,1)S(1)} %broadcast_select_fusion.5.anchor), custom_call_target="tpu_custom_call" | custom-call | flops 754974720 | bytes 983040 | tf_op jit(solution)/shard_map/attend/pallas_call | solution.py:154
  162.9 1.3 collective-permute-start.11
  164.2 1.5 collective-permute-start.12
  166.6 6.7 %collective-permute-done.11.below = bf16[384,640]{1,0:T(8,128)(2,1)S(1)} collective-permute-done((bf16[384,640]{1,0:T(8,128)(2,1)S(1)}, bf16[384,640]{1,0:T(8,128)(2,1)S(1)}, u32[]{:S(2)}, u32[]{:S(2)}) %collective-permute-start.11) | collective-permute-done | bytes 491552 | tf_op jit(solution)/shard_map/ppermute | solution.py:34
  173.5 2.7 %collective-permute-start.14 = (bf16[192,640]{1,0:T(8,128)(2,1)S(1)}, bf16[192,640]{1,0:T(8,128)(2,1)S(1)}, u32[]{:S(2)}, u32[]{:S(2)}) collective-permute-start(bf16[192,640]{1,0:T(8,128)(2,1)S(1)} %slice.132), channel_id=1, source_target_pairs={{0,3},{1,0},{2,1},{3,2},{4,7},{5,4},{6,5},{7,6},{8,11},{9,8},{10,9... | collective-permute-start | bytes 737288 | tf_op jit(solution)/shard_map/ppermute | solution.py:34
  176.2 1.3 power_select_fusion.2
  178.7 3.0 %out_own.1.total = f32[384,1280]{1,0:T(8,128)S(1)} custom-call(s32[4]{0:T(128)S(1)} %pad_add_fusion.2.order, bf16[384,1280]{1,0:T(8,128)(2,1)S(1)} %copy-done, bf16[384,640]{1,0:T(8,128)(2,1)S(1)} %attend.1.att, bf16[5120,1536]{1,0:T(8,128)(2,1)} %all-gather.2.cloned.1.call-done.w_q.w_kv.w.w_below.w_above), custom_call_target="tpu_custom_call" | custom-call | flops 629145600 | bytes 6291456 | tf_op jit(solution)/shard_map/out_own/pallas_call | solution.py:202
  181.7 4.2 %out_next.1.total = f32[384,1280]{1,0:T(8,128)S(1)} custom-call(s32[4]{0:T(128)S(1)} %pad_add_fusion.2.order, f32[384,1280]{1,0:T(8,128)S(1)} %out_own.1.total, bf16[384,640]{1,0:T(8,128)(2,1)S(1)} %collective-permute-done.11.below, bf16[384,640]{1,0:T(8,128)(2,1)S(1)} %collective-permute-done.12.above, ...), custom_call_target="tpu_custom_call" | custom-call | flops 1258291200 | bytes 6291456 | tf_op jit(solution)/shard_map/out_next/pallas_call | solution.py:202
  185.9 4.3 %out_last.1 = (bf16[384,1280]{1,0:T(8,128)(2,1)}, f32[2,8,192]{2,1,0:T(8,128)S(1)}) custom-call(s32[4]{0:T(128)S(1)} %pad_add_fusion.2.order, f32[384,1280]{1,0:T(8,128)S(1)} %out_next.1.total, bf16[192,640]{1,0:T(8,128)(2,1)S(1)} %collective-permute-done.13.first, bf16[192,640]{1,0:T(8,128)(2,1)S(1)} %collective-permute-done.14.second, ...), custom_call_target="tpu_custom_call" | custom-call | flops 629145600 | bytes 6291456 | tf_op jit(solution)/shard_map/out_last/pallas_call | solution.py:202
  190.3 6.1 %psum.7 = f32[2,384]{1,0:T(2,128)S(1)} all-reduce(f32[2,384]{1,0:T(2,128)S(1)} %pad_maximum_fusion.4), channel_id=1, replica_groups=mesh['ctx'=64,'tp'=4] {'tp'}, use_global_device_ids=true, to_apply=%region_5.6 | all-reduce | flops 768 | bytes 6144 | tf_op jit(solution)/shard_map/psum | solution.py:284
  200.1 2.6 %concatenate.40 = f32[128]{0:T(128)S(1)} concatenate(f32[1]{0:T(128)} %bitcast.21, f32[1]{0:T(128)} %slice.117, f32[1]{0:T(128)} %slice.120, f32[1]{0:T(128)} %bitcast.24, f32[124]{0:T(128)S(1)} %broadcast_in_dim.100), dimensions={0} | concatenate | bytes 1024 | tf_op jit(solution)/shard_map/concatenate | solution.py:308
  203.3 22.9 %all-to-all-start = ((f32[64,1,128]{2,1,0:T(1,128)}), f32[64,1,128]{2,1,0:T(1,128)S(1)}, u32[]{:S(2)}, u32[]{:S(2)}) async-start(f32[64,1,128]{2,1,0:T(1,128)} %broadcast_in_dim.101), calls=%async_computation | async-start | bytes 65536 | tf_op jit(solution)/shard_map/all_to_all | solution.py:309
  226.2 9.3 %all-to-all-done = f32[64,1,128]{2,1,0:T(1,128)S(1)} async-done(((f32[64,1,128]{2,1,0:T(1,128)}), f32[64,1,128]{2,1,0:T(1,128)S(1)}, u32[]{:S(2)}, u32[]{:S(2)}) %all-to-all-start) | async-done | bytes 32800 | tf_op jit(solution)/shard_map/all_to_all | solution.py:309
  (102 shorter events, 27.0 us)
Async XLA Ops:
  7.2 112.9 %all-gather.2.cloned.1.call-start = ((), (), s32[]{:S(2)}) async-start(), calls=%async_computation.1 | async-start | bytes 15974400 | tf_op jit(solution)/shard_map/all_gather | solution.py:249
  7.2 1.6 collective-permute-start.4
  10.4 109.6 %copy-start = (bf16[384,1280]{1,0:T(8,128)(2,1)S(1)}, bf16[384,1280]{1,0:T(8,128)(2,1)}, u32[]{:S(2)}) copy-start(bf16[384,1280]{1,0:T(8,128)(2,1)} %tokens.1) | copy-start | bytes 2949124
  10.5 35.5 %collective-permute-start = (bf16[384,1280]{1,0:T(8,128)(2,1)}, bf16[384,1280]{1,0:T(8,128)(2,1)S(1)}, u32[]{:S(2)}, u32[]{:S(2)}) collective-permute-start(bf16[384,1280]{1,0:T(8,128)(2,1)} %tokens.1), channel_id=1, source_target_pairs={{0,1},{1,2},{2,3},{3,0},{4,5},{5,6},{6,7},{7,4},{8,9},{9,10},{10,1... | collective-permute-start | bytes 2949128 | tf_op jit(solution)/shard_map/ppermute | solution.py:34
  17.6 29.1 %collective-permute-start.1 = (bf16[384,1280]{1,0:T(8,128)(2,1)}, bf16[384,1280]{1,0:T(8,128)(2,1)S(1)}, u32[]{:S(2)}, u32[]{:S(2)}) collective-permute-start(bf16[384,1280]{1,0:T(8,128)(2,1)} %tokens.1), channel_id=1, source_target_pairs={{0,3},{1,0},{2,1},{3,2},{4,7},{5,4},{6,5},{7,6},{8,11},{9,8},{10,9... | collective-permute-start | bytes 2949128 | tf_op jit(solution)/shard_map/ppermute | solution.py:34
  46.7 12.8 %collective-permute-start.2 = (bf16[192,1280]{1,0:T(8,128)(2,1)}, bf16[192,1280]{1,0:T(8,128)(2,1)}, u32[]{:S(2)}, u32[]{:S(2)}) collective-permute-start(bf16[192,1280]{1,0:T(8,128)(2,1)} %slice.129), channel_id=1, source_target_pairs={{0,1},{1,2},{2,3},{3,0},{4,5},{5,6},{6,7},{7,4},{8,9},{9,10},{10,1... | collective-permute-start | bytes 1474568 | tf_op jit(solution)/shard_map/ppermute | solution.py:34
  47.5 11.9 %collective-permute-start.3 = (bf16[192,1280]{1,0:T(8,128)(2,1)}, bf16[192,1280]{1,0:T(8,128)(2,1)}, u32[]{:S(2)}, u32[]{:S(2)}) collective-permute-start(bf16[192,1280]{1,0:T(8,128)(2,1)} %slice.130), channel_id=1, source_target_pairs={{0,3},{1,0},{2,1},{3,2},{4,7},{5,4},{6,5},{7,6},{8,11},{9,8},{10,9... | collective-permute-start | bytes 1474568 | tf_op jit(solution)/shard_map/ppermute | solution.py:34
  120.1 0.7 copy-start.1
  120.8 21.6 %copy-start.13 = (pred[64]{0:T(512)(128)(4,1)S(1)}, pred[64]{0:T(512)(128)(4,1)}, u32[]{:S(2)}) copy-start(pred[64]{0:T(512)(128)(4,1)} %constant.159) | copy-start | bytes 196
  120.8 27.0 %copy-start.12 = (pred[64]{0:T(512)(128)(4,1)S(1)}, pred[64]{0:T(512)(128)(4,1)}, u32[]{:S(2)}) copy-start(pred[64]{0:T(512)(128)(4,1)} %constant.154) | copy-start | bytes 196
  129.7 0.8 copy-start.2
  130.5 21.8 %copy-start.4 = (s32[384]{0:T(512)S(1)}, s32[384]{0:T(512)}, u32[]{:S(2)}) copy-start(s32[384]{0:T(512)} %param.37) | copy-start | bytes 4612
  130.5 21.8 %copy-start.7 = (s32[384]{0:T(512)S(1)}, s32[384]{0:T(512)}, u32[]{:S(2)}) copy-start(s32[384]{0:T(512)} %param.36) | copy-start | bytes 4612
  130.5 21.8 %copy-start.11 = (pred[64]{0:T(512)(128)(4,1)S(1)}, pred[64]{0:T(512)(128)(4,1)}, u32[]{:S(2)}) copy-start(pred[64]{0:T(512)(128)(4,1)} %constant.149) | copy-start | bytes 196
  130.5 26.6 %copy-start.10 = (pred[64]{0:T(512)(128)(4,1)S(1)}, pred[64]{0:T(512)(128)(4,1)}, u32[]{:S(2)}) copy-start(pred[64]{0:T(512)(128)(4,1)} %constant.144) | copy-start | bytes 196
  130.5 29.8 %copy-start.3 = (bf16[384,640]{1,0:T(8,128)(2,1)S(1)}, bf16[384,640]{1,0:T(8,128)(2,1)}, u32[]{:S(2)}) copy-start(bf16[384,640]{1,0:T(8,128)(2,1)} %copy-done.2) | copy-start | bytes 1474564
  130.5 3.5 %collective-permute-start.5 = (bf16[384,256]{1,0:T(8,128)(2,1)S(1)}, bf16[384,256]{1,0:T(8,128)(2,1)S(1)}, u32[]{:S(2)}, u32[]{:S(2)}) collective-permute-start(bf16[384,256]{1,0:T(8,128)(2,1)S(1)} %get-tuple-element.20.kv), channel_id=1, source_target_pairs={{0,4},{1,5},{2,6},{3,7}} | collective-permute-start | bytes 589832 | tf_op jit(solution)/shard_map/ppermute | solution.py:217
  134.7 5.7 %collective-permute-start.6 = (bf16[384,256]{1,0:T(8,128)(2,1)S(1)}, bf16[384,256]{1,0:T(8,128)(2,1)S(1)}, u32[]{:S(2)}, u32[]{:S(2)}) collective-permute-start(bf16[384,256]{1,0:T(8,128)(2,1)S(1)} %broadcast_select_fusion), channel_id=1, source_target_pairs={{0,128},{4,132},{1,129},{5,133},{2,130},{6,134},{3,131},{7,135}} | collective-permute-start | bytes 589832 | tf_op jit(solution)/shard_map/ppermute | solution.py:217
  141.1 4.7 %collective-permute-start.7 = (bf16[384,256]{1,0:T(8,128)(2,1)S(1)}, bf16[384,256]{1,0:T(8,128)(2,1)S(1)}, u32[]{:S(2)}, u32[]{:S(2)}) collective-permute-start(bf16[384,256]{1,0:T(8,128)(2,1)S(1)} %broadcast_select_fusion.1), channel_id=1, source_target_pairs={{0,32},{4,36},{128,160},{132,164},{1,33},{5,37},{129,161},{133,165... | collective-permute-start | bytes 589832 | tf_op jit(solution)/shard_map/ppermute | solution.py:217
  146.5 3.9 %collective-permute-start.8 = (bf16[384,256]{1,0:T(8,128)(2,1)S(1)}, bf16[384,256]{1,0:T(8,128)(2,1)S(1)}, u32[]{:S(2)}, u32[]{:S(2)}) collective-permute-start(bf16[384,256]{1,0:T(8,128)(2,1)S(1)} %broadcast_select_fusion.2), channel_id=1, source_target_pairs={{0,64},{4,68},{128,192},{132,196},{32,96},{36,100},{160,224},{164,... | collective-permute-start | bytes 589832 | tf_op jit(solution)/shard_map/ppermute | solution.py:217
  151.0 3.9 %collective-permute-start.9 = (bf16[384,256]{1,0:T(8,128)(2,1)S(1)}, bf16[384,256]{1,0:T(8,128)(2,1)S(1)}, u32[]{:S(2)}, u32[]{:S(2)}) collective-permute-start(bf16[384,256]{1,0:T(8,128)(2,1)S(1)} %broadcast_select_fusion.3), channel_id=1, source_target_pairs={{0,16},{4,20},{128,144},{132,148},{32,48},{36,52},{160,176},{164,1... | collective-permute-start | bytes 589832 | tf_op jit(solution)/shard_map/ppermute | solution.py:217
  155.6 4.1 %collective-permute-start.10 = (bf16[384,256]{1,0:T(8,128)(2,1)S(1)}, bf16[384,256]{1,0:T(8,128)(2,1)S(1)}, u32[]{:S(2)}, u32[]{:S(2)}) collective-permute-start(bf16[384,256]{1,0:T(8,128)(2,1)S(1)} %broadcast_select_fusion.4), channel_id=1, source_target_pairs={{0,8},{4,12},{128,136},{132,140},{32,40},{36,44},{160,168},{164,17... | collective-permute-start | bytes 589832 | tf_op jit(solution)/shard_map/ppermute | solution.py:217
  160.4 17.1 %copy-start.5 = (f32[1280]{0:T(1024)S(1)}, f32[1280]{0:T(1024)}, u32[]{:S(2)}) copy-start(f32[1280]{0:T(1024)} %param.32) | copy-start | bytes 15364
  160.4 17.1 %copy-start.6 = (f32[1280]{0:T(1024)S(1)}, f32[1280]{0:T(1024)}, u32[]{:S(2)}) copy-start(f32[1280]{0:T(1024)} %param.33) | copy-start | bytes 15364
  162.9 10.4 %collective-permute-start.11 = (bf16[384,640]{1,0:T(8,128)(2,1)S(1)}, bf16[384,640]{1,0:T(8,128)(2,1)S(1)}, u32[]{:S(2)}, u32[]{:S(2)}) collective-permute-start(bf16[384,640]{1,0:T(8,128)(2,1)S(1)} %attend.1.att), channel_id=1, source_target_pairs={{0,1},{1,2},{2,3},{3,0},{4,5},{5,6},{6,7},{7,4},{8,9},{9,10},{10,1... | collective-permute-start | bytes 1474568 | tf_op jit(solution)/shard_map/ppermute | solution.py:34
  164.2 9.2 %collective-permute-start.12 = (bf16[384,640]{1,0:T(8,128)(2,1)S(1)}, bf16[384,640]{1,0:T(8,128)(2,1)S(1)}, u32[]{:S(2)}, u32[]{:S(2)}) collective-permute-start(bf16[384,640]{1,0:T(8,128)(2,1)S(1)} %attend.1.att), channel_id=1, source_target_pairs={{0,3},{1,0},{2,1},{3,2},{4,7},{5,4},{6,5},{7,6},{8,11},{9,8},{10,9... | collective-permute-start | bytes 1474568 | tf_op jit(solution)/shard_map/ppermute | solution.py:34
  173.4 12.5 %collective-permute-start.13 = (bf16[192,640]{1,0:T(8,128)(2,1)S(1)}, bf16[192,640]{1,0:T(8,128)(2,1)S(1)}, u32[]{:S(2)}, u32[]{:S(2)}) collective-permute-start(bf16[192,640]{1,0:T(8,128)(2,1)S(1)} %slice.131), channel_id=1, source_target_pairs={{0,1},{1,2},{2,3},{3,0},{4,5},{5,6},{6,7},{7,4},{8,9},{9,10},{10,1... | collective-permute-start | bytes 737288 | tf_op jit(solution)/shard_map/ppermute | solution.py:34
  173.5 12.4 %collective-permute-start.14 = (bf16[192,640]{1,0:T(8,128)(2,1)S(1)}, bf16[192,640]{1,0:T(8,128)(2,1)S(1)}, u32[]{:S(2)}, u32[]{:S(2)}) collective-permute-start(bf16[192,640]{1,0:T(8,128)(2,1)S(1)} %slice.132), channel_id=1, source_target_pairs={{0,3},{1,0},{2,1},{3,2},{4,7},{5,4},{6,5},{7,6},{8,11},{9,8},{10,9... | collective-permute-start | bytes 737288 | tf_op jit(solution)/shard_map/ppermute | solution.py:34
  185.9 11.2 %copy-start.9 = (s32[384]{0:T(512)S(1)}, s32[384]{0:T(512)}, u32[]{:S(2)}) copy-start(s32[384]{0:T(512)} %param.35) | copy-start | bytes 4612
  196.4 42.8 %copy-start.8 = (f32[384]{0:T(512)}, f32[384]{0:T(512)S(1)}, u32[]{:S(2)}) copy-start(f32[384]{0:T(512)S(1)} %get-tuple-element.28) | copy-start | bytes 4612
  203.3 32.2 %all-to-all-start = ((f32[64,1,128]{2,1,0:T(1,128)}), f32[64,1,128]{2,1,0:T(1,128)S(1)}, u32[]{:S(2)}, u32[]{:S(2)}) async-start(f32[64,1,128]{2,1,0:T(1,128)} %broadcast_in_dim.101), calls=%async_computation | async-start | bytes 65536 | tf_op jit(solution)/shard_map/all_to_all | solution.py:309
Sparse Core Ops, SparseCore 0:
  10.7 109.2 all-gather.1

commit v2 on v1

v2 whole, which is shorter than its diff:
```python
import jax
import jax.numpy as jnp
from jax import lax
from jax.experimental import pallas as pl
from jax.experimental.pallas import tpu as pltpu
from jax.sharding import PartitionSpec as P

D = 5120
HD = 128
HALF = HD // 2
GROUP = 5
QW = GROUP * HD

EPS = 1e-06
GAMMA = 0.99
LAMBDA = 0.95
ROPE_BASE = 1000000.0
REWARD_SCALE = 0.25

X, Z, C, T = 4, 8, 2, 4
ROWS = 384
SHARD = 80
PIECE = D // T
MIB = 1 << 20

F32 = jnp.float32
BF16 = jnp.bfloat16


def place(x, z, c):
    return (x * Z + z) * C + c


def shift_tp(block, distance):
    return lax.ppermute(block, "tp", [(i, (i + distance) % T) for i in range(T)])


def ring_tp(block):
    half = block.shape[0] // 2
    below = shift_tp(block, 1)
    above = shift_tp(block, -1)
    first = shift_tp(below[:half], 1)
    second = shift_tp(above[half:], -1)
    return block, below, above, first, second


def params(mib=40):
    return pltpu.CompilerParams(vmem_limit_bytes=mib * MIB)


def interleave(core, own, other, joined):
    joined[:, pl.ds(core, 1)] = own[...].reshape(own.shape[-3], 1, *own.shape[-2:])
    joined[:, pl.ds(1 - core, 1)] = other[...].reshape(other.shape[-3], 1, *other.shape[-2:])
    return joined[...].reshape(-1, joined.shape[-1])


def turned(u, cosine, sine):
    return u * cosine[...] + pltpu.roll(u, HALF, 1) * sine[...]


def project_kv_kernel(
    order, own, below, above, first, second, gain, w_own, w_other, bias, cosine, sine, normed_out, kv_out, scale, acc, joined
):
    step = pl.program_id(0)
    half = first.shape[0]

    @pl.when(step == 0)
    def _():
        def squares(ref):
            x = ref[...].astype(F32)
            return jnp.sum(x * x, axis=-1, keepdims=True)

        far = jnp.concatenate([squares(first), squares(second)], axis=0)
        mean = (squares(own) + squares(below) + squares(above) + far) / D
        scale[...] = lax.rsqrt(mean + EPS)
        acc[...] = jnp.zeros_like(acc)

    def norm(x, rows):
        normed_out[0, rows, :] = (x.astype(F32) * scale[rows, :] * gain[0]).astype(BF16)

    for at, ref in enumerate((own, below, above)):

        @pl.when(step == at)
        def _(ref=ref):
            norm(ref[...], pl.ds(0, ROWS))

    @pl.when(step == T - 1)
    def _():
        norm(first[...], pl.ds(0, half))
        norm(second[...], pl.ds(half, half))

    w = interleave(order[T], w_own, w_other, joined)
    acc[...] += jnp.dot(normed_out[0], w, preferred_element_type=F32)

    @pl.when(step == T - 1)
    def _():
        kv_out[:, :HD] = turned(acc[:, :HD] + bias[:, :HD], cosine, sine).astype(BF16)
        kv_out[:, HD:] = (acc[:, HD:] + bias[:, HD:]).astype(BF16)


def whole(*shape):
    return pl.BlockSpec(shape, lambda k, order: (0,) * len(shape))


def shard_rows(n):
    return pl.BlockSpec((1, Z, SHARD, n), lambda k, order: (order[k], 0, 0, 0))


def project_kv(order, pieces, gain, w_own, w_other, bias, cosine, sine):
    grid = pltpu.PrefetchScalarGridSpec(
        num_scalar_prefetch=1,
        grid=(T,),
        in_specs=[whole(*piece.shape) for piece in pieces]
        + [
            pl.BlockSpec((1, 1, PIECE), lambda k, order: (order[k], 0, 0)),
            shard_rows(2 * HD),
            shard_rows(2 * HD),
            whole(1, 2 * HD),
            whole(ROWS, HD),
            whole(ROWS, HD),
        ],
        out_specs=[pl.BlockSpec((1, ROWS, PIECE), lambda k, order: (k, 0, 0)), whole(ROWS, 2 * HD)],
        scratch_shapes=[
            pltpu.VMEM((ROWS, 1), F32),
            pltpu.VMEM((ROWS, 2 * HD), F32),
            pltpu.VMEM((Z, C, SHARD, 2 * HD), BF16),
        ],
    )
    return pl.pallas_call(
        project_kv_kernel,
        grid_spec=grid,
        out_shape=[
            jax.ShapeDtypeStruct((T, ROWS, PIECE), BF16),
            jax.ShapeDtypeStruct((ROWS, 2 * HD), BF16),
        ],
        compiler_params=params(),
        cost_estimate=pl.CostEstimate(flops=4 * ROWS * D * HD, bytes_accessed=2 * D * (2 * HD + 2 * ROWS), transcendentals=0),
        name="project_kv",
    )(order, *pieces, gain, w_own, w_other, bias, cosine, sine)


def project_q_kernel(order, normed, w, bias, cosine, sine, q_out, acc):
    step = pl.program_id(0)

    @pl.when(step == 0)
    def _():
        acc[...] = jnp.zeros_like(acc)

    acc[...] += jnp.dot(normed[0], w[...], preferred_element_type=F32)

    @pl.when(step == T - 1)
    def _():
        for head in range(GROUP):
            span = slice(head * HD, (head + 1) * HD)
            q_out[:, span] = turned(acc[:, span] + bias[:, span], cosine, sine).astype(BF16)


def project_q(order, normed, w, bias, cosine, sine):
    grid = pltpu.PrefetchScalarGridSpec(
        num_scalar_prefetch=1,
        grid=(T,),
        in_specs=[
            pl.BlockSpec((1, ROWS, PIECE), lambda k, order: (k, 0, 0)),
            pl.BlockSpec((PIECE, QW), lambda k, order: (order[k], 1)),
            whole(1, QW),
            whole(ROWS, HD),
            whole(ROWS, HD),
        ],
        out_specs=whole(ROWS, QW),
        scratch_shapes=[pltpu.VMEM((ROWS, QW), F32)],
    )
    return pl.pallas_call(
        project_q_kernel,
        grid_spec=grid,
        out_shape=jax.ShapeDtypeStruct((ROWS, QW), BF16),
        compiler_params=params(),
        cost_estimate=pl.CostEstimate(flops=2 * ROWS * D * QW, bytes_accessed=2 * D * (QW + ROWS), transcendentals=0),
        name="project_q",
    )(order, normed, w, bias, cosine, sine)


def attend_kernel(index, q, kv, anchor, out, bias):
    keep_anchor = jnp.full((ROWS, ROWS), index[0], jnp.int32) > 0
    row = lax.broadcasted_iota(jnp.int32, (ROWS, ROWS), 0)
    col = lax.broadcasted_iota(jnp.int32, (ROWS, ROWS), 1)
    bias[:, :ROWS] = jnp.where(keep_anchor, 0.0, -jnp.inf)
    bias[:, ROWS:] = jnp.where(row >= col, 0.0, -jnp.inf)
    keys = jnp.concatenate([anchor[:, :HD], kv[:, :HD]], axis=0)
    vals = jnp.concatenate([anchor[:, HD:], kv[:, HD:]], axis=0)
    for head in range(GROUP):
        span = slice(head * HD, (head + 1) * HD)
        scores = lax.dot_general(q[:, span], keys, (((1,), (1,)), ((), ())), preferred_element_type=F32)
        scores = scores * (HD**-0.5) + bias[...]
        peak = jnp.max(scores, axis=-1, keepdims=True)
        weights = jnp.exp(scores - peak)
        total = jnp.sum(weights, axis=-1, keepdims=True)
        mixed = jnp.dot(weights.astype(BF16), vals, preferred_element_type=F32)
        out[:, span] = (mixed / total).astype(BF16)


def attend(index, q, kv, anchor):
    vmem = pl.BlockSpec(memory_space=pltpu.VMEM)
    return pl.pallas_call(
        attend_kernel,
        in_specs=[pl.BlockSpec(memory_space=pltpu.SMEM), vmem, vmem, vmem],
        out_specs=vmem,
        out_shape=jax.ShapeDtypeStruct((ROWS, QW), BF16),
        scratch_shapes=[pltpu.VMEM((ROWS, 2 * ROWS), F32)],
        compiler_params=params(),
        cost_estimate=pl.CostEstimate(
            flops=4 * ROWS * 2 * ROWS * QW, bytes_accessed=4 * ROWS * QW, transcendentals=ROWS * 2 * ROWS * GROUP
        ),
        name="attend",
    )(index, q, kv, anchor)


def times(a, w):
    return lax.dot_general(a, w, (((1,), (1,)), ((), ())), preferred_element_type=F32)


def out_own_kernel(order, tokens, att, w, out):
    out[...] = tokens[...].astype(F32) + times(att[...], w[...])


def out_next_kernel(order, total, below, above, w_below, w_above, out):
    some = total[...] + times(below[...], w_below[...])
    out[...] = some + times(above[...], w_above[...])


def out_last_kernel(order, total, first, second, w_far, gain, head, resid_out, stats_out):
    half = first.shape[0]
    lane = lax.broadcasted_iota(jnp.int32, (half, HD), 1)
    w = w_far[...]
    for at, ref in enumerate((first, second)):
        rows = pl.ds(at * half, half)
        resid = total[rows, :] + times(ref[...], w)
        resid_out[rows, :] = resid.astype(BF16)
        squares = jnp.sum(resid * resid, axis=-1, keepdims=True)
        products = jnp.sum(resid * gain[...] * head[...], axis=-1, keepdims=True)
        both = jnp.where(lane == 0, squares, products)
        stats_out[at] = both.T[:8, :]


def out_call(kernel, order, operands, w, picks, extra, out_shape, name):
    spec = lambda at: pl.BlockSpec((PIECE, QW), lambda i, order, at=at: (order[at], 0))
    grid = pltpu.PrefetchScalarGridSpec(
        num_scalar_prefetch=1,
        grid=(1,),
        in_specs=[whole(*o.shape) for o in operands] + [spec(at) for at in picks] + [whole(*e.shape) for e in extra],
        out_specs=jax.tree.map(lambda s: whole(*s.shape), out_shape),
    )
    return pl.pallas_call(
        kernel,
        grid_spec=grid,
        out_shape=out_shape,
        compiler_params=params(),
        cost_estimate=pl.CostEstimate(
            flops=2 * ROWS * QW * PIECE * len(picks), bytes_accessed=6 * MIB, transcendentals=0
        ),
        name=name,
    )(order, *operands, *([w] * len(picks)), *extra)


def values_kernel(stats, critic_bias, reward, discount, matrix, tail, edge, values_out, local_out, records_out):
    sums = stats[0] + stats[1] + stats[2] + stats[3]
    values = sums[1:2] * lax.rsqrt(sums[0:1] / D + EPS) + critic_bias[0]
    lane = lax.broadcasted_iota(jnp.int32, (1, ROWS), 1)
    following = jnp.where(lane == ROWS - 1, 0.0, pltpu.roll(values, ROWS - 1, 1))
    delta = reward[...] + discount[...] * following - values
    local = lax.dot_general(
        jnp.broadcast_to(delta, (8, ROWS)),
        matrix[...],
        (((1,), (1,)), ((), ())),
        precision=lax.Precision.HIGHEST,
        preferred_element_type=F32,
    )[0:1]
    values_out[...] = values
    local_out[...] = local
    head = lane[:, :HD] == 0
    record = jnp.zeros((1, HD), F32)
    for at, row in enumerate((values, local, tail[...], edge[...])):
        first = jnp.sum(jnp.where(head, row[:, :HD], 0.0), axis=-1, keepdims=True)
        record = jnp.where(lane[:, :HD] == at, first, record)
    records_out[...] = jnp.broadcast_to(record, records_out.shape)


def advantages_kernel(index, records, local, tail, edge, out):
    n = records.shape[0]
    row = lax.broadcasted_iota(jnp.int32, (n, HD), 0)

    def column(at):
        return jnp.broadcast_to(records[:, at : at + 1], (n, HD))

    def later(x, distance, fill):
        return jnp.where(row < n - distance, pltpu.roll(x, n - distance, 0), fill)

    first = column(0)
    term = column(1) + column(3) * later(first, 1, 0.0)
    decay = column(2)
    distance = 1
    while distance < n:
        term = term + decay * later(term, distance, 0.0)
        decay = decay * later(decay, distance, 1.0)
        distance *= 2
    after = row == index[0] + 1
    carry = jnp.sum(jnp.where(after, term, 0.0), axis=0, keepdims=True)
    value = jnp.sum(jnp.where(after, first, 0.0), axis=0, keepdims=True)
    for at in range(0, ROWS, HD):
        span = slice(at, at + HD)
        out[:, span] = local[:, span] + edge[:, span] * value + tail[:, span] * carry


def small_call(kernel, operands, scalars, out_shape, name):
    vmem = pl.BlockSpec(memory_space=pltpu.VMEM)
    smem = pl.BlockSpec(memory_space=pltpu.SMEM)
    return pl.pallas_call(
        kernel,
        in_specs=[smem if at in scalars else vmem for at in range(len(operands))],
        out_specs=jax.tree.map(lambda s: vmem, out_shape),
        out_shape=out_shape,
        compiler_params=params(),
        cost_estimate=pl.CostEstimate(flops=2 * ROWS * ROWS, bytes_accessed=MIB, transcendentals=0),
        name=name,
    )(*operands)


def gather_by_all_to_all(block, axis, groups, n):
    everywhere = jnp.broadcast_to(block[None], (n, *block.shape))
    return lax.all_to_all(everywhere, axis, 0, 0, axis_index_groups=groups)


Z_GROUPS = [[place(x, z, c) for z in range(Z)] for x in range(X) for c in range(C)]
X_GROUPS = [[place(x, z, c) for x in range(X)] for z in range(Z) for c in range(C)]


def other_core(block):
    return lax.ppermute(block, "ctx", [(i, i ^ 1) for i in range(X * Z * C)])


def broadcast_anchor(block):
    here = lax.axis_index("ctx")
    at = (here // (Z * C), here // C % Z, here % C)
    holders = [(0, 0, 0)]
    for stage in (((1, 0, 0), (3, 0, 0), (2, 0, 0)), ((0, 2, 0), (0, 6, 0), (0, 4, 0)), ((0, 1, 0),), ((0, 0, 1),)):
        holding = jnp.ones((), jnp.bool_)
        for axis in range(3):
            seen = sorted({h[axis] for h in holders})
            holding &= sum((at[axis] == v).astype(jnp.int32) for v in seen) > 0
        fresh, sent = [], None
        for dx, dz, dc in stage:
            targets = [((x + dx) % X, (z + dz) % Z, (c + dc) % C) for x, z, c in holders]
            got = lax.ppermute(block, "ctx", [(place(*a), place(*b)) for a, b in zip(holders, targets)])
            sent = got if sent is None else sent + got
            fresh += targets
        block = jnp.where(holding, block, sent)
        holders = holders + fresh
    return block


def on_device(
    tokens,
    input_gain,
    w_query,
    w_key,
    w_value,
    query_bias,
    key_bias,
    value_bias,
    w_out,
    final_gain,
    critic_head,
    critic_bias,
    rewards,
    turn_ends,
    episode_done,
):
    index = lax.axis_index("ctx")
    mine = lax.axis_index("tp")
    order = jnp.stack([mine, (mine + 3) % T, (mine + 1) % T, (mine + 2) % T, index % C]).astype(jnp.int32)

    corner = [
        (place(x, z, c) * T + y, place(y, z, c) * T + x) for x in range(X) for z in range(Z) for c in range(C) for y in range(T)
    ]
    out_block = lax.ppermute(w_out.T, ("ctx", "tp"), corner)
    weights = lax.all_gather(jnp.concatenate([out_block, w_query], axis=1), "ctx", axis=0, tiled=True)

    half = ROWS // 2
    below, above = shift_tp(tokens, 1), shift_tp(tokens, -1)
    kv_part = gather_by_all_to_all(jnp.concatenate([w_key, w_value], axis=1), "ctx", Z_GROUPS, Z)
    below, above, kv_part = lax.optimization_barrier((below, above, kv_part))
    first, second = shift_tp(below[:half], 1), shift_tp(above[half:], -1)
    kv_own = gather_by_all_to_all(kv_part, "ctx", X_GROUPS, X)
    first, second, kv_own = lax.optimization_barrier((first, second, kv_own))
    pieces = (tokens, below, above, first, second)
    kv_other = other_core(kv_own)

    positions = (index * ROWS + jnp.arange(ROWS)).astype(F32)
    steps = jnp.arange(HALF).astype(F32)
    inverse = 1.0 / ROPE_BASE ** (steps * 2.0 / HD)
    angle = positions[:, None] * inverse[None, :]
    cosine, sine = jnp.cos(angle), jnp.sin(angle)
    cosine = jnp.concatenate([cosine, cosine], axis=1)
    sine = jnp.concatenate([-sine, sine], axis=1)
    kv_bias = jnp.concatenate([key_bias, value_bias])[None, :]
    normed, kv = project_kv(order, pieces, input_gain.reshape(T, 1, PIECE), kv_own, kv_other, kv_bias, cosine, sine)
    anchor = broadcast_anchor(kv)
    query = project_q(order, normed, weights, query_bias[None, :], cosine, sine)
    att = attend(index.astype(jnp.int32)[None], query, kv, anchor)

    own, below, above, first, second = ring_tp(att)
    wide = jax.ShapeDtypeStruct((ROWS, PIECE), F32)
    total = out_call(out_own_kernel, order, [tokens, own], weights, (0,), [], wide, "out_own")
    total = out_call(out_next_kernel, order, [total, below, above], weights, (1, 2), [], wide, "out_next")
    residual_stream, stats = out_call(
        out_last_kernel,
        order,
        [total, first, second],
        weights,
        (3,),
        [final_gain[None, :], critic_head[None, :]],
        [jax.ShapeDtypeStruct((ROWS, PIECE), BF16), jax.ShapeDtypeStruct((2, 8, ROWS // 2), F32)],
        "out_last",
    )
    stats = gather_by_all_to_all(jnp.concatenate([stats[0], stats[1]], axis=1), "tp", None, T)

    ends = jnp.maximum(turn_ends, episode_done)
    discount = jnp.where(ends > 0, GAMMA, 1.0).astype(F32) * (1 - episode_done).astype(F32)
    reward = REWARD_SCALE * (rewards * ends).astype(F32)
    decaying = ends * (1 - episode_done)
    zero_int = jnp.zeros((1,), jnp.int32)
    decay_count = jnp.concatenate([zero_int, jnp.cumsum(decaying)])
    done_count = jnp.concatenate([zero_int, jnp.cumsum(episode_done)])
    rate = GAMMA * LAMBDA
    later = jnp.arange(ROWS)[None, :] >= jnp.arange(ROWS)[:, None]
    same_episode = done_count[None, :ROWS] == done_count[:ROWS, None]
    powers = (decay_count[None, :ROWS] - decay_count[:ROWS, None]).astype(F32)
    matrix = jnp.where(later & same_episode, jnp.power(rate, powers), 0.0)
    tail_powers = (decay_count[ROWS] - decay_count[:ROWS]).astype(F32)
    tail = jnp.where(done_count[ROWS] == done_count[:ROWS], jnp.power(rate, tail_powers), 0.0)[None, :]
    edge = (matrix[:, ROWS - 1] * discount[ROWS - 1])[None, :]

    n = lax.axis_size("ctx")
    line = jax.ShapeDtypeStruct((1, ROWS), F32)
    values, local, records = small_call(
        values_kernel,
        [stats, critic_bias, reward[None, :], discount[None, :], matrix, tail, edge],
        (1,),
        [line, line, jax.ShapeDtypeStruct((n, HD), F32)],
        "values",
    )
    records = lax.all_to_all(records, "ctx", 0, 0, tiled=True)
    advantages = small_call(
        advantages_kernel, [index.astype(jnp.int32)[None], records, local, tail, edge], (0,), line, "advantages"
    )
    return (residual_stream, values[0], advantages[0])


def solution(mesh):
    in_specs = (
        P("ctx", "tp"),
        P(),
        P("ctx", "tp"),
        P("ctx", "tp"),
        P("ctx", "tp"),
        P("tp"),
        P("tp"),
        P("tp"),
        P("tp", "ctx"),
        P("tp"),
        P("tp"),
        P(),
        P("ctx"),
        P("ctx"),
        P("ctx"),
    )
    out_specs = (P("ctx", "tp"), P("ctx"), P("ctx"))
    return jax.shard_map(
        on_device, mesh=mesh, in_specs=in_specs, out_specs=out_specs, check_vma=False
    )
```

time: 247 us -> 201 us (0.81)
  waiting for transfers between devices: 116 us -> 60.7 us
  blocking collectives: 6.06 us -> 20.4 us
  Pallas kernels: 22.8 us -> 30 us
  other arithmetic: 14 us -> 8.02 us
  local copies, waits for them, and re-layouts: 16.1 us -> 13 us
  starting transfers between devices: 55.3 us -> 52.5 us
    all_gather x1, waiting for transfers between devices: 60.6 us -> 0.02 us  [on_device(): lax.all_gather(jnp.concatenate([out_block, w_query], axis=1), 'ctx', axis...]
    all_to_all x0 -> x1, blocking collectives: none -> 20.4 us  [gather_by_all_to_all(): return lax.all_to_all(everywhere, axis, 0, 0, axis_index_groups=groups)]
    ppermute x8, waiting for transfers between devices: 35.6 us -> 16.1 us  [shift_tp(): lax.ppermute(block, 'tp', [(i, (i + distance) % T) for i in range(T)])]
    ppermute x6 -> x8, waiting for transfers between devices: 10.6 us -> 29.6 us  [broadcast_anchor(): lax.ppermute(block, 'ctx', [(place(*a), place(*b)) for a, b in zip(holder...]
    all_to_all x1, starting transfers between devices: 22.9 us -> 9.85 us  [on_device(): records = lax.all_to_all(records, 'ctx', 0, 0, tiled=True)]
    all_to_all x0 -> x2, starting transfers between devices: none -> 6.95 us  [gather_by_all_to_all(): return lax.all_to_all(everywhere, axis, 0, 0, axis_index_groups=groups)]
    pallas_call x1 -> x4, Pallas kernels: 8.92 us -> 15.2 us  [the longest x1 6.86 us: project_kv(): pl.pallas_call(project_kv_kernel, grid_spec=grid, out_shape=[jax.ShapeDty...]
    unnamed x28 -> x36, local copies, waits for them, and re-layouts: 1.56 us -> 7.78 us
  transfers between devices with their start and end apart: 17 -> 22, of which waited for: 11 -> 9; matrix products, arithmetic and copies ran while one was open for 5% -> 5% of each run, Pallas kernels for 3% -> 7%
where the time goes in v2:
time: 201 us; the launch traced here: 200 us
  waiting for transfers between devices  60.7 us (30%)
  starting transfers between devices  52.5 us (26%)
  Pallas kernels  30 us (15%)
  blocking collectives  20.4 us (10%)
  between operations  15.1 us (8%)
  local copies, waits for them, and re-layouts  13 us (6%)
  other arithmetic  8.02 us (4%)
    ppermute x8, waiting for transfers between devices, broadcast_anchor(): lax.ppermute(block, 'ctx', [(place(*a), place(*b)) for a, b in zip(holder...  29.6 us
    ppermute x8, starting transfers between devices, shift_tp(): lax.ppermute(block, 'tp', [(i, (i + distance) % T) for i in range(T)])  22.5 us
    all_to_all x1, blocking collectives, gather_by_all_to_all(): return lax.all_to_all(everywhere, axis, 0, 0, axis_index_groups=groups)  20.4 us
    ppermute x8, waiting for transfers between devices, shift_tp(): lax.ppermute(block, 'tp', [(i, (i + distance) % T) for i in range(T)])  16.1 us
    pallas_call x3, Pallas kernels, out_call(): pl.pallas_call(kernel, grid_spec=grid, out_shape=out_shape, compiler_para...  11.5 us
    all_to_all x1, starting transfers between devices, on_device(): records = lax.all_to_all(records, 'ctx', 0, 0, tiled=True)  9.85 us
    all_to_all x1, waiting for transfers between devices, on_device(): records = lax.all_to_all(records, 'ctx', 0, 0, tiled=True)  8.69 us
    unnamed x36, local copies, waits for them, and re-layouts  7.78 us
  transfers between devices with their start and end apart: 22, of which 9 were waited for; matrix products, arithmetic and copies ran while one was open for 5% of the time, Pallas kernels for 7%

profile of v2, /device:TPU:1, one launch (start us, length us, event | category | flops | bytes accessed | tf_op | source)
XLA Modules:
  0.0 199.7 jit_solution(5498240756934699076)
XLA Ops:
  7.2 1.6 collective-permute-start.5
  8.8 1.6 pad_maximum_fusion
  10.4 7.2 %collective-permute-start = (bf16[384,1280]{1,0:T(8,128)(2,1)}, bf16[384,1280]{1,0:T(8,128)(2,1)S(1)}, u32[]{:S(2)}, u32[]{:S(2)}) collective-permute-start(bf16[384,1280]{1,0:T(8,128)(2,1)} %tokens.1), channel_id=1, source_target_pairs={{0,1},{1,2},{2,3},{3,0},{4,5},{5,6},{6,7},{7,4},{8,9},{9,10},{10,1... | collective-permute-start | bytes 2949128 | tf_op jit(solution)/shard_map/ppermute | solution.py:35
  17.5 6.9 %collective-permute-start.1 = (bf16[384,1280]{1,0:T(8,128)(2,1)}, bf16[384,1280]{1,0:T(8,128)(2,1)}, u32[]{:S(2)}, u32[]{:S(2)}) collective-permute-start(bf16[384,1280]{1,0:T(8,128)(2,1)} %tokens.1), channel_id=1, source_target_pairs={{0,3},{1,0},{2,1},{3,2},{4,7},{5,4},{6,5},{7,6},{8,11},{9,8},{10,9... | collective-permute-start | bytes 2949128 | tf_op jit(solution)/shard_map/ppermute | solution.py:35
  25.3 20.4 %all_to_all.26 = bf16[8,80,256]{2,1,0:T(8,128)(2,1)S(1)} all-to-all(bf16[8,80,256]{2,1,0:T(8,128)(2,1)S(1)} %broadcast_in_dim.69), channel_id=1, replica_groups={{0,8,16,24,32,40,48,56},{4,12,20,28,36,44,52,60},{64,72,80,88,96,104,11..., dimensions={0} | all-to-all | bytes 655360 | tf_op jit(solution)/shard_map/all_to_all | solution.py:329
  47.0 3.7 %all-to-all-start.1 = ((bf16[4,8,80,256]{3,2,1,0:T(8,128)(2,1)}), bf16[4,8,80,256]{3,2,1,0:T(8,128)(2,1)S(1)}, u32[]{:S(2)}, u32[]{:S(2)}) async-start(bf16[4,8,80,256]{3,2,1,0:T(8,128)(2,1)} %broadcast_in_dim.70), calls=%async_computation.1 | async-start | bytes 2621440 | tf_op jit(solution)/shard_map/all_to_all | solution.py:329
  52.5 2.2 %collective-permute-start.3 = (bf16[192,1280]{1,0:T(8,128)(2,1)S(1)}, bf16[192,1280]{1,0:T(8,128)(2,1)S(1)}, u32[]{:S(2)}, u32[]{:S(2)}) collective-permute-start(bf16[192,1280]{1,0:T(8,128)(2,1)S(1)} %slice.55), channel_id=1, source_target_pairs={{0,3},{1,0},{2,1},{3,2},{4,7},{5,4},{6,5},{7,6},{8,11},{9,8},{10,9... | collective-permute-start | bytes 1474568 | tf_op jit(solution)/shard_map/ppermute | solution.py:35
  54.7 6.0 %collective-permute-done.2.first = bf16[192,1280]{1,0:T(8,128)(2,1)S(1)} collective-permute-done((bf16[192,1280]{1,0:T(8,128)(2,1)S(1)}, bf16[192,1280]{1,0:T(8,128)(2,1)S(1)}, u32[]{:S(2)}, u32[]{:S(2)}) %collective-permute-start.2) | collective-permute-done | bytes 491552 | tf_op jit(solution)/shard_map/ppermute | solution.py:35
  62.4 1.8 all-to-all-done.1.w_own
  64.2 5.3 %collective-permute-start.4 = (bf16[4,8,80,256]{3,2,1,0:T(8,128)(2,1)S(1)}, bf16[4,8,80,256]{3,2,1,0:T(8,128)(2,1)}, u32[]{:S(2)}, u32[]{:S(2)}) collective-permute-start(bf16[4,8,80,256]{3,2,1,0:T(8,128)(2,1)S(1)} %all-to-all-done.1.w_own), channel_id=1, source_target_pairs={{0,4},{4,0},{8,12},{12,8},{16,20},{20,16},{24,28},{28,24},{32,36},... | collective-permute-start | bytes 3932168 | tf_op jit(solution)/shard_map/ppermute | solution.py:337
  70.6 1.7 collective-permute-done.4.w_other
  72.3 1.2 copy-done.6
  74.5 6.9 %project_kv.1 = (bf16[4,384,1280]{2,1,0:T(8,128)(2,1)S(1)}, bf16[384,256]{1,0:T(8,128)(2,1)}) custom-call(s32[5]{0:T(128)S(1)} %stack.23.order, bf16[384,1280]{1,0:T(8,128)(2,1)S(1)} %copy-done.2, bf16[384,1280]{1,0:T(8,128)(2,1)S(1)} %collective-permute-done.below, bf16[384,1280]{1,0:T(8,128)(2,1)} %collective-permute-done.1.above, ...), custom_call_target="tpu_custom_call" | custom-call | flops 1006632960 | bytes 10485760 | tf_op jit(solution)/shard_map/project_kv/pallas_call | solution.py:129
  81.4 1.8 copy-done
  89.5 1.5 collective-permute-start.13
  91.0 29.6 %collective-permute-done.13 = bf16[384,256]{1,0:T(8,128)(2,1)S(1)} collective-permute-done((bf16[384,256]{1,0:T(8,128)(2,1)S(1)}, bf16[384,256]{1,0:T(8,128)(2,1)S(1)}, u32[]{:S(2)}, u32[]{:S(2)}) %collective-permute-start.13) | collective-permute-done | bytes 196640 | tf_op jit(solution)/shard_map/ppermute | solution.py:352
  120.7 2.1 %copy-done.1 = bf16[4,384,1280]{2,1,0:T(8,128)(2,1)S(1)} copy-done((bf16[4,384,1280]{2,1,0:T(8,128)(2,1)S(1)}, bf16[4,384,1280]{2,1,0:T(8,128)(2,1)}, u32[]{:S(2)}) %copy-start.1) | copy-done | bytes 3932184
  122.8 6.9 %project_q.1.q = bf16[384,640]{1,0:T(8,128)(2,1)S(1)} custom-call(s32[5]{0:T(128)S(1)} %stack.23.order, bf16[4,384,1280]{2,1,0:T(8,128)(2,1)S(1)} %copy-done.1, bf16[5120,1280]{1,0:T(8,128)(2,1)} %all-gather.2.cloned.1.call-done.w.w_below.w_above.w_far, f32[1,640]{1,0:T(1,128)S(1)} %broadcast_in_dim.72.bias, f32[384,128]{1,0:T(8,128)S(1)} %get-tuple-element.36.cosine, ...), custom_call_target="tpu_custom_call" | custom-call | flops 2516582400 | bytes 10485760 | tf_op jit(solution)/shard_map/project_q/pallas_call | solution.py:172
  129.7 3.3 %attend.1.att = bf16[384,640]{1,0:T(8,128)(2,1)S(1)} custom-call(s32[1]{0:T(128)} %bitcast.5.index, bf16[384,640]{1,0:T(8,128)(2,1)S(1)} %project_q.1.q, bf16[384,256]{1,0:T(8,128)(2,1)} %get-tuple-element.23.kv, bf16[384,256]{1,0:T(8,128)(2,1)S(1)} %broadcast_select_fusion.1.anchor), custom_call_target="tpu_custom_call" | custom-call | flops 754974720 | bytes 983040 | tf_op jit(solution)/shard_map/attend/pallas_call | solution.py:203
  133.0 1.3 collective-permute-start.14
  134.3 1.5 collective-permute-start.15
  137.3 9.7 %collective-permute-done.14.below = bf16[384,640]{1,0:T(8,128)(2,1)S(1)} collective-permute-done((bf16[384,640]{1,0:T(8,128)(2,1)S(1)}, bf16[384,640]{1,0:T(8,128)(2,1)S(1)}, u32[]{:S(2)}, u32[]{:S(2)}) %collective-permute-start.14) | collective-permute-done | bytes 491552 | tf_op jit(solution)/shard_map/ppermute | solution.py:35
  147.2 2.7 %collective-permute-start.17 = (bf16[192,640]{1,0:T(8,128)(2,1)S(1)}, bf16[192,640]{1,0:T(8,128)(2,1)S(1)}, u32[]{:S(2)}, u32[]{:S(2)}) collective-permute-start(bf16[192,640]{1,0:T(8,128)(2,1)S(1)} %slice.71), channel_id=1, source_target_pairs={{0,3},{1,0},{2,1},{3,2},{4,7},{5,4},{6,5},{7,6},{8,11},{9,8},{10,9... | collective-permute-start | bytes 737288 | tf_op jit(solution)/shard_map/ppermute | solution.py:35
  149.9 1.3 power_select_fusion.1
  151.8 2.9 %out_own.1.total = f32[384,1280]{1,0:T(8,128)S(1)} custom-call(s32[5]{0:T(128)S(1)} %stack.23.order, bf16[384,1280]{1,0:T(8,128)(2,1)S(1)} %copy-done.2, bf16[384,640]{1,0:T(8,128)(2,1)S(1)} %attend.1.att, bf16[5120,1280]{1,0:T(8,128)(2,1)} %all-gather.2.cloned.1.call-done.w.w_below.w_above.w_far), custom_call_target="tpu_custom_call" | custom-call | flops 629145600 | bytes 6291456 | tf_op jit(solution)/shard_map/out_own/pallas_call | solution.py:252
  154.8 4.2 %out_next.1.total = f32[384,1280]{1,0:T(8,128)S(1)} custom-call(s32[5]{0:T(128)S(1)} %stack.23.order, f32[384,1280]{1,0:T(8,128)S(1)} %out_own.1.total, bf16[384,640]{1,0:T(8,128)(2,1)S(1)} %collective-permute-done.14.below, bf16[384,640]{1,0:T(8,128)(2,1)S(1)} %collective-permute-done.15.above, ...), custom_call_target="tpu_custom_call" | custom-call | flops 1258291200 | bytes 6291456 | tf_op jit(solution)/shard_map/out_next/pallas_call | solution.py:252
  159.0 4.3 %out_last.1 = (bf16[384,1280]{1,0:T(8,128)(2,1)}, f32[2,8,192]{2,1,0:T(8,128)S(1)}) custom-call(s32[5]{0:T(128)S(1)} %stack.23.order, f32[384,1280]{1,0:T(8,128)S(1)} %out_next.1.total, bf16[192,640]{1,0:T(8,128)(2,1)S(1)} %collective-permute-done.16.first, bf16[192,640]{1,0:T(8,128)(2,1)S(1)} %collective-permute-done.17.second, ...), custom_call_target="tpu_custom_call" | custom-call | flops 629145600 | bytes 6291456 | tf_op jit(solution)/shard_map/out_last/pallas_call | solution.py:252
  164.0 3.3 %all-to-all-start.2 = ((f32[4,8,384]{2,1,0:T(8,128)}), f32[4,8,384]{2,1,0:T(8,128)S(1)}, u32[]{:S(2)}, u32[]{:S(2)}) async-start(f32[4,8,384]{2,1,0:T(8,128)} %broadcast_in_dim.75), calls=%async_computation.2 | async-start | bytes 98304 | tf_op jit(solution)/shard_map/all_to_all | solution.py:329
  168.9 2.8 %all-to-all-done.2.stats = f32[4,8,384]{2,1,0:T(8,128)S(1)} async-done(((f32[4,8,384]{2,1,0:T(8,128)}), f32[4,8,384]{2,1,0:T(8,128)S(1)}, u32[]{:S(2)}, u32[]{:S(2)}) %all-to-all-start.2) | async-done | bytes 49184 | tf_op jit(solution)/shard_map/all_to_all | solution.py:329
  171.7 1.3 values.1
  173.0 9.9 %all-to-all-start.3 = ((f32[64,1,128]{2,1,0:T(1,128)}), f32[64,1,128]{2,1,0:T(1,128)S(1)}, u32[]{:S(2)}, u32[]{:S(2)}) async-start(f32[64,1,128]{2,1,0:T(1,128)} %bitcast.19), calls=%async_computation.3 | async-start | bytes 65536 | tf_op jit(solution)/shard_map/all_to_all | solution.py:451
  183.5 8.7 %all-to-all-done.3 = f32[64,1,128]{2,1,0:T(1,128)S(1)} async-done(((f32[64,1,128]{2,1,0:T(1,128)}), f32[64,1,128]{2,1,0:T(1,128)S(1)}, u32[]{:S(2)}, u32[]{:S(2)}) %all-to-all-start.3) | async-done | bytes 32800 | tf_op jit(solution)/shard_map/all_to_all | solution.py:451
  (107 shorter events, 19.1 us)
Async XLA Ops:
  7.2 113.5 %all-gather.2.cloned.1.call-start = ((), (), s32[]{:S(2)}) async-start(), calls=%async_computation.4 | async-start | bytes 13312000 | tf_op jit(solution)/shard_map/all_gather | solution.py:385
  7.2 1.6 collective-permute-start.5
  10.4 35.5 %collective-permute-start = (bf16[384,1280]{1,0:T(8,128)(2,1)}, bf16[384,1280]{1,0:T(8,128)(2,1)S(1)}, u32[]{:S(2)}, u32[]{:S(2)}) collective-permute-start(bf16[384,1280]{1,0:T(8,128)(2,1)} %tokens.1), channel_id=1, source_target_pairs={{0,1},{1,2},{2,3},{3,0},{4,5},{5,6},{6,7},{7,4},{8,9},{9,10},{10,1... | collective-permute-start | bytes 2949128 | tf_op jit(solution)/shard_map/ppermute | solution.py:35
  17.5 28.3 %collective-permute-start.1 = (bf16[384,1280]{1,0:T(8,128)(2,1)}, bf16[384,1280]{1,0:T(8,128)(2,1)}, u32[]{:S(2)}, u32[]{:S(2)}) collective-permute-start(bf16[384,1280]{1,0:T(8,128)(2,1)} %tokens.1), channel_id=1, source_target_pairs={{0,3},{1,0},{2,1},{3,2},{4,7},{5,4},{6,5},{7,6},{8,11},{9,8},{10,9... | collective-permute-start | bytes 2949128 | tf_op jit(solution)/shard_map/ppermute | solution.py:35
  47.0 22.5 %copy-start.14 = (f32[640]{0:T(1024)S(1)}, f32[640]{0:T(1024)}, u32[]{:S(2)}) copy-start(f32[640]{0:T(1024)} %param.20) | copy-start | bytes 7684
  47.0 22.6 %copy-start.16 = (f32[128]{0:T(128)S(1)}, f32[128]{0:T(128)}, u32[]{:S(2)}) copy-start(f32[128]{0:T(128)} %param.22) | copy-start | bytes 1540
  47.0 22.6 %copy-start.17 = (f32[128]{0:T(128)S(1)}, f32[128]{0:T(128)}, u32[]{:S(2)}) copy-start(f32[128]{0:T(128)} %param.21) | copy-start | bytes 1540
  47.0 17.2 %all-to-all-start.1 = ((bf16[4,8,80,256]{3,2,1,0:T(8,128)(2,1)}), bf16[4,8,80,256]{3,2,1,0:T(8,128)(2,1)S(1)}, u32[]{:S(2)}, u32[]{:S(2)}) async-start(bf16[4,8,80,256]{3,2,1,0:T(8,128)(2,1)} %broadcast_in_dim.70), calls=%async_computation.1 | async-start | bytes 2621440 | tf_op jit(solution)/shard_map/all_to_all | solution.py:329
  50.7 21.6 %copy-start.2 = (bf16[384,1280]{1,0:T(8,128)(2,1)S(1)}, bf16[384,1280]{1,0:T(8,128)(2,1)}, u32[]{:S(2)}) copy-start(bf16[384,1280]{1,0:T(8,128)(2,1)} %tokens.1) | copy-start | bytes 2949124
  50.7 21.6 %copy-start.9 = (f32[5120]{0:T(1024)S(1)}, f32[5120]{0:T(1024)}, u32[]{:S(2)}) copy-start(f32[5120]{0:T(1024)} %param.16) | copy-start | bytes 61444
  50.8 9.9 %collective-permute-start.2 = (bf16[192,1280]{1,0:T(8,128)(2,1)S(1)}, bf16[192,1280]{1,0:T(8,128)(2,1)S(1)}, u32[]{:S(2)}, u32[]{:S(2)}) collective-permute-start(bf16[192,1280]{1,0:T(8,128)(2,1)S(1)} %slice.54), channel_id=1, source_target_pairs={{0,1},{1,2},{2,3},{3,0},{4,5},{5,6},{6,7},{7,4},{8,9},{9,10},{10,1... | collective-permute-start | bytes 1474568 | tf_op jit(solution)/shard_map/ppermute | solution.py:35
  52.5 9.2 %collective-permute-start.3 = (bf16[192,1280]{1,0:T(8,128)(2,1)S(1)}, bf16[192,1280]{1,0:T(8,128)(2,1)S(1)}, u32[]{:S(2)}, u32[]{:S(2)}) collective-permute-start(bf16[192,1280]{1,0:T(8,128)(2,1)S(1)} %slice.55), channel_id=1, source_target_pairs={{0,3},{1,0},{2,1},{3,2},{4,7},{5,4},{6,5},{7,6},{8,11},{9,8},{10,9... | collective-permute-start | bytes 1474568 | tf_op jit(solution)/shard_map/ppermute | solution.py:35
  64.2 8.1 %collective-permute-start.4 = (bf16[4,8,80,256]{3,2,1,0:T(8,128)(2,1)S(1)}, bf16[4,8,80,256]{3,2,1,0:T(8,128)(2,1)}, u32[]{:S(2)}, u32[]{:S(2)}) collective-permute-start(bf16[4,8,80,256]{3,2,1,0:T(8,128)(2,1)S(1)} %all-to-all-done.1.w_own), channel_id=1, source_target_pairs={{0,4},{4,0},{8,12},{12,8},{16,20},{20,16},{24,28},{28,24},{32,36},... | collective-permute-start | bytes 3932168 | tf_op jit(solution)/shard_map/ppermute | solution.py:337
  74.5 10.9 %copy-start.10 = (s32[384]{0:T(512)S(1)}, s32[384]{0:T(512)}, u32[]{:S(2)}) copy-start(s32[384]{0:T(512)} %param.29) | copy-start | bytes 4612
  74.5 10.9 %copy-start.11 = (s32[384]{0:T(512)S(1)}, s32[384]{0:T(512)}, u32[]{:S(2)}) copy-start(s32[384]{0:T(512)} %param.28) | copy-start | bytes 4612
  83.2 37.5 %copy-start.4 = (f32[384,128]{1,0:T(8,128)S(1)}, f32[384,128]{1,0:T(8,128)}, u32[]{:S(2)}) copy-start(f32[384,128]{1,0:T(8,128)} %copy-done.3) | copy-start | bytes 589828
  83.2 3.0 %collective-permute-start.8 = (bf16[384,256]{1,0:T(8,128)(2,1)}, bf16[384,256]{1,0:T(8,128)(2,1)S(1)}, u32[]{:S(2)}, u32[]{:S(2)}) collective-permute-start(bf16[384,256]{1,0:T(8,128)(2,1)} %get-tuple-element.23.kv), channel_id=1, source_target_pairs={{0,128},{1,129},{2,130},{3,131}} | collective-permute-start | bytes 589832 | tf_op jit(solution)/shard_map/ppermute | solution.py:352
  84.0 2.2 %collective-permute-start.6 = (bf16[384,256]{1,0:T(8,128)(2,1)}, bf16[384,256]{1,0:T(8,128)(2,1)S(1)}, u32[]{:S(2)}, u32[]{:S(2)}) collective-permute-start(bf16[384,256]{1,0:T(8,128)(2,1)} %get-tuple-element.23.kv), channel_id=1, source_target_pairs={{0,64},{1,65},{2,66},{3,67}} | collective-permute-start | bytes 589832 | tf_op jit(solution)/shard_map/ppermute | solution.py:352
  84.7 1.6 collective-permute-start.7
  86.4 2.3 %collective-permute-start.11 = (bf16[384,256]{1,0:T(8,128)(2,1)S(1)}, bf16[384,256]{1,0:T(8,128)(2,1)S(1)}, u32[]{:S(2)}, u32[]{:S(2)}) collective-permute-start(bf16[384,256]{1,0:T(8,128)(2,1)S(1)} %add_select_fusion.1), channel_id=1, source_target_pairs={{0,32},{64,96},{192,224},{128,160},{1,33},{65,97},{193,225},{129,1... | collective-permute-start | bytes 589832 | tf_op jit(solution)/shard_map/ppermute | solution.py:352
  87.0 1.6 collective-permute-start.9
  87.7 0.9 collective-permute-start.10
  88.7 0.8 collective-permute-start.12
  89.5 31.2 %collective-permute-start.13 = (bf16[384,256]{1,0:T(8,128)(2,1)S(1)}, bf16[384,256]{1,0:T(8,128)(2,1)S(1)}, u32[]{:S(2)}, u32[]{:S(2)}) collective-permute-start(bf16[384,256]{1,0:T(8,128)(2,1)S(1)} %broadcast_select_fusion), channel_id=1, source_target_pairs={{0,4},{64,68},{192,196},{128,132},{16,20},{80,84},{208,212},{144,1... | collective-permute-start | bytes 589832 | tf_op jit(solution)/shard_map/ppermute | solution.py:352
  129.7 21.5 %copy-start.12 = (f32[1280]{0:T(1024)S(1)}, f32[1280]{0:T(1024)}, u32[]{:S(2)}) copy-start(f32[1280]{0:T(1024)} %param.24) | copy-start | bytes 15364
  129.7 21.5 %copy-start.13 = (f32[1280]{0:T(1024)S(1)}, f32[1280]{0:T(1024)}, u32[]{:S(2)}) copy-start(f32[1280]{0:T(1024)} %param.25) | copy-start | bytes 15364
  133.0 14.0 %collective-permute-start.14 = (bf16[384,640]{1,0:T(8,128)(2,1)S(1)}, bf16[384,640]{1,0:T(8,128)(2,1)S(1)}, u32[]{:S(2)}, u32[]{:S(2)}) collective-permute-start(bf16[384,640]{1,0:T(8,128)(2,1)S(1)} %attend.1.att), channel_id=1, source_target_pairs={{0,1},{1,2},{2,3},{3,0},{4,5},{5,6},{6,7},{7,4},{8,9},{9,10},{10,1... | collective-permute-start | bytes 1474568 | tf_op jit(solution)/shard_map/ppermute | solution.py:35
  134.3 12.8 %collective-permute-start.15 = (bf16[384,640]{1,0:T(8,128)(2,1)S(1)}, bf16[384,640]{1,0:T(8,128)(2,1)S(1)}, u32[]{:S(2)}, u32[]{:S(2)}) collective-permute-start(bf16[384,640]{1,0:T(8,128)(2,1)S(1)} %attend.1.att), channel_id=1, source_target_pairs={{0,3},{1,0},{2,1},{3,2},{4,7},{5,4},{6,5},{7,6},{8,11},{9,8},{10,9... | collective-permute-start | bytes 1474568 | tf_op jit(solution)/shard_map/ppermute | solution.py:35
  147.0 12.0 %collective-permute-start.16 = (bf16[192,640]{1,0:T(8,128)(2,1)S(1)}, bf16[192,640]{1,0:T(8,128)(2,1)S(1)}, u32[]{:S(2)}, u32[]{:S(2)}) collective-permute-start(bf16[192,640]{1,0:T(8,128)(2,1)S(1)} %slice.70), channel_id=1, source_target_pairs={{0,1},{1,2},{2,3},{3,0},{4,5},{5,6},{6,7},{7,4},{8,9},{9,10},{10,1... | collective-permute-start | bytes 737288 | tf_op jit(solution)/shard_map/ppermute | solution.py:35
  147.2 11.8 %collective-permute-start.17 = (bf16[192,640]{1,0:T(8,128)(2,1)S(1)}, bf16[192,640]{1,0:T(8,128)(2,1)S(1)}, u32[]{:S(2)}, u32[]{:S(2)}) collective-permute-start(bf16[192,640]{1,0:T(8,128)(2,1)S(1)} %slice.71), channel_id=1, source_target_pairs={{0,3},{1,0},{2,1},{3,2},{4,7},{5,4},{6,5},{7,6},{8,11},{9,8},{10,9... | collective-permute-start | bytes 737288 | tf_op jit(solution)/shard_map/ppermute | solution.py:35
  164.0 7.6 %all-to-all-start.2 = ((f32[4,8,384]{2,1,0:T(8,128)}), f32[4,8,384]{2,1,0:T(8,128)S(1)}, u32[]{:S(2)}, u32[]{:S(2)}) async-start(f32[4,8,384]{2,1,0:T(8,128)} %broadcast_in_dim.75), calls=%async_computation.2 | async-start | bytes 98304 | tf_op jit(solution)/shard_map/all_to_all | solution.py:329
  173.0 19.1 %all-to-all-start.3 = ((f32[64,1,128]{2,1,0:T(1,128)}), f32[64,1,128]{2,1,0:T(1,128)S(1)}, u32[]{:S(2)}, u32[]{:S(2)}) async-start(f32[64,1,128]{2,1,0:T(1,128)} %bitcast.19), calls=%async_computation.3 | async-start | bytes 65536 | tf_op jit(solution)/shard_map/all_to_all | solution.py:451
  (8 other events, 25.9 us)
Sparse Core Ops, SparseCore 0:
  10.7 103.0 all-gather.1

commit v3 on v2

--- a/solution.py
+++ b/solution.py
@@ -35,22 +35,14 @@
     return lax.ppermute(block, "tp", [(i, (i + distance) % T) for i in range(T)])
 
 
-def ring_tp(block):
-    half = block.shape[0] // 2
-    below = shift_tp(block, 1)
-    above = shift_tp(block, -1)
-    first = shift_tp(below[:half], 1)
-    second = shift_tp(above[half:], -1)
-    return block, below, above, first, second
-
-
 def params(mib=40):
     return pltpu.CompilerParams(vmem_limit_bytes=mib * MIB)
 
 
 def interleave(core, own, other, joined):
-    joined[:, pl.ds(core, 1)] = own[...].reshape(own.shape[-3], 1, *own.shape[-2:])
-    joined[:, pl.ds(1 - core, 1)] = other[...].reshape(other.shape[-3], 1, *other.shape[-2:])
+    zs, _, rows, n = joined.shape
+    joined[:, pl.ds(core, 1)] = own[...].reshape(zs, 1, rows, n)
+    joined[:, pl.ds(1 - core, 1)] = other[...].reshape(zs, 1, rows, n)
     return joined[...].reshape(-1, joined.shape[-1])
 
 
@@ -58,39 +50,30 @@
     return u * cosine[...] + pltpu.roll(u, HALF, 1) * sine[...]
 
 
-def project_kv_kernel(
-    order, own, below, above, first, second, gain, w_own, w_other, bias, cosine, sine, normed_out, kv_out, scale, acc, joined
-):
+def norm_kernel(own, below, above, first, second, gain, normed_out):
+    def squares(ref):
+        x = ref[...].astype(F32)
+        return jnp.sum(x * x, axis=-1, keepdims=True)
+
+    half = first.shape[0]
+    far = jnp.concatenate([squares(first), squares(second)], axis=0)
+    mean = (squares(own) + squares(below) + squares(above) + far) / D
+    scale = lax.rsqrt(mean + EPS)
+    for at, ref in enumerate((own, below, above)):
+        normed_out[at] = (ref[...].astype(F32) * scale * gain[at]).astype(BF16)
+    normed_out[T - 1, :half] = (first[...].astype(F32) * scale[:half] * gain[T - 1]).astype(BF16)
+    normed_out[T - 1, half:] = (second[...].astype(F32) * scale[half:] * gain[T - 1]).astype(BF16)
+
+
+def project_kv_kernel(order, normed, w_own, w_other, bias, cosine, sine, kv_out, acc, joined):
     step = pl.program_id(0)
-    half = first.shape[0]
 
     @pl.when(step == 0)
     def _():
-        def squares(ref):
-            x = ref[...].astype(F32)
-            return jnp.sum(x * x, axis=-1, keepdims=True)
-
-        far = jnp.concatenate([squares(first), squares(second)], axis=0)
-        mean = (squares(own) + squares(below) + squares(above) + far) / D
-        scale[...] = lax.rsqrt(mean + EPS)
         acc[...] = jnp.zeros_like(acc)
 
-    def norm(x, rows):
-        normed_out[0, rows, :] = (x.astype(F32) * scale[rows, :] * gain[0]).astype(BF16)
-
-    for at, ref in enumerate((own, below, above)):
-
-        @pl.when(step == at)
-        def _(ref=ref):
-            norm(ref[...], pl.ds(0, ROWS))
-
-    @pl.when(step == T - 1)
-    def _():
-        norm(first[...], pl.ds(0, half))
-        norm(second[...], pl.ds(half, half))
-
     w = interleave(order[T], w_own, w_other, joined)
-    acc[...] += jnp.dot(normed_out[0], w, preferred_element_type=F32)
+    acc[...] += jnp.dot(normed[0], w, preferred_element_type=F32)
 
     @pl.when(step == T - 1)
     def _():
@@ -102,41 +85,31 @@
     return pl.BlockSpec(shape, lambda k, order: (0,) * len(shape))
 
 
-def shard_rows(n):
-    return pl.BlockSpec((1, Z, SHARD, n), lambda k, order: (order[k], 0, 0, 0))
-
-
-def project_kv(order, pieces, gain, w_own, w_other, bias, cosine, sine):
+def project_kv(order, normed, w_own, w_other, bias, cosine, sine):
+    rows = Z * SHARD
+    shards = pl.BlockSpec((1, rows, 2 * HD), lambda k, order: (order[k], 0, 0))
     grid = pltpu.PrefetchScalarGridSpec(
         num_scalar_prefetch=1,
         grid=(T,),
-        in_specs=[whole(*piece.shape) for piece in pieces]
-        + [
-            pl.BlockSpec((1, 1, PIECE), lambda k, order: (order[k], 0, 0)),
-            shard_rows(2 * HD),
-            shard_rows(2 * HD),
+        in_specs=[
+            pl.BlockSpec((1, ROWS, PIECE), lambda k, order: (k, 0, 0)),
+            shards,
+            shards,
             whole(1, 2 * HD),
             whole(ROWS, HD),
             whole(ROWS, HD),
         ],
-        out_specs=[pl.BlockSpec((1, ROWS, PIECE), lambda k, order: (k, 0, 0)), whole(ROWS, 2 * HD)],
-        scratch_shapes=[
-            pltpu.VMEM((ROWS, 1), F32),
-            pltpu.VMEM((ROWS, 2 * HD), F32),
-            pltpu.VMEM((Z, C, SHARD, 2 * HD), BF16),
-        ],
+        out_specs=whole(ROWS, 2 * HD),
+        scratch_shapes=[pltpu.VMEM((ROWS, 2 * HD), F32), pltpu.VMEM((Z, C, SHARD, 2 * HD), BF16)],
     )
     return pl.pallas_call(
         project_kv_kernel,
         grid_spec=grid,
-        out_shape=[
-            jax.ShapeDtypeStruct((T, ROWS, PIECE), BF16),
-            jax.ShapeDtypeStruct((ROWS, 2 * HD), BF16),
-        ],
+        out_shape=jax.ShapeDtypeStruct((ROWS, 2 * HD), BF16),
         compiler_params=params(),
-        cost_estimate=pl.CostEstimate(flops=4 * ROWS * D * HD, bytes_accessed=2 * D * (2 * HD + 2 * ROWS), transcendentals=0),
+        cost_estimate=pl.CostEstimate(flops=4 * ROWS * D * HD, bytes_accessed=2 * D * (2 * HD + ROWS), transcendentals=0),
         name="project_kv",
-    )(order, *pieces, gain, w_own, w_other, bias, cosine, sine)
+    )(order, normed, w_own, w_other, bias, cosine, sine)
 
 
 def project_q_kernel(order, normed, w, bias, cosine, sine, q_out, acc):
@@ -229,16 +202,15 @@
 
 def out_last_kernel(order, total, first, second, w_far, gain, head, resid_out, stats_out):
     half = first.shape[0]
-    lane = lax.broadcasted_iota(jnp.int32, (half, HD), 1)
+    lane = lax.broadcasted_iota(jnp.int32, (ROWS, HD), 1)
     w = w_far[...]
-    for at, ref in enumerate((first, second)):
-        rows = pl.ds(at * half, half)
-        resid = total[rows, :] + times(ref[...], w)
-        resid_out[rows, :] = resid.astype(BF16)
-        squares = jnp.sum(resid * resid, axis=-1, keepdims=True)
-        products = jnp.sum(resid * gain[...] * head[...], axis=-1, keepdims=True)
-        both = jnp.where(lane == 0, squares, products)
-        stats_out[at] = both.T[:8, :]
+    resid = total[...] + times(jnp.concatenate([first[...], second[...]], axis=0), w)
+    resid_out[...] = resid.astype(BF16)
+    squares = jnp.sum(resid * resid, axis=-1, keepdims=True)
+    products = jnp.sum(resid * gain[...] * head[...], axis=-1, keepdims=True)
+    both = jnp.where(lane == 0, squares, products).T[:8, :]
+    for at in range(T):
+        stats_out[at] = both
 
 
 def out_call(kernel, order, operands, w, picks, extra, out_shape, name):
@@ -310,6 +282,11 @@
         out[:, span] = local[:, span] + edge[:, span] * value + tail[:, span] * carry
 
 
+def norm(*operands):
+    shape = jax.ShapeDtypeStruct((T, ROWS, PIECE), BF16)
+    return small_call(norm_kernel, operands, (), shape, "norm")
+
+
 def small_call(kernel, operands, scalars, out_shape, name):
     vmem = pl.BlockSpec(memory_space=pltpu.VMEM)
     smem = pl.BlockSpec(memory_space=pltpu.SMEM)
@@ -337,11 +314,14 @@
     return lax.ppermute(block, "ctx", [(i, i ^ 1) for i in range(X * Z * C)])
 
 
-def broadcast_anchor(block):
+TREE = (((1, 0, 0), (3, 0, 0), (2, 0, 0)), ((0, 2, 0), (0, 6, 0), (0, 4, 0)), ((0, 1, 0),), ((0, 0, 1),))
+
+
+def broadcast_anchor(block, query):
     here = lax.axis_index("ctx")
     at = (here // (Z * C), here // C % Z, here % C)
     holders = [(0, 0, 0)]
-    for stage in (((1, 0, 0), (3, 0, 0), (2, 0, 0)), ((0, 2, 0), (0, 6, 0), (0, 4, 0)), ((0, 1, 0),), ((0, 0, 1),)):
+    for stage in TREE:
         holding = jnp.ones((), jnp.bool_)
         for axis in range(3):
             seen = sorted({h[axis] for h in holders})
@@ -352,9 +332,11 @@
             got = lax.ppermute(block, "ctx", [(place(*a), place(*b)) for a, b in zip(holders, targets)])
             sent = got if sent is None else sent + got
             fresh += targets
+        if stage is TREE[-2]:
+            sent, query = lax.optimization_barrier((sent, query))
         block = jnp.where(holding, block, sent)
         holders = holders + fresh
-    return block
+    return block, query
 
 
 def on_device(
@@ -389,10 +371,11 @@
     kv_part = gather_by_all_to_all(jnp.concatenate([w_key, w_value], axis=1), "ctx", Z_GROUPS, Z)
     below, above, kv_part = lax.optimization_barrier((below, above, kv_part))
     first, second = shift_tp(below[:half], 1), shift_tp(above[half:], -1)
-    kv_own = gather_by_all_to_all(kv_part, "ctx", X_GROUPS, X)
+    kv_own = gather_by_all_to_all(kv_part.reshape(Z * SHARD, 2 * HD), "ctx", X_GROUPS, X)
     first, second, kv_own = lax.optimization_barrier((first, second, kv_own))
-    pieces = (tokens, below, above, first, second)
     kv_other = other_core(kv_own)
+    gain = lax.dynamic_slice_in_dim(jnp.tile(input_gain.reshape(T, 1, PIECE), (2, 1, 1)), mine, T, 0)
+    normed = norm(tokens, below, above, first, second, gain[jnp.array([0, 3, 1, 2])])
 
     positions = (index * ROWS + jnp.arange(ROWS)).astype(F32)
     steps = jnp.arange(HALF).astype(F32)
@@ -402,14 +385,16 @@
     cosine = jnp.concatenate([cosine, cosine], axis=1)
     sine = jnp.concatenate([-sine, sine], axis=1)
     kv_bias = jnp.concatenate([key_bias, value_bias])[None, :]
-    normed, kv = project_kv(order, pieces, input_gain.reshape(T, 1, PIECE), kv_own, kv_other, kv_bias, cosine, sine)
-    anchor = broadcast_anchor(kv)
+    kv = project_kv(order, normed, kv_own, kv_other, kv_bias, cosine, sine)
     query = project_q(order, normed, weights, query_bias[None, :], cosine, sine)
+    anchor, query = broadcast_anchor(kv, query)
     att = attend(index.astype(jnp.int32)[None], query, kv, anchor)
 
-    own, below, above, first, second = ring_tp(att)
+    below, above = shift_tp(att, 1), shift_tp(att, -1)
     wide = jax.ShapeDtypeStruct((ROWS, PIECE), F32)
-    total = out_call(out_own_kernel, order, [tokens, own], weights, (0,), [], wide, "out_own")
+    total = out_call(out_own_kernel, order, [tokens, att], weights, (0,), [], wide, "out_own")
+    total, below, above = lax.optimization_barrier((total, below, above))
+    first, second = shift_tp(below[:half], 1), shift_tp(above[half:], -1)
     total = out_call(out_next_kernel, order, [total, below, above], weights, (1, 2), [], wide, "out_next")
     residual_stream, stats = out_call(
         out_last_kernel,
@@ -418,10 +403,10 @@
         weights,
         (3,),
         [final_gain[None, :], critic_head[None, :]],
-        [jax.ShapeDtypeStruct((ROWS, PIECE), BF16), jax.ShapeDtypeStruct((2, 8, ROWS // 2), F32)],
+        [jax.ShapeDtypeStruct((ROWS, PIECE), BF16), jax.ShapeDtypeStruct((T, 8, ROWS), F32)],
         "out_last",
     )
-    stats = gather_by_all_to_all(jnp.concatenate([stats[0], stats[1]], axis=1), "tp", None, T)
+    stats = lax.all_to_all(stats, "tp", 0, 0)
 
     ends = jnp.maximum(turn_ends, episode_done)
     discount = jnp.where(ends > 0, GAMMA, 1.0).astype(F32) * (1 - episode_done).astype(F32)

time: 201 us -> 194 us (0.965)
  waiting for transfers between devices: 60.7 us -> 55.9 us
    all_gather x1, waiting for transfers between devices: 0.02 us -> 28.4 us  [on_device(): lax.all_gather(jnp.concatenate([out_block, w_query], axis=1), 'ctx', axis...]
    ppermute x8, waiting for transfers between devices: 29.6 us -> 1.8 us  [broadcast_anchor(): lax.ppermute(block, 'ctx', [(place(*a), place(*b)) for a, b in zip(holder...]
    ppermute x8, waiting for transfers between devices: 16.1 us -> 12.4 us  [shift_tp(): lax.ppermute(block, 'tp', [(i, (i + distance) % T) for i in range(T)])]
    all_to_all x0 -> x1, starting transfers between devices: none -> 3.27 us  [on_device(): stats = lax.all_to_all(stats, 'tp', 0, 0)]
    all_to_all x2 -> x1, starting transfers between devices: 6.95 us -> 3.68 us  [gather_by_all_to_all(): return lax.all_to_all(everywhere, axis, 0, 0, axis_index_groups=groups)]
    pallas_call x2 -> x3, Pallas kernels: 1.49 us -> 4.5 us  [small_call(): pl.pallas_call(kernel, in_specs=[smem if at in scalars else vmem for at i...]
    all_to_all x2 -> x1, waiting for transfers between devices: 4.62 us -> 1.8 us  [gather_by_all_to_all(): return lax.all_to_all(everywhere, axis, 0, 0, axis_index_groups=groups)]
    all_to_all x0 -> x1, waiting for transfers between devices: none -> 2.8 us  [on_device(): stats = lax.all_to_all(stats, 'tp', 0, 0)]
  transfers between devices with their start and end apart: 22 -> 22, of which waited for: 9 -> 9; matrix products, arithmetic and copies ran while one was open for 5% -> 6% of each run, Pallas kernels for 7% -> 11%
where the time goes in v3:
time: 194 us; the launch traced here: 193 us
  waiting for transfers between devices  55.9 us (29%)
  starting transfers between devices  53.2 us (27%)
  Pallas kernels  29.1 us (15%)
  blocking collectives  20.4 us (11%)
  between operations  15.4 us (8%)
  local copies, waits for them, and re-layouts  11.2 us (6%)
  other arithmetic  7.94 us (4%)
    all_gather x1, waiting for transfers between devices, on_device(): lax.all_gather(jnp.concatenate([out_block, w_query], axis=1), 'ctx', axis...  28.4 us
    ppermute x8, starting transfers between devices, shift_tp(): lax.ppermute(block, 'tp', [(i, (i + distance) % T) for i in range(T)])  22.5 us
    all_to_all x1, blocking collectives, gather_by_all_to_all(): return lax.all_to_all(everywhere, axis, 0, 0, axis_index_groups=groups)  20.4 us
    ppermute x8, waiting for transfers between devices, shift_tp(): lax.ppermute(block, 'tp', [(i, (i + distance) % T) for i in range(T)])  12.4 us
    pallas_call x3, Pallas kernels, out_call(): pl.pallas_call(kernel, grid_spec=grid, out_shape=out_shape, compiler_para...  11.1 us
    all_to_all x1, starting transfers between devices, on_device(): records = lax.all_to_all(records, 'ctx', 0, 0, tiled=True)  10.6 us
    all_to_all x1, waiting for transfers between devices, on_device(): records = lax.all_to_all(records, 'ctx', 0, 0, tiled=True)  8.69 us
    pallas_call x1, Pallas kernels, project_q(): pl.pallas_call(project_q_kernel, grid_spec=grid, out_shape=jax.ShapeDtype...  6.79 us
  transfers between devices with their start and end apart: 22, of which 9 were waited for; matrix products, arithmetic and copies ran while one was open for 6% of the time, Pallas kernels for 11%

profile of v3, /device:TPU:1, one launch (start us, length us, event | category | flops | bytes accessed | tf_op | source)
XLA Modules:
  0.0 193.1 jit_solution(12012589116331917430)
XLA Ops:
  7.2 1.6 collective-permute-start.12
  8.8 1.6 pad_maximum_fusion
  10.4 7.2 %collective-permute-start = (bf16[384,1280]{1,0:T(8,128)(2,1)}, bf16[384,1280]{1,0:T(8,128)(2,1)S(1)}, u32[]{:S(2)}, u32[]{:S(2)}) collective-permute-start(bf16[384,1280]{1,0:T(8,128)(2,1)} %tokens.1), channel_id=1, source_target_pairs={{0,1},{1,2},{2,3},{3,0},{4,5},{5,6},{6,7},{7,4},{8,9},{9,10},{10,1... | collective-permute-start | bytes 2949128 | tf_op jit(solution)/shard_map/ppermute | solution.py:35
  17.5 6.9 %collective-permute-start.1 = (bf16[384,1280]{1,0:T(8,128)(2,1)}, bf16[384,1280]{1,0:T(8,128)(2,1)}, u32[]{:S(2)}, u32[]{:S(2)}) collective-permute-start(bf16[384,1280]{1,0:T(8,128)(2,1)} %tokens.1), channel_id=1, source_target_pairs={{0,3},{1,0},{2,1},{3,2},{4,7},{5,4},{6,5},{7,6},{8,11},{9,8},{10,9... | collective-permute-start | bytes 2949128 | tf_op jit(solution)/shard_map/ppermute | solution.py:35
  25.3 20.4 %all_to_all.26 = bf16[8,80,256]{2,1,0:T(8,128)(2,1)S(1)} all-to-all(bf16[8,80,256]{2,1,0:T(8,128)(2,1)S(1)} %broadcast_in_dim.67), channel_id=1, replica_groups={{0,8,16,24,32,40,48,56},{4,12,20,28,36,44,52,60},{64,72,80,88,96,104,11..., dimensions={0} | all-to-all | bytes 655360 | tf_op jit(solution)/shard_map/all_to_all | solution.py:306
  45.8 1.1 broadcast_in_dim.69
  47.0 3.7 %all-to-all-start.1 = ((bf16[4,640,256]{2,1,0:T(8,128)(2,1)}), bf16[4,640,256]{2,1,0:T(8,128)(2,1)S(1)}, u32[]{:S(2)}, u32[]{:S(2)}) async-start(bf16[4,640,256]{2,1,0:T(8,128)(2,1)} %broadcast_in_dim.69), calls=%async_computation.1 | async-start | bytes 2621440 | tf_op jit(solution)/shard_map/all_to_all | solution.py:306
  52.5 2.2 %collective-permute-start.3 = (bf16[192,1280]{1,0:T(8,128)(2,1)S(1)}, bf16[192,1280]{1,0:T(8,128)(2,1)S(1)}, u32[]{:S(2)}, u32[]{:S(2)}) collective-permute-start(bf16[192,1280]{1,0:T(8,128)(2,1)S(1)} %slice.49), channel_id=1, source_target_pairs={{0,3},{1,0},{2,1},{3,2},{4,7},{5,4},{6,5},{7,6},{8,11},{9,8},{10,9... | collective-permute-start | bytes 1474568 | tf_op jit(solution)/shard_map/ppermute | solution.py:35
  54.7 6.0 %collective-permute-done.2.first = bf16[192,1280]{1,0:T(8,128)(2,1)S(1)} collective-permute-done((bf16[192,1280]{1,0:T(8,128)(2,1)S(1)}, bf16[192,1280]{1,0:T(8,128)(2,1)S(1)}, u32[]{:S(2)}, u32[]{:S(2)}) %collective-permute-start.2) | collective-permute-done | bytes 491552 | tf_op jit(solution)/shard_map/ppermute | solution.py:35
  62.4 1.8 all-to-all-done.1.w_own
  64.2 5.3 %collective-permute-start.4 = (bf16[4,640,256]{2,1,0:T(8,128)(2,1)S(1)}, bf16[4,640,256]{2,1,0:T(8,128)(2,1)}, u32[]{:S(2)}, u32[]{:S(2)}) collective-permute-start(bf16[4,640,256]{2,1,0:T(8,128)(2,1)S(1)} %all-to-all-done.1.w_own), channel_id=1, source_target_pairs={{0,4},{4,0},{8,12},{12,8},{16,20},{20,16},{24,28},{28,24},{32,36},... | collective-permute-start | bytes 3932168 | tf_op jit(solution)/shard_map/ppermute | solution.py:314
  72.3 1.2 copy-done.6
  74.5 3.0 %norm.1.normed = bf16[4,384,1280]{2,1,0:T(8,128)(2,1)S(1)} custom-call(bf16[384,1280]{1,0:T(8,128)(2,1)S(1)} %copy-done.2, bf16[384,1280]{1,0:T(8,128)(2,1)S(1)} %collective-permute-done.below, bf16[384,1280]{1,0:T(8,128)(2,1)} %collective-permute-done.1.above, bf16[192,1280]{1,0:T(8,128)(2,1)S(1)} %copy-done.6, bf16[192,1280]{1,0:T(8,128)(2,1)S(1)} %copy-done.8, ...), custom_call_target="tpu_custom_call" | custom-call | flops 294912 | bytes 1048576 | tf_op jit(solution)/shard_map/norm/pallas_call | solution.py:293
  77.5 4.4 %project_kv.1.kv = bf16[384,256]{1,0:T(8,128)(2,1)S(1)} custom-call(s32[5]{0:T(128)S(1)} %stack.23.order, bf16[4,384,1280]{2,1,0:T(8,128)(2,1)S(1)} %norm.1.normed, bf16[4,640,256]{2,1,0:T(8,128)(2,1)S(1)} %all-to-all-done.1.w_own, bf16[4,640,256]{2,1,0:T(8,128)(2,1)} %collective-permute-done.4.w_other, f32[1,256]{1,0:T(1,128)S(1)} %bitcast.26, ...), custom_call_target="tpu_custom_call" | custom-call | flops 1006632960 | bytes 6553600 | tf_op jit(solution)/shard_map/project_kv/pallas_call | solution.py:105
  87.3 28.4 %all-gather.2.cloned.1.call-done.w.w_below.w_above.w_far = bf16[5120,1280]{1,0:T(8,128)(2,1)} async-done(((bf16[80,1280]{1,0:T(8,128)(2,1)}), bf16[5120,1280]{1,0:T(8,128)(2,1)}) %all-gather.2.cloned.1.call-update) | async-done | bytes 13107216 | tf_op jit(solution)/shard_map/all_gather | solution.py:367
  115.7 2.1 %copy-done.1 = bf16[4,384,1280]{2,1,0:T(8,128)(2,1)S(1)} copy-done((bf16[4,384,1280]{2,1,0:T(8,128)(2,1)S(1)}, bf16[4,384,1280]{2,1,0:T(8,128)(2,1)}, u32[]{:S(2)}) %copy-start.1) | copy-done | bytes 3932184
  117.8 6.8 %project_q.1.q = bf16[384,640]{1,0:T(8,128)(2,1)S(1)} custom-call(s32[5]{0:T(128)S(1)} %stack.23.order, bf16[4,384,1280]{2,1,0:T(8,128)(2,1)S(1)} %copy-done.1, bf16[5120,1280]{1,0:T(8,128)(2,1)} %all-gather.2.cloned.1.call-done.w.w_below.w_above.w_far, f32[1,640]{1,0:T(1,128)S(1)} %broadcast_in_dim.72.bias, f32[384,128]{1,0:T(8,128)S(1)} %get-tuple-element.40.cosine, ...), custom_call_target="tpu_custom_call" | custom-call | flops 2516582400 | bytes 10485760 | tf_op jit(solution)/shard_map/project_q/pallas_call | solution.py:145
  124.6 1.5 collective-permute-start.13
  126.2 1.8 collective-permute-done.13
  128.0 2.4 %attend.1.att = bf16[384,640]{1,0:T(8,128)(2,1)S(1)} custom-call(s32[1]{0:T(128)} %bitcast.5.index, bf16[384,640]{1,0:T(8,128)(2,1)S(1)} %project_q.1.q, bf16[384,256]{1,0:T(8,128)(2,1)S(1)} %project_kv.1.kv, bf16[384,256]{1,0:T(8,128)(2,1)S(1)} %broadcast_select_fusion.1.anchor), custom_call_target="tpu_custom_call" | custom-call | flops 754974720 | bytes 983040 | tf_op jit(solution)/shard_map/attend/pallas_call | solution.py:176
  131.4 1.7 collective-permute-start.15
  135.3 2.9 %out_own.1.total = f32[384,1280]{1,0:T(8,128)S(1)} custom-call(s32[5]{0:T(128)S(1)} %stack.23.order, bf16[384,1280]{1,0:T(8,128)(2,1)S(1)} %copy-done.2, bf16[384,640]{1,0:T(8,128)(2,1)S(1)} %attend.1.att, bf16[5120,1280]{1,0:T(8,128)(2,1)} %all-gather.2.cloned.1.call-done.w.w_below.w_above.w_far), custom_call_target="tpu_custom_call" | custom-call | flops 629145600 | bytes 6291456 | tf_op jit(solution)/shard_map/out_own/pallas_call | solution.py:224
  138.2 6.1 %collective-permute-done.14.below = bf16[384,640]{1,0:T(8,128)(2,1)S(1)} collective-permute-done((bf16[384,640]{1,0:T(8,128)(2,1)S(1)}, bf16[384,640]{1,0:T(8,128)(2,1)S(1)}, u32[]{:S(2)}, u32[]{:S(2)}) %collective-permute-start.14) | collective-permute-done | bytes 491552 | tf_op jit(solution)/shard_map/ppermute | solution.py:35
  145.4 1.9 collective-permute-start.17
  147.2 1.3 power_select_fusion.1
  148.5 4.2 %out_next.1.total = f32[384,1280]{1,0:T(8,128)S(1)} custom-call(s32[5]{0:T(128)S(1)} %stack.23.order, f32[384,1280]{1,0:T(8,128)S(1)} %out_own.1.total, bf16[384,640]{1,0:T(8,128)(2,1)S(1)} %collective-permute-done.14.below, bf16[384,640]{1,0:T(8,128)(2,1)S(1)} %collective-permute-done.15.above, ...), custom_call_target="tpu_custom_call" | custom-call | flops 1258291200 | bytes 6291456 | tf_op jit(solution)/shard_map/out_next/pallas_call | solution.py:224
  152.8 3.9 %out_last.1 = (bf16[384,1280]{1,0:T(8,128)(2,1)}, f32[4,8,384]{2,1,0:T(8,128)}) custom-call(s32[5]{0:T(128)S(1)} %stack.23.order, f32[384,1280]{1,0:T(8,128)S(1)} %out_next.1.total, bf16[192,640]{1,0:T(8,128)(2,1)S(1)} %collective-permute-done.16.first, bf16[192,640]{1,0:T(8,128)(2,1)S(1)} %collective-permute-done.17.second, ...), custom_call_target="tpu_custom_call" | custom-call | flops 629145600 | bytes 6291456 | tf_op jit(solution)/shard_map/out_last/pallas_call | solution.py:224
  156.7 3.3 %all-to-all-start.2 = ((f32[4,8,384]{2,1,0:T(8,128)}), f32[4,8,384]{2,1,0:T(8,128)S(1)}, u32[]{:S(2)}, u32[]{:S(2)}) async-start(f32[4,8,384]{2,1,0:T(8,128)} %get-tuple-element.31), calls=%async_computation.2 | async-start | bytes 98304 | tf_op jit(solution)/shard_map/all_to_all | solution.py:409
  161.5 2.8 %all-to-all-done.2.stats = f32[4,8,384]{2,1,0:T(8,128)S(1)} async-done(((f32[4,8,384]{2,1,0:T(8,128)}), f32[4,8,384]{2,1,0:T(8,128)S(1)}, u32[]{:S(2)}, u32[]{:S(2)}) %all-to-all-start.2) | async-done | bytes 49184 | tf_op jit(solution)/shard_map/all_to_all | solution.py:409
  164.3 1.3 values.1
  165.7 10.6 %all-to-all-start.3 = ((f32[64,1,128]{2,1,0:T(1,128)}), f32[64,1,128]{2,1,0:T(1,128)S(1)}, u32[]{:S(2)}, u32[]{:S(2)}) async-start(f32[64,1,128]{2,1,0:T(1,128)} %bitcast.17), calls=%async_computation.3 | async-start | bytes 65536 | tf_op jit(solution)/shard_map/all_to_all | solution.py:436
  176.8 8.7 %all-to-all-done.3 = f32[64,1,128]{2,1,0:T(1,128)S(1)} async-done(((f32[64,1,128]{2,1,0:T(1,128)}), f32[64,1,128]{2,1,0:T(1,128)S(1)}, u32[]{:S(2)}, u32[]{:S(2)}) %all-to-all-start.3) | async-done | bytes 32800 | tf_op jit(solution)/shard_map/all_to_all | solution.py:436
  (114 shorter events, 19.8 us)
Async XLA Ops:
  7.2 108.5 %all-gather.2.cloned.1.call-start = ((), (), s32[]{:S(2)}) async-start(), calls=%async_computation.4 | async-start | bytes 13312000 | tf_op jit(solution)/shard_map/all_gather | solution.py:367
  7.2 1.6 collective-permute-start.12
  10.4 35.5 %collective-permute-start = (bf16[384,1280]{1,0:T(8,128)(2,1)}, bf16[384,1280]{1,0:T(8,128)(2,1)S(1)}, u32[]{:S(2)}, u32[]{:S(2)}) collective-permute-start(bf16[384,1280]{1,0:T(8,128)(2,1)} %tokens.1), channel_id=1, source_target_pairs={{0,1},{1,2},{2,3},{3,0},{4,5},{5,6},{6,7},{7,4},{8,9},{9,10},{10,1... | collective-permute-start | bytes 2949128 | tf_op jit(solution)/shard_map/ppermute | solution.py:35
  17.5 28.3 %collective-permute-start.1 = (bf16[384,1280]{1,0:T(8,128)(2,1)}, bf16[384,1280]{1,0:T(8,128)(2,1)}, u32[]{:S(2)}, u32[]{:S(2)}) collective-permute-start(bf16[384,1280]{1,0:T(8,128)(2,1)} %tokens.1), channel_id=1, source_target_pairs={{0,3},{1,0},{2,1},{3,2},{4,7},{5,4},{6,5},{7,6},{8,11},{9,8},{10,9... | collective-permute-start | bytes 2949128 | tf_op jit(solution)/shard_map/ppermute | solution.py:35
  47.0 22.5 %copy-start.9 = (f32[5120]{0:T(1024)S(1)}, f32[5120]{0:T(1024)}, u32[]{:S(2)}) copy-start(f32[5120]{0:T(1024)} %param.17) | copy-start | bytes 61444
  47.0 22.6 %copy-start.16 = (s32[4]{0:T(128)S(1)}, s32[4]{0:T(128)}, u32[]{:S(2)}) copy-start(s32[4]{0:T(128)} %constant.123) | copy-start | bytes 52
  47.0 17.2 %all-to-all-start.1 = ((bf16[4,640,256]{2,1,0:T(8,128)(2,1)}), bf16[4,640,256]{2,1,0:T(8,128)(2,1)S(1)}, u32[]{:S(2)}, u32[]{:S(2)}) async-start(bf16[4,640,256]{2,1,0:T(8,128)(2,1)} %broadcast_in_dim.69), calls=%async_computation.1 | async-start | bytes 2621440 | tf_op jit(solution)/shard_map/all_to_all | solution.py:306
  50.7 19.6 %copy-start.14 = (f32[640]{0:T(1024)S(1)}, f32[640]{0:T(1024)}, u32[]{:S(2)}) copy-start(f32[640]{0:T(1024)} %param.21) | copy-start | bytes 7684
  50.7 19.6 %copy-start.10 = (s32[384]{0:T(512)S(1)}, s32[384]{0:T(512)}, u32[]{:S(2)}) copy-start(s32[384]{0:T(512)} %param.30) | copy-start | bytes 4612
  50.7 19.6 %copy-start.11 = (s32[384]{0:T(512)S(1)}, s32[384]{0:T(512)}, u32[]{:S(2)}) copy-start(s32[384]{0:T(512)} %param.29) | copy-start | bytes 4612
  50.7 20.6 %copy-start.17 = (f32[128]{0:T(128)S(1)}, f32[128]{0:T(128)}, u32[]{:S(2)}) copy-start(f32[128]{0:T(128)} %param.23) | copy-start | bytes 1540
  50.7 20.6 %copy-start.18 = (f32[128]{0:T(128)S(1)}, f32[128]{0:T(128)}, u32[]{:S(2)}) copy-start(f32[128]{0:T(128)} %param.22) | copy-start | bytes 1540
  50.7 21.5 %copy-start.2 = (bf16[384,1280]{1,0:T(8,128)(2,1)S(1)}, bf16[384,1280]{1,0:T(8,128)(2,1)}, u32[]{:S(2)}) copy-start(bf16[384,1280]{1,0:T(8,128)(2,1)} %tokens.1) | copy-start | bytes 2949124
  50.8 9.9 %collective-permute-start.2 = (bf16[192,1280]{1,0:T(8,128)(2,1)S(1)}, bf16[192,1280]{1,0:T(8,128)(2,1)S(1)}, u32[]{:S(2)}, u32[]{:S(2)}) collective-permute-start(bf16[192,1280]{1,0:T(8,128)(2,1)S(1)} %slice.48), channel_id=1, source_target_pairs={{0,1},{1,2},{2,3},{3,0},{4,5},{5,6},{6,7},{7,4},{8,9},{9,10},{10,1... | collective-permute-start | bytes 1474568 | tf_op jit(solution)/shard_map/ppermute | solution.py:35
  52.5 9.2 %collective-permute-start.3 = (bf16[192,1280]{1,0:T(8,128)(2,1)S(1)}, bf16[192,1280]{1,0:T(8,128)(2,1)S(1)}, u32[]{:S(2)}, u32[]{:S(2)}) collective-permute-start(bf16[192,1280]{1,0:T(8,128)(2,1)S(1)} %slice.49), channel_id=1, source_target_pairs={{0,3},{1,0},{2,1},{3,2},{4,7},{5,4},{6,5},{7,6},{8,11},{9,8},{10,9... | collective-permute-start | bytes 1474568 | tf_op jit(solution)/shard_map/ppermute | solution.py:35
  64.2 13.3 %collective-permute-start.4 = (bf16[4,640,256]{2,1,0:T(8,128)(2,1)S(1)}, bf16[4,640,256]{2,1,0:T(8,128)(2,1)}, u32[]{:S(2)}, u32[]{:S(2)}) collective-permute-start(bf16[4,640,256]{2,1,0:T(8,128)(2,1)S(1)} %all-to-all-done.1.w_own), channel_id=1, source_target_pairs={{0,4},{4,0},{8,12},{12,8},{16,20},{20,16},{24,28},{28,24},{32,36},... | collective-permute-start | bytes 3932168 | tf_op jit(solution)/shard_map/ppermute | solution.py:314
  77.5 9.0 %copy-start.15 = (s32[384]{0:T(512)S(1)}, s32[384]{0:T(512)}, u32[]{:S(2)}) copy-start(s32[384]{0:T(512)} %param.28) | copy-start | bytes 4612
  82.0 33.7 %copy-start.4 = (f32[384,128]{1,0:T(8,128)S(1)}, f32[384,128]{1,0:T(8,128)}, u32[]{:S(2)}) copy-start(f32[384,128]{1,0:T(8,128)} %copy-done.3) | copy-start | bytes 589828
  82.0 2.4 %collective-permute-start.7 = (bf16[384,256]{1,0:T(8,128)(2,1)S(1)}, bf16[384,256]{1,0:T(8,128)(2,1)S(1)}, u32[]{:S(2)}, u32[]{:S(2)}) collective-permute-start(bf16[384,256]{1,0:T(8,128)(2,1)S(1)} %project_kv.1.kv), channel_id=1, source_target_pairs={{0,128},{1,129},{2,130},{3,131}} | collective-permute-start | bytes 589832 | tf_op jit(solution)/shard_map/ppermute | solution.py:332
  82.8 1.6 collective-permute-start.5
  83.5 0.9 collective-permute-start.6
  84.5 2.1 %collective-permute-start.10 = (bf16[384,256]{1,0:T(8,128)(2,1)S(1)}, bf16[384,256]{1,0:T(8,128)(2,1)S(1)}, u32[]{:S(2)}, u32[]{:S(2)}) collective-permute-start(bf16[384,256]{1,0:T(8,128)(2,1)S(1)} %add_select_fusion.1), channel_id=1, source_target_pairs={{0,32},{64,96},{192,224},{128,160},{1,33},{65,97},{193,225},{129,1... | collective-permute-start | bytes 589832 | tf_op jit(solution)/shard_map/ppermute | solution.py:332
  85.1 1.4 collective-permute-start.8
  85.8 0.7 collective-permute-start.9
  86.6 38.0 %collective-permute-start.11 = (bf16[384,256]{1,0:T(8,128)(2,1)S(1)}, bf16[384,256]{1,0:T(8,128)(2,1)S(1)}, u32[]{:S(2)}, u32[]{:S(2)}) collective-permute-start(bf16[384,256]{1,0:T(8,128)(2,1)S(1)} %add_select_fusion), channel_id=1, source_target_pairs={{0,8},{64,72},{192,200},{128,136},{16,24},{80,88},{208,216},{144,1... | collective-permute-start | bytes 589832 | tf_op jit(solution)/shard_map/ppermute | solution.py:332
  124.6 3.3 %collective-permute-start.13 = (bf16[384,256]{1,0:T(8,128)(2,1)S(1)}, bf16[384,256]{1,0:T(8,128)(2,1)S(1)}, u32[]{:S(2)}, u32[]{:S(2)}) collective-permute-start(bf16[384,256]{1,0:T(8,128)(2,1)S(1)} %broadcast_select_fusion), channel_id=1, source_target_pairs={{0,4},{64,68},{192,196},{128,132},{16,20},{80,84},{208,212},{144,1... | collective-permute-start | bytes 589832 | tf_op jit(solution)/shard_map/ppermute | solution.py:332
  130.4 14.0 %collective-permute-start.14 = (bf16[384,640]{1,0:T(8,128)(2,1)S(1)}, bf16[384,640]{1,0:T(8,128)(2,1)S(1)}, u32[]{:S(2)}, u32[]{:S(2)}) collective-permute-start(bf16[384,640]{1,0:T(8,128)(2,1)S(1)} %attend.1.att), channel_id=1, source_target_pairs={{0,1},{1,2},{2,3},{3,0},{4,5},{5,6},{6,7},{7,4},{8,9},{9,10},{10,1... | collective-permute-start | bytes 1474568 | tf_op jit(solution)/shard_map/ppermute | solution.py:35
  131.4 12.9 %collective-permute-start.15 = (bf16[384,640]{1,0:T(8,128)(2,1)S(1)}, bf16[384,640]{1,0:T(8,128)(2,1)S(1)}, u32[]{:S(2)}, u32[]{:S(2)}) collective-permute-start(bf16[384,640]{1,0:T(8,128)(2,1)S(1)} %attend.1.att), channel_id=1, source_target_pairs={{0,3},{1,0},{2,1},{3,2},{4,7},{5,4},{6,5},{7,6},{8,11},{9,8},{10,9... | collective-permute-start | bytes 1474568 | tf_op jit(solution)/shard_map/ppermute | solution.py:35
  144.4 8.4 %collective-permute-start.16 = (bf16[192,640]{1,0:T(8,128)(2,1)S(1)}, bf16[192,640]{1,0:T(8,128)(2,1)S(1)}, u32[]{:S(2)}, u32[]{:S(2)}) collective-permute-start(bf16[192,640]{1,0:T(8,128)(2,1)S(1)} %slice.50), channel_id=1, source_target_pairs={{0,1},{1,2},{2,3},{3,0},{4,5},{5,6},{6,7},{7,4},{8,9},{9,10},{10,1... | collective-permute-start | bytes 737288 | tf_op jit(solution)/shard_map/ppermute | solution.py:35
  145.4 7.4 %collective-permute-start.17 = (bf16[192,640]{1,0:T(8,128)(2,1)S(1)}, bf16[192,640]{1,0:T(8,128)(2,1)S(1)}, u32[]{:S(2)}, u32[]{:S(2)}) collective-permute-start(bf16[192,640]{1,0:T(8,128)(2,1)S(1)} %slice.51), channel_id=1, source_target_pairs={{0,3},{1,0},{2,1},{3,2},{4,7},{5,4},{6,5},{7,6},{8,11},{9,8},{10,9... | collective-permute-start | bytes 737288 | tf_op jit(solution)/shard_map/ppermute | solution.py:35
  156.7 7.6 %all-to-all-start.2 = ((f32[4,8,384]{2,1,0:T(8,128)}), f32[4,8,384]{2,1,0:T(8,128)S(1)}, u32[]{:S(2)}, u32[]{:S(2)}) async-start(f32[4,8,384]{2,1,0:T(8,128)} %get-tuple-element.31), calls=%async_computation.2 | async-start | bytes 98304 | tf_op jit(solution)/shard_map/all_to_all | solution.py:409
  165.7 19.9 %all-to-all-start.3 = ((f32[64,1,128]{2,1,0:T(1,128)}), f32[64,1,128]{2,1,0:T(1,128)S(1)}, u32[]{:S(2)}, u32[]{:S(2)}) async-start(f32[64,1,128]{2,1,0:T(1,128)} %bitcast.17), calls=%async_computation.3 | async-start | bytes 65536 | tf_op jit(solution)/shard_map/all_to_all | solution.py:436
  (9 other events, 30.7 us)
Sparse Core Ops, SparseCore 0:
  10.7 104.8 all-gather.1

commit v4 on v3

v4 whole, which is shorter than its diff:
```python
import math

import jax
import jax.numpy as jnp
from jax import lax
from jax.experimental import pallas as pl
from jax.experimental.pallas import tpu as pltpu
from jax.sharding import PartitionSpec as P

D = 5120
HD = 128
HALF = HD // 2
GROUP = 5
QW = GROUP * HD

EPS = 1e-06
GAMMA = 0.99
LAMBDA = 0.95
ROPE_BASE = 1000000.0
REWARD_SCALE = 0.25

X, Z, C, T = 4, 8, 2, 4
ROWS = 384
SHARD = 80
PIECE = D // T
MIB = 1 << 20

F32 = jnp.float32
BF16 = jnp.bfloat16


def place(x, z, c):
    return (x * Z + z) * C + c


def shift_tp(block, distance):
    return lax.ppermute(block, "tp", [(i, (i + distance) % T) for i in range(T)])


def local_call(kernel, operands, places, out_shape, name, flops, nbytes, scratch=(), mib=20):
    spaces = {"s": pltpu.SMEM, "v": pltpu.VMEM, "a": pl.ANY}
    return pl.pallas_call(
        kernel,
        in_specs=[pl.BlockSpec(memory_space=spaces[p]) for p in places],
        out_specs=jax.tree.map(lambda s: pl.BlockSpec(memory_space=pltpu.VMEM), out_shape),
        out_shape=out_shape,
        scratch_shapes=list(scratch),
        compiler_params=pltpu.CompilerParams(vmem_limit_bytes=mib * MIB),
        cost_estimate=pl.CostEstimate(flops=flops, bytes_accessed=nbytes, transcendentals=0),
        name=name,
    )(*operands)


def turned(u, cosine, sine):
    return u * cosine[...] + pltpu.roll(u, HALF, 1) * sine[...]


def norm_kernel(order, own, below, above, first, second, gain, normed_out):
    def squares(ref):
        x = ref[...].astype(F32)
        return jnp.sum(x * x, axis=-1, keepdims=True)

    half = first.shape[0]
    far = jnp.concatenate([squares(first), squares(second)], axis=0)
    mean = (squares(own) + squares(below) + squares(above) + far) / D
    scale = lax.rsqrt(mean + EPS)
    for at, ref in enumerate((own, below, above)):
        normed_out[at] = (ref[...].astype(F32) * scale * gain[order[at]]).astype(BF16)
    normed_out[T - 1, :half] = (first[...].astype(F32) * scale[:half] * gain[order[T - 1]]).astype(BF16)
    normed_out[T - 1, half:] = (second[...].astype(F32) * scale[half:] * gain[order[T - 1]]).astype(BF16)


def norm(order, pieces, gain):
    shape = jax.ShapeDtypeStruct((T, ROWS, PIECE), BF16)
    return local_call(norm_kernel, [order, *pieces, gain], "s" + "v" * 6, shape, "norm", 6 * ROWS * D, 4 * ROWS * D)


def project_kv_kernel(
    order, normed, w_own, w_other, bias, cosine, sine, kv_out, key_out, value_out, mark_out, joined, sems
):
    core = order[T]
    copies = []
    for k in range(T):
        for at, (ref, lane) in enumerate(((w_own, core), (w_other, 1 - core))):
            copy = pltpu.make_async_copy(ref.at[order[k]], joined.at[k, :, lane], sems.at[k, at])
            copy.start()
            copies.append(copy)
    total = jnp.zeros((ROWS, 2 * HD), F32)
    for k in range(T):
        copies[2 * k].wait()
        copies[2 * k + 1].wait()
        total += jnp.dot(normed[k], joined[k].reshape(PIECE, 2 * HD), preferred_element_type=F32)
    key = turned(total[:, :HD] + bias[:, :HD], cosine, sine).astype(BF16)
    value = (total[:, HD:] + bias[:, HD:]).astype(BF16)
    kv_out[:, :HD] = key
    kv_out[:, HD:] = value
    key_out[...] = key
    value_out[...] = value
    mark_out[...] = jnp.zeros_like(mark_out)


def project_kv(order, normed, w_own, w_other, bias, cosine, sine):
    one = jax.ShapeDtypeStruct((ROWS, HD), BF16)
    return local_call(
        project_kv_kernel,
        [order, normed, w_own, w_other, bias, cosine, sine],
        "svaavvv",
        [jax.ShapeDtypeStruct((ROWS, 2 * HD), BF16), one, one, jax.ShapeDtypeStruct((1, ROWS), jnp.int32)],
        "project_kv",
        4 * ROWS * D * HD,
        2 * D * (2 * HD + ROWS),
        [pltpu.VMEM((T, Z, C, SHARD, 2 * HD), BF16), pltpu.SemaphoreType.DMA((T, 2))],
    )


def project_q_kernel(order, normed, w, bias, cosine, sine, q_out, held, acc, sems):
    parts = 4
    members = Z * C // parts

    def copies(k):
        for part in range(parts):
            source = w.at[pl.ds(order[k] * Z * C + part * members, members), 1]
            yield pltpu.make_async_copy(source, held.at[k, pl.ds(part * members, members)], sems.at[k, part])

    for k in range(2):
        for copy in copies(k):
            copy.start()
    for k in range(T):
        for copy in copies(k):
            copy.wait()
        if k + 2 < T:
            for copy in copies(k + 2):
                copy.start()
        part = jnp.dot(normed[k], held[k].reshape(PIECE, QW), preferred_element_type=F32)
        acc[...] = part if k == 0 else acc[...] + part
    for head in range(GROUP):
        span = slice(head * HD, (head + 1) * HD)
        q_out[:, span] = turned(acc[:, span] + bias[:, span], cosine, sine).astype(BF16)


def project_q(order, normed, w, bias, cosine, sine):
    return local_call(
        project_q_kernel,
        [order, normed, w, bias, cosine, sine],
        "svavvv",
        jax.ShapeDtypeStruct((ROWS, QW), BF16),
        "project_q",
        2 * ROWS * D * QW,
        2 * D * (QW + ROWS),
        [pltpu.VMEM((T, Z * C, SHARD, QW), BF16), pltpu.VMEM((ROWS, QW), F32), pltpu.SemaphoreType.DMA((T, 4))],
        52,
    )


def attend_kernel(index, q, kv, mine, other, out, seen, bias):
    core = index[1]
    seen[core, :ROWS] = mine[...]
    seen[1 - core, :ROWS] = other[...]
    seen[0, ROWS:] = kv[:, :HD]
    seen[1, ROWS:] = kv[:, HD:]
    row = lax.broadcasted_iota(jnp.int32, (ROWS, ROWS), 0)
    col = lax.broadcasted_iota(jnp.int32, (ROWS, ROWS), 1)
    bias[:, :ROWS] = jnp.where(jnp.full((ROWS, ROWS), index[0], jnp.int32) > 0, 0.0, -jnp.inf)
    bias[:, ROWS:] = jnp.where(row >= col, 0.0, -jnp.inf)
    for head in range(GROUP):
        span = slice(head * HD, (head + 1) * HD)
        scores = lax.dot_general(q[:, span], seen[0], (((1,), (1,)), ((), ())), preferred_element_type=F32)
        scores = scores + bias[...]
        peak = jnp.max(scores, axis=-1, keepdims=True)
        weights = jnp.exp2((scores - peak) * (HD**-0.5 * math.log2(math.e)))
        total = jnp.sum(weights, axis=-1, keepdims=True)
        mixed = jnp.dot(weights.astype(BF16), seen[1], preferred_element_type=F32)
        out[:, span] = (mixed / total).astype(BF16)


def attend(index, q, kv, mine, other):
    return local_call(
        attend_kernel,
        [index, q, kv, mine, other],
        "svvvv",
        jax.ShapeDtypeStruct((ROWS, QW), BF16),
        "attend",
        4 * ROWS * 2 * ROWS * QW,
        4 * ROWS * QW,
        [pltpu.VMEM((2, 2 * ROWS, HD), BF16), pltpu.VMEM((ROWS, 2 * ROWS), F32)],
    )


def times(a, w):
    return lax.dot_general(a, w, (((1,), (1,)), ((), ())), preferred_element_type=F32)


def halves_kernel(below, above, total, first, second):
    half = first.shape[0]
    first[...] = below[:half]
    second[...] = above[half:]


def stack_kernel(first, second, out):
    out[0] = first[...]
    out[1] = second[...]


def rows_of(w, group):
    return w[pl.ds(lax.rem(group + 2, X) * Z * C, Z * C)].reshape(PIECE, QW)


def out_own_kernel(order, att, w, out):
    out[...] = times(att[...], rows_of(w, order[0]))


def out_next_kernel(order, total, below, above, w, out):
    some = total[...] + times(below[...], rows_of(w, order[1]))
    out[...] = some + times(above[...], rows_of(w, order[2]))


def out_last_kernel(order, tokens, total, first, second, w, gain, head, resid_out, stats_out):
    lane = lax.broadcasted_iota(jnp.int32, (ROWS, HD), 1)
    resid = tokens[...].astype(F32) + total[...] + times(jnp.concatenate([first[...], second[...]], axis=0), rows_of(w, order[T - 1]))
    resid_out[...] = resid.astype(BF16)
    squares = jnp.sum(resid * resid, axis=-1, keepdims=True)
    products = jnp.sum(resid * gain[...] * head[...], axis=-1, keepdims=True)
    both = jnp.where(lane == 0, squares, products).T[:8, :]
    for at in range(T):
        stats_out[at] = both


def values_kernel(stats, critic_bias, reward, discount, matrix, tail, edge, values_out, local_out, records_out):
    sums = stats[0] + stats[1] + stats[2] + stats[3]
    values = sums[1:2] * lax.rsqrt(sums[0:1] / D + EPS) + critic_bias[0]
    lane = lax.broadcasted_iota(jnp.int32, (1, ROWS), 1)
    following = jnp.where(lane == ROWS - 1, 0.0, pltpu.roll(values, ROWS - 1, 1))
    delta = reward[...] + discount[...] * following - values
    local = lax.dot_general(
        jnp.broadcast_to(delta, (8, ROWS)),
        matrix[...],
        (((1,), (1,)), ((), ())),
        precision=lax.Precision.HIGHEST,
        preferred_element_type=F32,
    )[0:1]
    values_out[...] = values
    local_out[...] = local
    head = lane[:, :HD] == 0
    record = jnp.zeros((1, HD), F32)
    for at, row in enumerate((values, local, tail[...], edge[...])):
        first = jnp.sum(jnp.where(head, row[:, :HD], 0.0), axis=-1, keepdims=True)
        record = jnp.where(lane[:, :HD] == at, first, record)
    records_out[...] = jnp.broadcast_to(record, records_out.shape)


def advantages_kernel(index, records, local, tail, edge, out):
    n = records.shape[0]
    row = lax.broadcasted_iota(jnp.int32, (n, HD), 0)

    def column(at):
        return jnp.broadcast_to(records[:, at : at + 1], (n, HD))

    def later(x, distance, fill):
        return jnp.where(row < n - distance, pltpu.roll(x, n - distance, 0), fill)

    first = column(0)
    term = column(1) + column(3) * later(first, 1, 0.0)
    decay = column(2)
    distance = 1
    while distance < n:
        term = term + decay * later(term, distance, 0.0)
        decay = decay * later(decay, distance, 1.0)
        distance *= 2
    after = row == index[0] + 1
    carry = jnp.sum(jnp.where(after, term, 0.0), axis=0, keepdims=True)
    value = jnp.sum(jnp.where(after, first, 0.0), axis=0, keepdims=True)
    for at in range(0, ROWS, HD):
        span = slice(at, at + HD)
        out[:, span] = local[:, span] + edge[:, span] * value + tail[:, span] * carry


def gather_by_all_to_all(block, axis, groups, n):
    everywhere = jnp.broadcast_to(block[None], (n, *block.shape))
    return lax.all_to_all(everywhere, axis, 0, 0, axis_index_groups=groups)


Z_GROUPS = [[place(x, z, c) for z in range(Z)] for x in range(X) for c in range(C)]
X_GROUPS = [[place(x, z, c) for x in range(X)] for z in range(Z) for c in range(C)]


def other_core(block):
    return lax.ppermute(block, "ctx", [(i, i ^ 1) for i in range(X * Z * C)])


OVER_X = ((1, 0), (3, 0), (2, 0))
OVER_Z = ((0, 2), (0, 6), (0, 4))
LAST = ((0, 1),)
TREES = ((OVER_X, OVER_Z, LAST), (OVER_Z, OVER_X, LAST))


def broadcast_anchor(key, value):
    here = lax.axis_index("ctx")
    x, z, core = here // (Z * C), here // C % Z, here % C
    block = jnp.where(core == 0, key, lax.ppermute(value, "ctx", [(0, 1)]))
    holders = [[(0, 0)], [(0, 0)]]
    for stages in zip(*TREES):
        holding = jnp.zeros((), jnp.bool_)
        for c in range(C):
            xs, zs = ({h[axis] for h in holders[c]} for axis in range(2))
            among = lambda at, seen: sum((at == v).astype(jnp.int32) for v in seen) > 0
            holding |= (core == c) & among(x, sorted(xs)) & among(z, sorted(zs))
        sent = None
        fresh = [[], []]
        for shifts in zip(*stages):
            pairs = []
            for c, (dx, dz) in enumerate(shifts):
                targets = [((px + dx) % X, (pz + dz) % Z) for px, pz in holders[c]]
                pairs += [(place(*a, c), place(*b, c)) for a, b in zip(holders[c], targets)]
                fresh[c] += targets
            got = lax.ppermute(block, "ctx", pairs)
            sent = got if sent is None else sent + got
        block = jnp.where(holding, block, sent)
        holders = [old + new for old, new in zip(holders, fresh)]
    return block, other_core(block)


def on_device(
    tokens,
    input_gain,
    w_query,
    w_key,
    w_value,
    query_bias,
    key_bias,
    value_bias,
    w_out,
    final_gain,
    critic_head,
    critic_bias,
    rewards,
    turn_ends,
    episode_done,
):
    index = lax.axis_index("ctx")
    mine = lax.axis_index("tp")
    order = jnp.stack([mine, (mine + 3) % T, (mine + 1) % T, (mine + 2) % T, index % C]).astype(jnp.int32)

    corner = [
        (place(x, z, c) * T + y, place((y + 2) % X, z, c) * T + x)
        for x in range(X)
        for z in range(Z)
        for c in range(C)
        for y in range(T)
    ]
    out_block = lax.ppermute(w_out.T, ("ctx", "tp"), corner)
    both = local_call(
        stack_kernel, [out_block, w_query], "vv", jax.ShapeDtypeStruct((2, SHARD, QW), BF16), "stack", 0, 8 * SHARD * QW
    )
    weights = lax.all_gather(both, "ctx")

    half = ROWS // 2
    below, above = shift_tp(tokens, 1), shift_tp(tokens, -1)
    kv_part = gather_by_all_to_all(jnp.concatenate([w_key, w_value], axis=1), "ctx", Z_GROUPS, Z)
    below, above, kv_part = lax.optimization_barrier((below, above, kv_part))
    first, second = shift_tp(below[:half], 1), shift_tp(above[half:], -1)
    kv_own = gather_by_all_to_all(kv_part, "ctx", X_GROUPS, X)
    first, second, kv_own = lax.optimization_barrier((first, second, kv_own))
    normed = norm(order, (tokens, below, above, first, second), input_gain.reshape(T, 1, PIECE))
    kv_other = other_core(kv_own)
    positions = (index * ROWS + jnp.arange(ROWS)).astype(F32)
    steps = jnp.arange(HALF).astype(F32)
    inverse = 1.0 / ROPE_BASE ** (steps * 2.0 / HD)
    angle = positions[:, None] * inverse[None, :]
    cosine, sine = jnp.cos(angle), jnp.sin(angle)
    cosine = jnp.concatenate([cosine, cosine], axis=1)
    sine = jnp.concatenate([-sine, sine], axis=1)
    kv_bias = jnp.concatenate([key_bias, value_bias])[None, :]
    kv, key, value, mark = project_kv(order, normed, kv_own, kv_other, kv_bias, cosine, sine)
    query = project_q(order, normed, weights, query_bias[None, :], cosine, sine)
    held, sent = broadcast_anchor(key, value)
    att = attend(jnp.stack([index, index % C]).astype(jnp.int32), query, kv, held, sent)

    weights, att = lax.optimization_barrier((weights, att))
    w_o = weights[:, 0]
    below, above = shift_tp(att, 1), shift_tp(att, -1)
    wide = jax.ShapeDtypeStruct((ROWS, PIECE), F32)
    flops, nbytes = 2 * ROWS * QW * PIECE, 6 * MIB
    total = local_call(out_own_kernel, [order, att, w_o], "svv", wide, "out_own", flops, nbytes)
    pair = jax.ShapeDtypeStruct((half, QW), BF16)
    first, second = local_call(
        halves_kernel, [below, above, total], "vva", [pair, pair], "halves", 0, 4 * half * QW
    )
    first, second = shift_tp(first, 1), shift_tp(second, -1)
    total = local_call(out_next_kernel, [order, total, below, above, w_o], "svvvv", wide, "out_next", 2 * flops, nbytes)
    residual_stream, stats = local_call(
        out_last_kernel,
        [order, tokens, total, first, second, w_o, final_gain[None, :], critic_head[None, :]],
        "svvvvvvv",
        [jax.ShapeDtypeStruct((ROWS, PIECE), BF16), jax.ShapeDtypeStruct((T, 8, ROWS), F32)],
        "out_last",
        flops,
        nbytes,
    )
    stats = lax.all_to_all(stats, "tp", 0, 0)

    turn_ends, episode_done = turn_ends + mark[0], episode_done + mark[0]
    ends = jnp.maximum(turn_ends, episode_done)
    discount = jnp.where(ends > 0, GAMMA, 1.0).astype(F32) * (1 - episode_done).astype(F32)
    reward = REWARD_SCALE * (rewards * ends).astype(F32)
    decaying = ends * (1 - episode_done)
    zero_int = jnp.zeros((1,), jnp.int32)
    decay_count = jnp.concatenate([zero_int, jnp.cumsum(decaying)])
    done_count = jnp.concatenate([zero_int, jnp.cumsum(episode_done)])
    rate = GAMMA * LAMBDA
    later = jnp.arange(ROWS)[None, :] >= jnp.arange(ROWS)[:, None]
    same_episode = done_count[None, :ROWS] == done_count[:ROWS, None]
    powers = (decay_count[None, :ROWS] - decay_count[:ROWS, None]).astype(F32)
    matrix = jnp.where(later & same_episode, jnp.power(rate, powers), 0.0)
    tail_powers = (decay_count[ROWS] - decay_count[:ROWS]).astype(F32)
    tail = jnp.where(done_count[ROWS] == done_count[:ROWS], jnp.power(rate, tail_powers), 0.0)[None, :]
    edge = (matrix[:, ROWS - 1] * discount[ROWS - 1])[None, :]

    n = lax.axis_size("ctx")
    line = jax.ShapeDtypeStruct((1, ROWS), F32)
    values, local, records = local_call(
        values_kernel,
        [stats, critic_bias, reward[None, :], discount[None, :], matrix, tail, edge],
        "vsvvvvv",
        [line, line, jax.ShapeDtypeStruct((n, HD), F32)],
        "values",
        2 * ROWS * ROWS,
        MIB,
    )
    records = lax.all_to_all(records, "ctx", 0, 0, tiled=True)
    advantages = local_call(
        advantages_kernel,
        [index.astype(jnp.int32)[None], records, local, tail, edge],
        "svvvv",
        line,
        "advantages",
        ROWS,
        MIB,
    )
    return (residual_stream, values[0], advantages[0])


def solution(mesh):
    in_specs = (
        P("ctx", "tp"),
        P(),
        P("ctx", "tp"),
        P("ctx", "tp"),
        P("ctx", "tp"),
        P("tp"),
        P("tp"),
        P("tp"),
        P("tp", "ctx"),
        P("tp"),
        P("tp"),
        P(),
        P("ctx"),
        P("ctx"),
        P("ctx"),
    )
    out_specs = (P("ctx", "tp"), P("ctx"), P("ctx"))
    return jax.shard_map(
        on_device, mesh=mesh, in_specs=in_specs, out_specs=out_specs, check_vma=False
    )
```

time: 194 us -> 187 us (0.964)
  waiting for transfers between devices: 55.9 us -> 48.8 us
  local copies, waits for them, and re-layouts: 11.2 us -> 15.4 us
  Pallas kernels: 29.1 us -> 26.7 us
    all_gather x1, waiting for transfers between devices: 28.4 us -> 8.06 us  [on_device(): weights = lax.all_gather(both, 'ctx')]
    ppermute x8, starting transfers between devices: 6.32 us -> 14.2 us  [the longest x7 13 us: broadcast_anchor(): got = lax.ppermute(block, 'ctx', pairs)]
    ppermute x8, starting transfers between devices: 22.5 us -> 15 us  [shift_tp(): lax.ppermute(block, 'tp', [(i, (i + distance) % T) for i in range(T)])]
    ppermute x8, waiting for transfers between devices: 1.8 us -> 9.35 us  [the longest x7 7.9 us: broadcast_anchor(): got = lax.ppermute(block, 'ctx', pairs)]
    squeeze x0 -> x1, local copies, waits for them, and re-layouts: none -> 3.43 us  [on_device(): w_o = weights[:, 0]]
    all_to_all x1, starting transfers between devices: 10.6 us -> 7.72 us  [on_device(): records = lax.all_to_all(records, 'ctx', 0, 0, tiled=True)]
    ppermute x8, waiting for transfers between devices: 12.4 us -> 15 us  [shift_tp(): lax.ppermute(block, 'tp', [(i, (i + distance) % T) for i in range(T)])]
    pallas_call x9 -> x11, Pallas kernels: 29.1 us -> 26.7 us  [local_call(): pl.pallas_call(kernel, in_specs=[pl.BlockSpec(memory_space=spaces[p]) for...]
  transfers between devices with their start and end apart: 22 -> 23, of which waited for: 9 -> 16; matrix products, arithmetic and copies ran while one was open for 6% -> 7% of each run, Pallas kernels for 11% -> 10%
where the time goes in v4:
time: 187 us; the launch traced here: 186 us
  starting transfers between devices  53.3 us (29%)
  waiting for transfers between devices  48.8 us (26%)
  Pallas kernels  26.7 us (14%)
  blocking collectives  20.6 us (11%)
  local copies, waits for them, and re-layouts  15.4 us (8%)
  between operations  15.1 us (8%)
  other arithmetic  6.44 us (3%)
    pallas_call x11, Pallas kernels, local_call(): pl.pallas_call(kernel, in_specs=[pl.BlockSpec(memory_space=spaces[p]) for...  26.7 us
    all_to_all x1, blocking collectives, gather_by_all_to_all(): return lax.all_to_all(everywhere, axis, 0, 0, axis_index_groups=groups)  20.6 us
    ppermute x8, starting transfers between devices, shift_tp(): lax.ppermute(block, 'tp', [(i, (i + distance) % T) for i in range(T)])  15 us
    ppermute x8, waiting for transfers between devices, shift_tp(): lax.ppermute(block, 'tp', [(i, (i + distance) % T) for i in range(T)])  15 us
    ppermute x7, starting transfers between devices, broadcast_anchor(): got = lax.ppermute(block, 'ctx', pairs)  13 us
    all_to_all x1, waiting for transfers between devices, on_device(): records = lax.all_to_all(records, 'ctx', 0, 0, tiled=True)  8.75 us
    all_gather x1, waiting for transfers between devices, on_device(): weights = lax.all_gather(both, 'ctx')  8.06 us
    ppermute x7, waiting for transfers between devices, broadcast_anchor(): got = lax.ppermute(block, 'ctx', pairs)  7.9 us
  transfers between devices with their start and end apart: 23, of which 16 were waited for; matrix products, arithmetic and copies ran while one was open for 7% of the time, Pallas kernels for 10%

profile of v4, /device:TPU:1, one launch (start us, length us, event | category | flops | bytes accessed | tf_op | source)
XLA Modules:
  0.0 186.3 jit_solution(15833836792339052593)
XLA Ops:
  7.2 3.7 %collective-permute-start = (bf16[80,640]{1,0:T(8,128)(2,1)}, bf16[80,640]{1,0:T(8,128)(2,1)S(1)}, u32[]{:S(2)}, u32[]{:S(2)}) collective-permute-start(bf16[80,640]{1,0:T(8,128)(2,1)} %bitcast.36), channel_id=1, source_target_pairs={{0,128},{1,192},{2,0},{3,64},{4,132},{5,196},{6,4},{7,68},{8,136},... | collective-permute-start | bytes 307208 | tf_op jit(solution)/shard_map/ppermute | solution.py:350
  10.9 2.4 %collective-permute-done.first = bf16[80,640]{1,0:T(8,128)(2,1)S(1)} collective-permute-done((bf16[80,640]{1,0:T(8,128)(2,1)}, bf16[80,640]{1,0:T(8,128)(2,1)S(1)}, u32[]{:S(2)}, u32[]{:S(2)}) %collective-permute-start) | collective-permute-done | bytes 102432 | tf_op jit(solution)/shard_map/ppermute | solution.py:350
  15.0 3.1 %collective-permute-start.1 = (bf16[384,1280]{1,0:T(8,128)(2,1)}, bf16[384,1280]{1,0:T(8,128)(2,1)S(1)}, u32[]{:S(2)}, u32[]{:S(2)}) collective-permute-start(bf16[384,1280]{1,0:T(8,128)(2,1)} %tokens.1), channel_id=1, source_target_pairs={{0,1},{1,2},{2,3},{3,0},{4,5},{5,6},{6,7},{7,4},{8,9},{9,10},{10,1... | collective-permute-start | bytes 2949128 | tf_op jit(solution)/shard_map/ppermute | solution.py:37
  18.1 3.5 %collective-permute-start.2 = (bf16[384,1280]{1,0:T(8,128)(2,1)}, bf16[384,1280]{1,0:T(8,128)(2,1)}, u32[]{:S(2)}, u32[]{:S(2)}) collective-permute-start(bf16[384,1280]{1,0:T(8,128)(2,1)} %tokens.1), channel_id=1, source_target_pairs={{0,3},{1,0},{2,1},{3,2},{4,7},{5,4},{6,5},{7,6},{8,11},{9,8},{10,9... | collective-permute-start | bytes 2949128 | tf_op jit(solution)/shard_map/ppermute | solution.py:37
  22.4 20.6 %all_to_all.26 = bf16[8,80,256]{2,1,0:T(8,128)(2,1)S(1)} all-to-all(bf16[8,80,256]{2,1,0:T(8,128)(2,1)S(1)} %broadcast_in_dim.59), channel_id=1, replica_groups={{0,8,16,24,32,40,48,56},{4,12,20,28,36,44,52,60},{64,72,80,88,96,104,11..., dimensions={0} | all-to-all | bytes 655360 | tf_op jit(solution)/shard_map/all_to_all | solution.py:279
  44.7 3.5 %all-to-all-start.1 = ((bf16[4,8,80,256]{3,2,1,0:T(8,128)(2,1)}), bf16[4,8,80,256]{3,2,1,0:T(8,128)(2,1)S(1)}, u32[]{:S(2)}, u32[]{:S(2)}) async-start(bf16[4,8,80,256]{3,2,1,0:T(8,128)(2,1)} %broadcast_in_dim.60), calls=%async_computation.1 | async-start | bytes 2621440 | tf_op jit(solution)/shard_map/all_to_all | solution.py:279
  50.0 2.2 %collective-permute-start.4 = (bf16[192,1280]{1,0:T(8,128)(2,1)S(1)}, bf16[192,1280]{1,0:T(8,128)(2,1)S(1)}, u32[]{:S(2)}, u32[]{:S(2)}) collective-permute-start(bf16[192,1280]{1,0:T(8,128)(2,1)S(1)} %slice.46), channel_id=1, source_target_pairs={{0,3},{1,0},{2,1},{3,2},{4,7},{5,4},{6,5},{7,6},{8,11},{9,8},{10,9... | collective-permute-start | bytes 1474568 | tf_op jit(solution)/shard_map/ppermute | solution.py:37
  52.1 6.6 %collective-permute-done.3.first = bf16[192,1280]{1,0:T(8,128)(2,1)S(1)} collective-permute-done((bf16[192,1280]{1,0:T(8,128)(2,1)S(1)}, bf16[192,1280]{1,0:T(8,128)(2,1)S(1)}, u32[]{:S(2)}, u32[]{:S(2)}) %collective-permute-start.3) | collective-permute-done | bytes 491552 | tf_op jit(solution)/shard_map/ppermute | solution.py:37
  60.6 1.7 all-to-all-done.1.w_own
  62.3 4.7 %collective-permute-start.5 = (bf16[4,8,80,256]{3,2,1,0:T(8,128)(2,1)S(1)}, bf16[4,8,80,256]{3,2,1,0:T(8,128)(2,1)}, u32[]{:S(2)}, u32[]{:S(2)}) collective-permute-start(bf16[4,8,80,256]{3,2,1,0:T(8,128)(2,1)S(1)} %all-to-all-done.1.w_own), channel_id=1, source_target_pairs={{0,4},{4,0},{8,12},{12,8},{16,20},{20,16},{24,28},{28,24},{32,36},... | collective-permute-start | bytes 3932168 | tf_op jit(solution)/shard_map/ppermute | solution.py:287
  71.1 3.4 %norm.1.normed = bf16[4,384,1280]{2,1,0:T(8,128)(2,1)S(1)} custom-call(s32[5]{0:T(128)S(1)} %stack.31.order, bf16[384,1280]{1,0:T(8,128)(2,1)S(1)} %copy-done.1, bf16[384,1280]{1,0:T(8,128)(2,1)S(1)} %collective-permute-done.1.below, bf16[384,1280]{1,0:T(8,128)(2,1)} %collective-permute-done.2.above, bf16[192,1280]{1,0:T(8,128)(2,1)S(1)} %copy-done.5, ...), custom_call_target="tpu_custom_call" | custom-call | flops 11796480 | bytes 7864320 | tf_op jit(solution)/shard_map/norm/pallas_call | solution.py:42
  74.4 4.2 %project_kv.1 = (bf16[384,256]{1,0:T(8,128)(2,1)S(1)}, bf16[384,128]{1,0:T(8,128)(2,1)S(1)}, bf16[384,128]{1,0:T(8,128)(2,1)S(1)}, s32[1,384]{1,0:T(1,128)S(1)}) custom-call(s32[5]{0:T(128)S(1)} %stack.31.order, bf16[4,384,1280]{2,1,0:T(8,128)(2,1)S(1)} %norm.1.normed, bf16[4,8,80,256]{3,2,1,0:T(8,128)(2,1)S(1)} %all-to-all-done.1.w_own, ...), custom_call_target="tpu_custom_call" | custom-call | flops 1006632960 | bytes 6553600 | tf_op jit(solution)/shard_map/project_kv/pallas_call | solution.py:42
  78.6 1.9 copy-done
  84.6 2.5 %collective-permute-start.7 = (bf16[384,128]{1,0:T(8,128)(2,1)S(1)}, bf16[384,128]{1,0:T(8,128)(2,1)S(1)}, u32[]{:S(2)}, u32[]{:S(2)}) collective-permute-start(bf16[384,128]{1,0:T(8,128)(2,1)S(1)} %broadcast_select_fusion), channel_id=1, source_target_pairs={{0,64},{4,20},{1,65},{5,21},{2,66},{6,22},{3,67},{7,23}} | collective-permute-start | bytes 294920 | tf_op jit(solution)/shard_map/ppermute | solution.py:315
  87.1 3.9 %collective-permute-start.8 = (bf16[384,128]{1,0:T(8,128)(2,1)S(1)}, bf16[384,128]{1,0:T(8,128)(2,1)S(1)}, u32[]{:S(2)}, u32[]{:S(2)}) collective-permute-start(bf16[384,128]{1,0:T(8,128)(2,1)S(1)} %broadcast_select_fusion), channel_id=1, source_target_pairs={{0,192},{4,52},{1,193},{5,53},{2,194},{6,54},{3,195},{7,55}} | collective-permute-start | bytes 294920 | tf_op jit(solution)/shard_map/ppermute | solution.py:315
  92.5 1.8 collective-permute-done.8
  94.3 1.8 collective-permute-done.9
  104.8 2.8 %collective-permute-done.13 = bf16[384,128]{1,0:T(8,128)(2,1)S(1)} collective-permute-done((bf16[384,128]{1,0:T(8,128)(2,1)S(1)}, bf16[384,128]{1,0:T(8,128)(2,1)S(1)}, u32[]{:S(2)}, u32[]{:S(2)}) %collective-permute-start.13) | collective-permute-done | bytes 98336 | tf_op jit(solution)/shard_map/ppermute | solution.py:315
  108.5 8.1 %all-gather.3.cloned.1.call-done = bf16[128,80,640]{2,1,0:T(8,128)(2,1)} async-done(((bf16[2,80,640]{2,1,0:T(8,128)(2,1)}), bf16[128,80,640]{2,1,0:T(8,128)(2,1)}) %all-gather.3.cloned.1.call-update) | async-done | bytes 13107216 | tf_op jit(solution)/shard_map/all_gather | solution.py:354
  117.5 7.7 %project_q.1.q = bf16[384,640]{1,0:T(8,128)(2,1)S(1)} custom-call(s32[5]{0:T(128)S(1)} %stack.31.order, bf16[4,384,1280]{2,1,0:T(8,128)(2,1)} %copy-done, bf16[64,2,80,640]{3,2,1,0:T(8,128)(2,1)} %bitcast.32, f32[1,640]{1,0:T(1,128)S(1)} %broadcast_in_dim.61.bias, f32[384,128]{1,0:T(8,128)S(1)} %get-tuple-element.48.cosine, f32[384,128]{1,0:T(8,128)S(1)} %copy-done.3), custom_call_target="tpu_custom_call" | custom-call | flops 2516582400 | bytes 10485760 | tf_op jit(solution)/shard_map/project_q/pallas_call | solution.py:42
  125.1 2.8 %attend.1.att = bf16[384,640]{1,0:T(8,128)(2,1)S(1)} custom-call(s32[2]{0:T(128)S(1)} %pad_add_fusion.2.index, bf16[384,640]{1,0:T(8,128)(2,1)S(1)} %project_q.1.q, bf16[384,256]{1,0:T(8,128)(2,1)S(1)} %get-tuple-element.28.kv, bf16[384,128]{1,0:T(8,128)(2,1)S(1)} %broadcast_select_fusion.1.mine, bf16[384,128]{1,0:T(8,128)(2,1)S(1)} %collective-permute-done.14.other), custom_call_target="tpu_custom_call" | custom-call | flops 754974720 | bytes 983040 | tf_op jit(solution)/shard_map/attend/pallas_call | solution.py:42
  129.3 1.5 collective-permute-start.16
  130.7 3.4 %slice_bitcast_fusion.w = bf16[64,80,640]{2,1,0:T(8,128)(2,1)S(1)} fusion(bf16[64,2,80,640]{3,2,1,0:T(8,128)(2,1)} %bitcast.33), kind=kLoop, calls=%fused_computation | loop fusion | bytes 13107200 | tf_op jit(solution)/shard_map/squeeze | solution.py:379
  134.2 1.5 out_own.1.total
  135.7 6.2 %collective-permute-done.15.below = bf16[384,640]{1,0:T(8,128)(2,1)S(1)} collective-permute-done((bf16[384,640]{1,0:T(8,128)(2,1)S(1)}, bf16[384,640]{1,0:T(8,128)(2,1)S(1)}, u32[]{:S(2)}, u32[]{:S(2)}) %collective-permute-start.15) | collective-permute-done | bytes 491552 | tf_op jit(solution)/shard_map/ppermute | solution.py:37
  142.9 1.8 collective-permute-start.18
  146.0 2.3 %out_next.1.total = f32[384,1280]{1,0:T(8,128)S(1)} custom-call(s32[5]{0:T(128)S(1)} %stack.31.order, f32[384,1280]{1,0:T(8,128)S(1)} %out_own.1.total, bf16[384,640]{1,0:T(8,128)(2,1)S(1)} %collective-permute-done.15.below, bf16[384,640]{1,0:T(8,128)(2,1)S(1)} %collective-permute-done.16.above, bf16[64,80,640]{2,1,0:T(8,128)(2,1)S(1)} %slice_bitcast_fusion.w), custom_call_target="tpu_custom_call" | custom-call | flops 1258291200 | bytes 6291456 | tf_op jit(solution)/shard_map/out_next/pallas_call | solution.py:42
  149.6 2.7 %out_last.1 = (bf16[384,1280]{1,0:T(8,128)(2,1)}, f32[4,8,384]{2,1,0:T(8,128)}) custom-call(s32[5]{0:T(128)S(1)} %stack.31.order, bf16[384,1280]{1,0:T(8,128)(2,1)S(1)} %copy-done.1, f32[384,1280]{1,0:T(8,128)S(1)} %out_next.1.total, bf16[192,640]{1,0:T(8,128)(2,1)S(1)} %collective-permute-done.17.first, ...), custom_call_target="tpu_custom_call" | custom-call | flops 629145600 | bytes 6291456 | tf_op jit(solution)/shard_map/out_last/pallas_call | solution.py:42
  152.2 3.7 %all-to-all-start.2 = ((f32[4,8,384]{2,1,0:T(8,128)}), f32[4,8,384]{2,1,0:T(8,128)S(1)}, u32[]{:S(2)}, u32[]{:S(2)}) async-start(f32[4,8,384]{2,1,0:T(8,128)} %get-tuple-element.36), calls=%async_computation.2 | async-start | bytes 98304 | tf_op jit(solution)/shard_map/all_to_all | solution.py:399
  156.8 3.5 %all-to-all-done.2.stats = f32[4,8,384]{2,1,0:T(8,128)S(1)} async-done(((f32[4,8,384]{2,1,0:T(8,128)}), f32[4,8,384]{2,1,0:T(8,128)S(1)}, u32[]{:S(2)}, u32[]{:S(2)}) %all-to-all-start.2) | async-done | bytes 49184 | tf_op jit(solution)/shard_map/all_to_all | solution.py:399
  161.6 7.7 %all-to-all-start.3 = ((f32[64,1,128]{2,1,0:T(1,128)}), f32[64,1,128]{2,1,0:T(1,128)S(1)}, u32[]{:S(2)}, u32[]{:S(2)}) async-start(f32[64,1,128]{2,1,0:T(1,128)} %bitcast.19), calls=%async_computation.3 | async-start | bytes 65536 | tf_op jit(solution)/shard_map/all_to_all | solution.py:429
  170.0 8.8 %all-to-all-done.3 = f32[64,1,128]{2,1,0:T(1,128)S(1)} async-done(((f32[64,1,128]{2,1,0:T(1,128)}), f32[64,1,128]{2,1,0:T(1,128)S(1)}, u32[]{:S(2)}, u32[]{:S(2)}) %all-to-all-start.3) | async-done | bytes 32800 | tf_op jit(solution)/shard_map/all_to_all | solution.py:429
  (110 shorter events, 35.6 us)
Async XLA Ops:
  7.2 61.8 %copy-start.1 = (bf16[384,1280]{1,0:T(8,128)(2,1)S(1)}, bf16[384,1280]{1,0:T(8,128)(2,1)}, u32[]{:S(2)}) copy-start(bf16[384,1280]{1,0:T(8,128)(2,1)} %tokens.1) | copy-start | bytes 2949124
  7.2 109.4 %all-gather.3.cloned.1.call-start = ((), (), s32[]{:S(2)}) async-start(), calls=%async_computation.4 | async-start | bytes 13312000 | tf_op jit(solution)/shard_map/all_gather | solution.py:354
  7.2 6.1 %collective-permute-start = (bf16[80,640]{1,0:T(8,128)(2,1)}, bf16[80,640]{1,0:T(8,128)(2,1)S(1)}, u32[]{:S(2)}, u32[]{:S(2)}) collective-permute-start(bf16[80,640]{1,0:T(8,128)(2,1)} %bitcast.36), channel_id=1, source_target_pairs={{0,128},{1,192},{2,0},{3,64},{4,132},{5,196},{6,4},{7,68},{8,136},... | collective-permute-start | bytes 307208 | tf_op jit(solution)/shard_map/ppermute | solution.py:350
  14.2 52.8 %copy-start.14 = (f32[640]{0:T(1024)S(1)}, f32[640]{0:T(1024)}, u32[]{:S(2)}) copy-start(f32[640]{0:T(1024)} %param.20) | copy-start | bytes 7684
  14.2 52.8 %copy-start.12 = (f32[1280]{0:T(1024)S(1)}, f32[1280]{0:T(1024)}, u32[]{:S(2)}) copy-start(f32[1280]{0:T(1024)} %param.24) | copy-start | bytes 15364
  14.2 52.8 %copy-start.13 = (f32[1280]{0:T(1024)S(1)}, f32[1280]{0:T(1024)}, u32[]{:S(2)}) copy-start(f32[1280]{0:T(1024)} %param.25) | copy-start | bytes 15364
  14.2 53.7 %copy-start.16 = (f32[128]{0:T(128)S(1)}, f32[128]{0:T(128)}, u32[]{:S(2)}) copy-start(f32[128]{0:T(128)} %param.22) | copy-start | bytes 1540
  14.2 53.7 %copy-start.17 = (f32[128]{0:T(128)S(1)}, f32[128]{0:T(128)}, u32[]{:S(2)}) copy-start(f32[128]{0:T(128)} %param.21) | copy-start | bytes 1540
  14.2 54.7 %copy-start.9 = (f32[5120]{0:T(1024)S(1)}, f32[5120]{0:T(1024)}, u32[]{:S(2)}) copy-start(f32[5120]{0:T(1024)} %param.16) | copy-start | bytes 61444
  15.0 28.5 %collective-permute-start.1 = (bf16[384,1280]{1,0:T(8,128)(2,1)}, bf16[384,1280]{1,0:T(8,128)(2,1)S(1)}, u32[]{:S(2)}, u32[]{:S(2)}) collective-permute-start(bf16[384,1280]{1,0:T(8,128)(2,1)} %tokens.1), channel_id=1, source_target_pairs={{0,1},{1,2},{2,3},{3,0},{4,5},{5,6},{6,7},{7,4},{8,9},{9,10},{10,1... | collective-permute-start | bytes 2949128 | tf_op jit(solution)/shard_map/ppermute | solution.py:37
  18.1 25.4 %collective-permute-start.2 = (bf16[384,1280]{1,0:T(8,128)(2,1)}, bf16[384,1280]{1,0:T(8,128)(2,1)}, u32[]{:S(2)}, u32[]{:S(2)}) collective-permute-start(bf16[384,1280]{1,0:T(8,128)(2,1)} %tokens.1), channel_id=1, source_target_pairs={{0,3},{1,0},{2,1},{3,2},{4,7},{5,4},{6,5},{7,6},{8,11},{9,8},{10,9... | collective-permute-start | bytes 2949128 | tf_op jit(solution)/shard_map/ppermute | solution.py:37
  44.7 17.7 %all-to-all-start.1 = ((bf16[4,8,80,256]{3,2,1,0:T(8,128)(2,1)}), bf16[4,8,80,256]{3,2,1,0:T(8,128)(2,1)S(1)}, u32[]{:S(2)}, u32[]{:S(2)}) async-start(bf16[4,8,80,256]{3,2,1,0:T(8,128)(2,1)} %broadcast_in_dim.60), calls=%async_computation.1 | async-start | bytes 2621440 | tf_op jit(solution)/shard_map/all_to_all | solution.py:279
  48.2 10.5 %collective-permute-start.3 = (bf16[192,1280]{1,0:T(8,128)(2,1)S(1)}, bf16[192,1280]{1,0:T(8,128)(2,1)S(1)}, u32[]{:S(2)}, u32[]{:S(2)}) collective-permute-start(bf16[192,1280]{1,0:T(8,128)(2,1)S(1)} %slice.45), channel_id=1, source_target_pairs={{0,1},{1,2},{2,3},{3,0},{4,5},{5,6},{6,7},{7,4},{8,9},{9,10},{10,1... | collective-permute-start | bytes 1474568 | tf_op jit(solution)/shard_map/ppermute | solution.py:37
  50.0 9.9 %collective-permute-start.4 = (bf16[192,1280]{1,0:T(8,128)(2,1)S(1)}, bf16[192,1280]{1,0:T(8,128)(2,1)S(1)}, u32[]{:S(2)}, u32[]{:S(2)}) collective-permute-start(bf16[192,1280]{1,0:T(8,128)(2,1)S(1)} %slice.46), channel_id=1, source_target_pairs={{0,3},{1,0},{2,1},{3,2},{4,7},{5,4},{6,5},{7,6},{8,11},{9,8},{10,9... | collective-permute-start | bytes 1474568 | tf_op jit(solution)/shard_map/ppermute | solution.py:37
  62.3 12.1 %collective-permute-start.5 = (bf16[4,8,80,256]{3,2,1,0:T(8,128)(2,1)S(1)}, bf16[4,8,80,256]{3,2,1,0:T(8,128)(2,1)}, u32[]{:S(2)}, u32[]{:S(2)}) collective-permute-start(bf16[4,8,80,256]{3,2,1,0:T(8,128)(2,1)S(1)} %all-to-all-done.1.w_own), channel_id=1, source_target_pairs={{0,4},{4,0},{8,12},{12,8},{16,20},{20,16},{24,28},{28,24},{32,36},... | collective-permute-start | bytes 3932168 | tf_op jit(solution)/shard_map/ppermute | solution.py:287
  68.9 9.7 %copy-start.2 = (f32[384,128]{1,0:T(8,128)}, f32[384,128]{1,0:T(8,128)S(1)}, u32[]{:S(2)}) copy-start(f32[384,128]{1,0:T(8,128)S(1)} %get-tuple-element.49.sine) | copy-start | bytes 589828
  71.1 32.0 %copy-start.15 = (s32[384]{0:T(512)S(1)}, s32[384]{0:T(512)}, u32[]{:S(2)}) copy-start(s32[384]{0:T(512)} %param.27) | copy-start | bytes 4612
  81.4 3.2 %collective-permute-start.6 = (bf16[384,128]{1,0:T(8,128)(2,1)S(1)}, bf16[384,128]{1,0:T(8,128)(2,1)S(1)}, u32[]{:S(2)}, u32[]{:S(2)}) collective-permute-start(bf16[384,128]{1,0:T(8,128)(2,1)S(1)} %get-tuple-element.30), channel_id=1, source_target_pairs={{0,4},{1,5},{2,6},{3,7}} | collective-permute-start | bytes 294920 | tf_op jit(solution)/shard_map/ppermute | solution.py:299
  84.6 7.9 %collective-permute-start.7 = (bf16[384,128]{1,0:T(8,128)(2,1)S(1)}, bf16[384,128]{1,0:T(8,128)(2,1)S(1)}, u32[]{:S(2)}, u32[]{:S(2)}) collective-permute-start(bf16[384,128]{1,0:T(8,128)(2,1)S(1)} %broadcast_select_fusion), channel_id=1, source_target_pairs={{0,64},{4,20},{1,65},{5,21},{2,66},{6,22},{3,67},{7,23}} | collective-permute-start | bytes 294920 | tf_op jit(solution)/shard_map/ppermute | solution.py:315
  87.1 7.2 %collective-permute-start.8 = (bf16[384,128]{1,0:T(8,128)(2,1)S(1)}, bf16[384,128]{1,0:T(8,128)(2,1)S(1)}, u32[]{:S(2)}, u32[]{:S(2)}) collective-permute-start(bf16[384,128]{1,0:T(8,128)(2,1)S(1)} %broadcast_select_fusion), channel_id=1, source_target_pairs={{0,192},{4,52},{1,193},{5,53},{2,194},{6,54},{3,195},{7,55}} | collective-permute-start | bytes 294920 | tf_op jit(solution)/shard_map/ppermute | solution.py:315
  90.9 5.1 %collective-permute-start.9 = (bf16[384,128]{1,0:T(8,128)(2,1)S(1)}, bf16[384,128]{1,0:T(8,128)(2,1)S(1)}, u32[]{:S(2)}, u32[]{:S(2)}) collective-permute-start(bf16[384,128]{1,0:T(8,128)(2,1)S(1)} %broadcast_select_fusion), channel_id=1, source_target_pairs={{0,128},{4,36},{1,129},{5,37},{2,130},{6,38},{3,131},{7,39}} | collective-permute-start | bytes 294920 | tf_op jit(solution)/shard_map/ppermute | solution.py:315
  96.1 4.4 %collective-permute-start.10 = (bf16[384,128]{1,0:T(8,128)(2,1)S(1)}, bf16[384,128]{1,0:T(8,128)(2,1)S(1)}, u32[]{:S(2)}, u32[]{:S(2)}) collective-permute-start(bf16[384,128]{1,0:T(8,128)(2,1)S(1)} %add_select_fusion.1), channel_id=1, source_target_pairs={{0,16},{64,80},{192,208},{128,144},{4,68},{20,84},{52,116},{36,100... | collective-permute-start | bytes 294920 | tf_op jit(solution)/shard_map/ppermute | solution.py:315
  97.4 3.1 %collective-permute-start.11 = (bf16[384,128]{1,0:T(8,128)(2,1)S(1)}, bf16[384,128]{1,0:T(8,128)(2,1)S(1)}, u32[]{:S(2)}, u32[]{:S(2)}) collective-permute-start(bf16[384,128]{1,0:T(8,128)(2,1)S(1)} %add_select_fusion.1), channel_id=1, source_target_pairs={{0,48},{64,112},{192,240},{128,176},{4,196},{20,212},{52,244},{36,... | collective-permute-start | bytes 294920 | tf_op jit(solution)/shard_map/ppermute | solution.py:315
  98.7 3.0 %collective-permute-start.12 = (bf16[384,128]{1,0:T(8,128)(2,1)S(1)}, bf16[384,128]{1,0:T(8,128)(2,1)S(1)}, u32[]{:S(2)}, u32[]{:S(2)}) collective-permute-start(bf16[384,128]{1,0:T(8,128)(2,1)S(1)} %add_select_fusion.1), channel_id=1, source_target_pairs={{0,32},{64,96},{192,224},{128,160},{4,132},{20,148},{52,180},{36,1... | collective-permute-start | bytes 294920 | tf_op jit(solution)/shard_map/ppermute | solution.py:315
  101.7 5.9 %collective-permute-start.13 = (bf16[384,128]{1,0:T(8,128)(2,1)S(1)}, bf16[384,128]{1,0:T(8,128)(2,1)S(1)}, u32[]{:S(2)}, u32[]{:S(2)}) collective-permute-start(bf16[384,128]{1,0:T(8,128)(2,1)S(1)} %add_select_fusion), channel_id=1, source_target_pairs={{0,8},{64,72},{192,200},{128,136},{16,24},{80,88},{208,216},{144,1... | collective-permute-start | bytes 294920 | tf_op jit(solution)/shard_map/ppermute | solution.py:315
  107.7 17.5 %collective-permute-start.14 = (bf16[384,128]{1,0:T(8,128)(2,1)S(1)}, bf16[384,128]{1,0:T(8,128)(2,1)S(1)}, u32[]{:S(2)}, u32[]{:S(2)}) collective-permute-start(bf16[384,128]{1,0:T(8,128)(2,1)S(1)} %broadcast_select_fusion.1.mine), channel_id=1, source_target_pairs={{0,4},{4,0},{8,12},{12,8},{16,20},{20,16},{24,28},{28,24},{32,36},... | collective-permute-start | bytes 294920 | tf_op jit(solution)/shard_map/ppermute | solution.py:287
  128.0 13.9 %collective-permute-start.15 = (bf16[384,640]{1,0:T(8,128)(2,1)S(1)}, bf16[384,640]{1,0:T(8,128)(2,1)S(1)}, u32[]{:S(2)}, u32[]{:S(2)}) collective-permute-start(bf16[384,640]{1,0:T(8,128)(2,1)S(1)} %attend.1.att), channel_id=1, source_target_pairs={{0,1},{1,2},{2,3},{3,0},{4,5},{5,6},{6,7},{7,4},{8,9},{9,10},{10,1... | collective-permute-start | bytes 1474568 | tf_op jit(solution)/shard_map/ppermute | solution.py:37
  129.3 12.6 %collective-permute-start.16 = (bf16[384,640]{1,0:T(8,128)(2,1)S(1)}, bf16[384,640]{1,0:T(8,128)(2,1)S(1)}, u32[]{:S(2)}, u32[]{:S(2)}) collective-permute-start(bf16[384,640]{1,0:T(8,128)(2,1)S(1)} %attend.1.att), channel_id=1, source_target_pairs={{0,3},{1,0},{2,1},{3,2},{4,7},{5,4},{6,5},{7,6},{8,11},{9,8},{10,9... | collective-permute-start | bytes 1474568 | tf_op jit(solution)/shard_map/ppermute | solution.py:37
  141.9 7.7 %collective-permute-start.17 = (bf16[192,640]{1,0:T(8,128)(2,1)S(1)}, bf16[192,640]{1,0:T(8,128)(2,1)S(1)}, u32[]{:S(2)}, u32[]{:S(2)}) collective-permute-start(bf16[192,640]{1,0:T(8,128)(2,1)S(1)} %get-tuple-element.33), channel_id=1, source_target_pairs={{0,1},{1,2},{2,3},{3,0},{4,5},{5,6},{6,7},{7,4},{8,9},{9,10},{10,1... | collective-permute-start | bytes 737288 | tf_op jit(solution)/shard_map/ppermute | solution.py:37
  142.9 6.7 %collective-permute-start.18 = (bf16[192,640]{1,0:T(8,128)(2,1)S(1)}, bf16[192,640]{1,0:T(8,128)(2,1)S(1)}, u32[]{:S(2)}, u32[]{:S(2)}) collective-permute-start(bf16[192,640]{1,0:T(8,128)(2,1)S(1)} %get-tuple-element.34), channel_id=1, source_target_pairs={{0,3},{1,0},{2,1},{3,2},{4,7},{5,4},{6,5},{7,6},{8,11},{9,8},{10,9... | collective-permute-start | bytes 737288 | tf_op jit(solution)/shard_map/ppermute | solution.py:37
  152.2 8.1 %all-to-all-start.2 = ((f32[4,8,384]{2,1,0:T(8,128)}), f32[4,8,384]{2,1,0:T(8,128)S(1)}, u32[]{:S(2)}, u32[]{:S(2)}) async-start(f32[4,8,384]{2,1,0:T(8,128)} %get-tuple-element.36), calls=%async_computation.2 | async-start | bytes 98304 | tf_op jit(solution)/shard_map/all_to_all | solution.py:399
  161.6 17.1 %all-to-all-start.3 = ((f32[64,1,128]{2,1,0:T(1,128)}), f32[64,1,128]{2,1,0:T(1,128)S(1)}, u32[]{:S(2)}, u32[]{:S(2)}) async-start(f32[64,1,128]{2,1,0:T(1,128)} %bitcast.19), calls=%async_computation.3 | async-start | bytes 65536 | tf_op jit(solution)/shard_map/all_to_all | solution.py:429
  (9 other events, 26.2 us)
Sparse Core Ops, SparseCore 0:
  15.1 101.4 all-gather.2

commit v5 on v4

--- a/solution.py
+++ b/solution.py
@@ -52,7 +52,7 @@
 
 
 def turned(u, cosine, sine):
-    return u * cosine[...] + pltpu.roll(u, HALF, 1) * sine[...]
+    return u * cosine + pltpu.roll(u, HALF, 1) * sine
 
 
 def norm_kernel(order, own, below, above, first, second, gain, normed_out):
@@ -76,7 +76,7 @@
 
 
 def project_kv_kernel(
-    order, normed, w_own, w_other, bias, cosine, sine, kv_out, key_out, value_out, mark_out, joined, sems
+    order, normed, w_own, w_other, bias, cosine, sine, key_out, value_out, mark_out, joined, sems
 ):
     core = order[T]
     copies = []
@@ -90,10 +90,8 @@
         copies[2 * k].wait()
         copies[2 * k + 1].wait()
         total += jnp.dot(normed[k], joined[k].reshape(PIECE, 2 * HD), preferred_element_type=F32)
-    key = turned(total[:, :HD] + bias[:, :HD], cosine, sine).astype(BF16)
+    key = turned(total[:, :HD] + bias[:, :HD], cosine[...], sine[...]).astype(BF16)
     value = (total[:, HD:] + bias[:, HD:]).astype(BF16)
-    kv_out[:, :HD] = key
-    kv_out[:, HD:] = value
     key_out[...] = key
     value_out[...] = value
     mark_out[...] = jnp.zeros_like(mark_out)
@@ -105,7 +103,7 @@
         project_kv_kernel,
         [order, normed, w_own, w_other, bias, cosine, sine],
         "svaavvv",
-        [jax.ShapeDtypeStruct((ROWS, 2 * HD), BF16), one, one, jax.ShapeDtypeStruct((1, ROWS), jnp.int32)],
+        [one, one, jax.ShapeDtypeStruct((1, ROWS), jnp.int32)],
         "project_kv",
         4 * ROWS * D * HD,
         2 * D * (2 * HD + ROWS),
@@ -113,87 +111,78 @@
     )
 
 
-def project_q_kernel(order, normed, w, bias, cosine, sine, q_out, held, acc, sems):
-    parts = 4
-    members = Z * C // parts
-
-    def copies(k):
-        for part in range(parts):
+def attend_kernel(
+    order, index, normed, w, cosine, sine, mine, other, key, value, query_bias,
+    top, bottom, pieces, held, acc, angles, seen, bias, sems, piece_sems, angle_sems, seen_sems,
+):
+    core = order[T]
+    members = Z * C // 2
+    stream = []
+    for k in range(T):
+        stream.append(pltpu.make_async_copy(normed.at[k], pieces.at[k], piece_sems.at[k]))
+        for part in range(2):
             source = w.at[pl.ds(order[k] * Z * C + part * members, members), 1]
-            yield pltpu.make_async_copy(source, held.at[k, pl.ds(part * members, members)], sems.at[k, part])
-
-    for k in range(2):
-        for copy in copies(k):
-            copy.start()
-    for k in range(T):
-        for copy in copies(k):
-            copy.wait()
-        if k + 2 < T:
-            for copy in copies(k + 2):
-                copy.start()
-        part = jnp.dot(normed[k], held[k].reshape(PIECE, QW), preferred_element_type=F32)
-        acc[...] = part if k == 0 else acc[...] + part
-    for head in range(GROUP):
-        span = slice(head * HD, (head + 1) * HD)
-        q_out[:, span] = turned(acc[:, span] + bias[:, span], cosine, sine).astype(BF16)
-
-
-def project_q(order, normed, w, bias, cosine, sine):
-    return local_call(
-        project_q_kernel,
-        [order, normed, w, bias, cosine, sine],
-        "svavvv",
-        jax.ShapeDtypeStruct((ROWS, QW), BF16),
-        "project_q",
-        2 * ROWS * D * QW,
-        2 * D * (QW + ROWS),
-        [pltpu.VMEM((T, Z * C, SHARD, QW), BF16), pltpu.VMEM((ROWS, QW), F32), pltpu.SemaphoreType.DMA((T, 4))],
-        52,
-    )
-
-
-def attend_kernel(index, q, kv, mine, other, out, seen, bias):
-    core = index[1]
-    seen[core, :ROWS] = mine[...]
-    seen[1 - core, :ROWS] = other[...]
-    seen[0, ROWS:] = kv[:, :HD]
-    seen[1, ROWS:] = kv[:, HD:]
+            stream.append(pltpu.make_async_copy(source, held.at[k, pl.ds(part * members, members)], sems.at[k, part]))
+    stream += [pltpu.make_async_copy(ref, angles.at[at], angle_sems.at[at]) for at, ref in enumerate((cosine, sine))]
+    near, far = pl.ds(ROWS, ROWS), pl.ds(0, ROWS)
+    for at, (ref, lane, rows) in enumerate(((mine, core, far), (other, 1 - core, far), (key, 0, near), (value, 1, near))):
+        stream.append(pltpu.make_async_copy(ref, seen.at[lane, rows], seen_sems.at[at]))
+    ahead = 9
+    for copy in stream[:ahead]:
+        copy.start()
     row = lax.broadcasted_iota(jnp.int32, (ROWS, ROWS), 0)
     col = lax.broadcasted_iota(jnp.int32, (ROWS, ROWS), 1)
     bias[:, :ROWS] = jnp.where(jnp.full((ROWS, ROWS), index[0], jnp.int32) > 0, 0.0, -jnp.inf)
     bias[:, ROWS:] = jnp.where(row >= col, 0.0, -jnp.inf)
+    for at, copy in enumerate(stream):
+        copy.wait()
+        if at + ahead < len(stream):
+            stream[at + ahead].start()
+        k = at // 3
+        if at % 3 == 2 and k < T:
+            part = jnp.dot(pieces[k], held[k].reshape(PIECE, QW), preferred_element_type=F32)
+            acc[...] = part if k == 0 else acc[...] + part
     for head in range(GROUP):
         span = slice(head * HD, (head + 1) * HD)
-        scores = lax.dot_general(q[:, span], seen[0], (((1,), (1,)), ((), ())), preferred_element_type=F32)
+        query = turned(acc[:, span] + query_bias[:, span], angles[0], angles[1]).astype(BF16)
+        scores = lax.dot_general(query, seen[0], (((1,), (1,)), ((), ())), preferred_element_type=F32)
         scores = scores + bias[...]
         peak = jnp.max(scores, axis=-1, keepdims=True)
         weights = jnp.exp2((scores - peak) * (HD**-0.5 * math.log2(math.e)))
         total = jnp.sum(weights, axis=-1, keepdims=True)
         mixed = jnp.dot(weights.astype(BF16), seen[1], preferred_element_type=F32)
-        out[:, span] = (mixed / total).astype(BF16)
-
-
-def attend(index, q, kv, mine, other):
+        mixed = (mixed / total).astype(BF16)
+        top[:, span], bottom[:, span] = mixed[: ROWS // 2], mixed[ROWS // 2 :]
+
+
+def attend(order, index, normed, w, cosine, sine, mine, other, key, value, query_bias):
+    half = jax.ShapeDtypeStruct((ROWS // 2, QW), BF16)
     return local_call(
         attend_kernel,
-        [index, q, kv, mine, other],
-        "svvvv",
-        jax.ShapeDtypeStruct((ROWS, QW), BF16),
+        [order, index, normed, w, cosine, sine, mine, other, key, value, query_bias],
+        "ssaaaaaaaav",
+        [half, half],
         "attend",
-        4 * ROWS * 2 * ROWS * QW,
-        4 * ROWS * QW,
-        [pltpu.VMEM((2, 2 * ROWS, HD), BF16), pltpu.VMEM((ROWS, 2 * ROWS), F32)],
+        2 * ROWS * D * QW + 4 * ROWS * 2 * ROWS * QW,
+        2 * D * (QW + ROWS),
+        [
+            pltpu.VMEM((T, ROWS, PIECE), BF16),
+            pltpu.VMEM((T, Z * C, SHARD, QW), BF16),
+            pltpu.VMEM((ROWS, QW), F32),
+            pltpu.VMEM((2, ROWS, HD), F32),
+            pltpu.VMEM((2, 2 * ROWS, HD), BF16),
+            pltpu.VMEM((ROWS, 2 * ROWS), F32),
+            pltpu.SemaphoreType.DMA((T, 2)),
+            pltpu.SemaphoreType.DMA((T,)),
+            pltpu.SemaphoreType.DMA((2,)),
+            pltpu.SemaphoreType.DMA((4,)),
+        ],
+        50,
     )
 
 
 def times(a, w):
     return lax.dot_general(a, w, (((1,), (1,)), ((), ())), preferred_element_type=F32)
-
-
-def halves_kernel(below, above, total, first, second):
-    half = first.shape[0]
-    first[...] = below[:half]
-    second[...] = above[half:]
 
 
 def stack_kernel(first, second, out):
@@ -201,22 +190,35 @@
     out[1] = second[...]
 
 
-def rows_of(w, group):
-    return w[pl.ds(lax.rem(group + 2, X) * Z * C, Z * C)].reshape(PIECE, QW)
-
-
-def out_own_kernel(order, att, w, out):
-    out[...] = times(att[...], rows_of(w, order[0]))
-
-
-def out_next_kernel(order, total, below, above, w, out):
-    some = total[...] + times(below[...], rows_of(w, order[1]))
-    out[...] = some + times(above[...], rows_of(w, order[2]))
-
-
-def out_last_kernel(order, tokens, total, first, second, w, gain, head, resid_out, stats_out):
+def joined(top, bottom):
+    return jnp.concatenate([top[...], bottom[...]], axis=0)
+
+
+def out_own_kernel(order, top, bottom, w, out, *refs):
+    targets, sems = [refs[-2], *refs[:-2]], refs[-1]
+    members = Z * C
+    copies = [
+        pltpu.make_async_copy(w.at[pl.ds(lax.rem(order[at] + 2, X) * members, members), 0], target, sems.at[at])
+        for at, target in enumerate(targets)
+    ]
+    copies[0].start()
+    copies[1].start()
+    copies[0].wait()
+    copies[2].start()
+    copies[3].start()
+    out[...] = times(joined(top, bottom), targets[0][...].reshape(PIECE, QW))
+    for copy in copies[1:]:
+        copy.wait()
+
+
+def out_next_kernel(total, below_top, below_bottom, above_top, above_bottom, w_below, w_above, out):
+    some = total[...] + times(joined(below_top, below_bottom), w_below[...].reshape(PIECE, QW))
+    out[...] = some + times(joined(above_top, above_bottom), w_above[...].reshape(PIECE, QW))
+
+
+def out_last_kernel(tokens, total, top, bottom, w, gain, head, resid_out, stats_out):
     lane = lax.broadcasted_iota(jnp.int32, (ROWS, HD), 1)
-    resid = tokens[...].astype(F32) + total[...] + times(jnp.concatenate([first[...], second[...]], axis=0), rows_of(w, order[T - 1]))
+    resid = tokens[...].astype(F32) + total[...] + times(joined(top, bottom), w[...].reshape(PIECE, QW))
     resid_out[...] = resid.astype(BF16)
     squares = jnp.sum(resid * resid, axis=-1, keepdims=True)
     products = jnp.sum(resid * gain[...] * head[...], axis=-1, keepdims=True)
@@ -370,34 +372,7 @@
     cosine = jnp.concatenate([cosine, cosine], axis=1)
     sine = jnp.concatenate([-sine, sine], axis=1)
     kv_bias = jnp.concatenate([key_bias, value_bias])[None, :]
-    kv, key, value, mark = project_kv(order, normed, kv_own, kv_other, kv_bias, cosine, sine)
-    query = project_q(order, normed, weights, query_bias[None, :], cosine, sine)
-    held, sent = broadcast_anchor(key, value)
-    att = attend(jnp.stack([index, index % C]).astype(jnp.int32), query, kv, held, sent)
-
-    weights, att = lax.optimization_barrier((weights, att))
-    w_o = weights[:, 0]
-    below, above = shift_tp(att, 1), shift_tp(att, -1)
-    wide = jax.ShapeDtypeStruct((ROWS, PIECE), F32)
-    flops, nbytes = 2 * ROWS * QW * PIECE, 6 * MIB
-    total = local_call(out_own_kernel, [order, att, w_o], "svv", wide, "out_own", flops, nbytes)
-    pair = jax.ShapeDtypeStruct((half, QW), BF16)
-    first, second = local_call(
-        halves_kernel, [below, above, total], "vva", [pair, pair], "halves", 0, 4 * half * QW
-    )
-    first, second = shift_tp(first, 1), shift_tp(second, -1)
-    total = local_call(out_next_kernel, [order, total, below, above, w_o], "svvvv", wide, "out_next", 2 * flops, nbytes)
-    residual_stream, stats = local_call(
-        out_last_kernel,
-        [order, tokens, total, first, second, w_o, final_gain[None, :], critic_head[None, :]],
-        "svvvvvvv",
-        [jax.ShapeDtypeStruct((ROWS, PIECE), BF16), jax.ShapeDtypeStruct((T, 8, ROWS), F32)],
-        "out_last",
-        flops,
-        nbytes,
-    )
-    stats = lax.all_to_all(stats, "tp", 0, 0)
-
+    key, value, mark = project_kv(order, normed, kv_own, kv_other, kv_bias, cosine, sine)
     turn_ends, episode_done = turn_ends + mark[0], episode_done + mark[0]
     ends = jnp.maximum(turn_ends, episode_done)
     discount = jnp.where(ends > 0, GAMMA, 1.0).astype(F32) * (1 - episode_done).astype(F32)
@@ -414,6 +389,49 @@
     tail_powers = (decay_count[ROWS] - decay_count[:ROWS]).astype(F32)
     tail = jnp.where(done_count[ROWS] == done_count[:ROWS], jnp.power(rate, tail_powers), 0.0)[None, :]
     edge = (matrix[:, ROWS - 1] * discount[ROWS - 1])[None, :]
+
+    held, sent = broadcast_anchor(key, value)
+    sent, tail, edge = lax.optimization_barrier((sent, tail, edge))
+    index_ref = index.astype(jnp.int32)[None]
+    top, bottom = attend(order, index_ref, normed, weights, cosine, sine, held, sent, key, value, query_bias[None, :])
+
+    below_top, above_bottom = shift_tp(top, 1), shift_tp(bottom, -1)
+    below_bottom, above_top = shift_tp(bottom, 1), shift_tp(top, -1)
+    flops = 2 * ROWS * QW * PIECE
+    wide = jax.ShapeDtypeStruct((ROWS, PIECE), F32)
+    group = jax.ShapeDtypeStruct((Z * C, SHARD, QW), BF16)
+    total, w_below, w_above, w_far = local_call(
+        out_own_kernel,
+        [order, top, bottom, weights],
+        "svva",
+        [wide, group, group, group],
+        "out_own",
+        flops,
+        8 * MIB,
+        [pltpu.VMEM(group.shape, BF16), pltpu.SemaphoreType.DMA((T,))],
+        42,
+    )
+    total, below_top = lax.optimization_barrier((total, below_top))
+    far_top, far_bottom = shift_tp(below_top, 1), shift_tp(above_bottom, -1)
+    total = local_call(
+        out_next_kernel,
+        [total, below_top, below_bottom, above_top, above_bottom, w_below, w_above],
+        "vvvvvvv",
+        wide,
+        "out_next",
+        2 * flops,
+        6 * MIB,
+    )
+    residual_stream, stats = local_call(
+        out_last_kernel,
+        [tokens, total, far_top, far_bottom, w_far, final_gain[None, :], critic_head[None, :]],
+        "vvvvvvv",
+        [jax.ShapeDtypeStruct((ROWS, PIECE), BF16), jax.ShapeDtypeStruct((T, 8, ROWS), F32)],
+        "out_last",
+        flops,
+        6 * MIB,
+    )
+    stats = lax.all_to_all(stats, "tp", 0, 0)
 
     n = lax.axis_size("ctx")
     line = jax.ShapeDtypeStruct((1, ROWS), F32)

time: 187 us -> 182 us (0.973)
  local copies, waits for them, and re-layouts: 15.4 us -> 7.16 us
  starting transfers between devices: 53.3 us -> 56 us
    unnamed x36, local copies, waits for them, and re-layouts: 7.39 us -> 2.65 us
    squeeze x1 -> x0, local copies, waits for them, and re-layouts: 3.43 us -> none  [on_device(): w_o = weights[:, 0]]
    ppermute x8 -> x10, waiting for transfers between devices: 15 us -> 12.3 us  [shift_tp(): lax.ppermute(block, 'tp', [(i, (i + distance) % T) for i in range(T)])]
    ppermute x8 -> x10, starting transfers between devices: 15 us -> 17.6 us  [shift_tp(): lax.ppermute(block, 'tp', [(i, (i + distance) % T) for i in range(T)])]
    pallas_call x11 -> x9, Pallas kernels: 26.7 us -> 28.3 us  [local_call(): pl.pallas_call(kernel, in_specs=[pl.BlockSpec(memory_space=spaces[p]) for...]
  transfers between devices with their start and end apart: 23 -> 25, of which waited for: 16 -> 17; matrix products, arithmetic and copies ran while one was open for 7% -> 6% of each run, Pallas kernels for 10% -> 7%
where the time goes in v5:
time: 182 us; the launch traced here: 181 us
  starting transfers between devices  56 us (31%)
  waiting for transfers between devices  47.7 us (26%)
  Pallas kernels  28.3 us (16%)
  blocking collectives  20.6 us (11%)
  between operations  15.2 us (8%)
  local copies, waits for them, and re-layouts  7.16 us (4%)
  other arithmetic  6.4 us (4%)
    pallas_call x9, Pallas kernels, local_call(): pl.pallas_call(kernel, in_specs=[pl.BlockSpec(memory_space=spaces[p]) for...  28.3 us
    all_to_all x1, blocking collectives, gather_by_all_to_all(): return lax.all_to_all(everywhere, axis, 0, 0, axis_index_groups=groups)  20.6 us
    ppermute x10, starting transfers between devices, shift_tp(): lax.ppermute(block, 'tp', [(i, (i + distance) % T) for i in range(T)])  17.6 us
    ppermute x7, starting transfers between devices, broadcast_anchor(): got = lax.ppermute(block, 'ctx', pairs)  13.3 us
    ppermute x10, waiting for transfers between devices, shift_tp(): lax.ppermute(block, 'tp', [(i, (i + distance) % T) for i in range(T)])  12.3 us
    all_gather x1, waiting for transfers between devices, on_device(): weights = lax.all_gather(both, 'ctx')  9.21 us
    all_to_all x1, waiting for transfers between devices, on_device(): records = lax.all_to_all(records, 'ctx', 0, 0, tiled=True)  8.69 us
    all_to_all x1, starting transfers between devices, on_device(): records = lax.all_to_all(records, 'ctx', 0, 0, tiled=True)  7.95 us
  transfers between devices with their start and end apart: 25, of which 17 were waited for; matrix products, arithmetic and copies ran while one was open for 6% of the time, Pallas kernels for 7%

profile of v5, /device:TPU:1, one launch (start us, length us, event | category | flops | bytes accessed | tf_op | source)
XLA Modules:
  0.0 181.3 jit_solution(9834811789068248049)
XLA Ops:
  7.2 3.7 %collective-permute-start.4 = (bf16[80,640]{1,0:T(8,128)(2,1)}, bf16[80,640]{1,0:T(8,128)(2,1)S(1)}, u32[]{:S(2)}, u32[]{:S(2)}) collective-permute-start(bf16[80,640]{1,0:T(8,128)(2,1)} %bitcast.34), channel_id=1, source_target_pairs={{0,128},{1,192},{2,0},{3,64},{4,132},{5,196},{6,4},{7,68},{8,136},... | collective-permute-start | bytes 307208 | tf_op jit(solution)/shard_map/ppermute | solution.py:352
  10.9 2.4 %collective-permute-done.4.first = bf16[80,640]{1,0:T(8,128)(2,1)S(1)} collective-permute-done((bf16[80,640]{1,0:T(8,128)(2,1)}, bf16[80,640]{1,0:T(8,128)(2,1)S(1)}, u32[]{:S(2)}, u32[]{:S(2)}) %collective-permute-start.4) | collective-permute-done | bytes 102432 | tf_op jit(solution)/shard_map/ppermute | solution.py:352
  14.9 3.1 %collective-permute-start = (bf16[384,1280]{1,0:T(8,128)(2,1)}, bf16[384,1280]{1,0:T(8,128)(2,1)S(1)}, u32[]{:S(2)}, u32[]{:S(2)}) collective-permute-start(bf16[384,1280]{1,0:T(8,128)(2,1)} %tokens.1), channel_id=1, source_target_pairs={{0,1},{1,2},{2,3},{3,0},{4,5},{5,6},{6,7},{7,4},{8,9},{9,10},{10,1... | collective-permute-start | bytes 2949128 | tf_op jit(solution)/shard_map/ppermute | solution.py:37
  18.0 3.5 %collective-permute-start.1 = (bf16[384,1280]{1,0:T(8,128)(2,1)}, bf16[384,1280]{1,0:T(8,128)(2,1)}, u32[]{:S(2)}, u32[]{:S(2)}) collective-permute-start(bf16[384,1280]{1,0:T(8,128)(2,1)} %tokens.1), channel_id=1, source_target_pairs={{0,3},{1,0},{2,1},{3,2},{4,7},{5,4},{6,5},{7,6},{8,11},{9,8},{10,9... | collective-permute-start | bytes 2949128 | tf_op jit(solution)/shard_map/ppermute | solution.py:37
  22.3 20.6 %all_to_all.26 = bf16[8,80,256]{2,1,0:T(8,128)(2,1)S(1)} all-to-all(bf16[8,80,256]{2,1,0:T(8,128)(2,1)S(1)} %broadcast_in_dim.63), channel_id=1, replica_groups={{0,8,16,24,32,40,48,56},{4,12,20,28,36,44,52,60},{64,72,80,88,96,104,11..., dimensions={0} | all-to-all | bytes 655360 | tf_op jit(solution)/shard_map/all_to_all | solution.py:281
  44.6 3.5 %all-to-all-start.1 = ((bf16[4,8,80,256]{3,2,1,0:T(8,128)(2,1)}), bf16[4,8,80,256]{3,2,1,0:T(8,128)(2,1)S(1)}, u32[]{:S(2)}, u32[]{:S(2)}) async-start(bf16[4,8,80,256]{3,2,1,0:T(8,128)(2,1)} %broadcast_in_dim.64), calls=%async_computation.1 | async-start | bytes 2621440 | tf_op jit(solution)/shard_map/all_to_all | solution.py:281
  50.0 2.2 %collective-permute-start.3 = (bf16[192,1280]{1,0:T(8,128)(2,1)S(1)}, bf16[192,1280]{1,0:T(8,128)(2,1)S(1)}, u32[]{:S(2)}, u32[]{:S(2)}) collective-permute-start(bf16[192,1280]{1,0:T(8,128)(2,1)S(1)} %slice.43), channel_id=1, source_target_pairs={{0,3},{1,0},{2,1},{3,2},{4,7},{5,4},{6,5},{7,6},{8,11},{9,8},{10,9... | collective-permute-start | bytes 1474568 | tf_op jit(solution)/shard_map/ppermute | solution.py:37
  52.1 6.6 %collective-permute-done.2.first = bf16[192,1280]{1,0:T(8,128)(2,1)S(1)} collective-permute-done((bf16[192,1280]{1,0:T(8,128)(2,1)S(1)}, bf16[192,1280]{1,0:T(8,128)(2,1)S(1)}, u32[]{:S(2)}, u32[]{:S(2)}) %collective-permute-start.2) | collective-permute-done | bytes 491552 | tf_op jit(solution)/shard_map/ppermute | solution.py:37
  60.6 1.7 all-to-all-done.1.w_own
  62.3 4.7 %collective-permute-start.5 = (bf16[4,8,80,256]{3,2,1,0:T(8,128)(2,1)S(1)}, bf16[4,8,80,256]{3,2,1,0:T(8,128)(2,1)}, u32[]{:S(2)}, u32[]{:S(2)}) collective-permute-start(bf16[4,8,80,256]{3,2,1,0:T(8,128)(2,1)S(1)} %all-to-all-done.1.w_own), channel_id=1, source_target_pairs={{0,4},{4,0},{8,12},{12,8},{16,20},{20,16},{24,28},{28,24},{32,36},... | collective-permute-start | bytes 3932168 | tf_op jit(solution)/shard_map/ppermute | solution.py:289
  68.2 2.9 %norm.1.normed = bf16[4,384,1280]{2,1,0:T(8,128)(2,1)S(1)} custom-call(s32[5]{0:T(128)S(1)} %stack.24.order, bf16[384,1280]{1,0:T(8,128)(2,1)S(1)} %copy-done.1, bf16[384,1280]{1,0:T(8,128)(2,1)S(1)} %collective-permute-done.below, bf16[384,1280]{1,0:T(8,128)(2,1)} %collective-permute-done.1.above, bf16[192,1280]{1,0:T(8,128)(2,1)S(1)} %copy-done.5, ...), custom_call_target="tpu_custom_call" | custom-call | flops 11796480 | bytes 7864320 | tf_op jit(solution)/shard_map/norm/pallas_call | solution.py:42
  71.3 4.6 %project_kv.1 = (bf16[384,128]{1,0:T(8,128)(2,1)S(1)}, bf16[384,128]{1,0:T(8,128)(2,1)S(1)}, s32[1,384]{1,0:T(1,128)S(1)}) custom-call(s32[5]{0:T(128)S(1)} %stack.24.order, bf16[4,384,1280]{2,1,0:T(8,128)(2,1)S(1)} %norm.1.normed, bf16[4,8,80,256]{3,2,1,0:T(8,128)(2,1)S(1)} %all-to-all-done.1.w_own, bf16[4,8,80,256]{3,2,1,0:T(8,128)(2,1)} %collective-permute-done.5.w_other, ...), custom_call_target="tpu_custom_call" | custom-call | flops 1006632960 | bytes 6553600 | tf_op jit(solution)/shard_map/project_kv/pallas_call | solution.py:42
  80.0 2.8 %collective-permute-start.7 = (bf16[384,128]{1,0:T(8,128)(2,1)S(1)}, bf16[384,128]{1,0:T(8,128)(2,1)S(1)}, u32[]{:S(2)}, u32[]{:S(2)}) collective-permute-start(bf16[384,128]{1,0:T(8,128)(2,1)S(1)} %broadcast_select_fusion), channel_id=1, source_target_pairs={{0,64},{4,20},{1,65},{5,21},{2,66},{6,22},{3,67},{7,23}} | collective-permute-start | bytes 294920 | tf_op jit(solution)/shard_map/ppermute | solution.py:317
  82.8 3.7 %collective-permute-start.8 = (bf16[384,128]{1,0:T(8,128)(2,1)S(1)}, bf16[384,128]{1,0:T(8,128)(2,1)S(1)}, u32[]{:S(2)}, u32[]{:S(2)}) collective-permute-start(bf16[384,128]{1,0:T(8,128)(2,1)S(1)} %broadcast_select_fusion), channel_id=1, source_target_pairs={{0,192},{4,52},{1,193},{5,53},{2,194},{6,54},{3,195},{7,55}} | collective-permute-start | bytes 294920 | tf_op jit(solution)/shard_map/ppermute | solution.py:317
  86.6 1.6 collective-permute-start.9
  89.2 1.8 collective-permute-done.9
  97.2 1.9 %collective-permute-done.12 = bf16[384,128]{1,0:T(8,128)(2,1)S(1)} collective-permute-done((bf16[384,128]{1,0:T(8,128)(2,1)S(1)}, bf16[384,128]{1,0:T(8,128)(2,1)S(1)}, u32[]{:S(2)}, u32[]{:S(2)}) %collective-permute-start.12) | collective-permute-done | bytes 98336 | tf_op jit(solution)/shard_map/ppermute | solution.py:317
  102.3 2.3 %collective-permute-done.13 = bf16[384,128]{1,0:T(8,128)(2,1)S(1)} collective-permute-done((bf16[384,128]{1,0:T(8,128)(2,1)S(1)}, bf16[384,128]{1,0:T(8,128)(2,1)S(1)}, u32[]{:S(2)}, u32[]{:S(2)}) %collective-permute-start.13) | collective-permute-done | bytes 98336 | tf_op jit(solution)/shard_map/ppermute | solution.py:317
  106.2 9.2 %all-gather.3.cloned.1.call-done = bf16[128,80,640]{2,1,0:T(8,128)(2,1)} async-done(((bf16[2,80,640]{2,1,0:T(8,128)(2,1)}), bf16[128,80,640]{2,1,0:T(8,128)(2,1)}) %all-gather.3.cloned.1.call-update) | async-done | bytes 13107216 | tf_op jit(solution)/shard_map/all_gather | solution.py:356
  115.4 10.7 %attend.1 = (bf16[192,640]{1,0:T(8,128)(2,1)S(1)}, bf16[192,640]{1,0:T(8,128)(2,1)S(1)}) custom-call(s32[5]{0:T(128)S(1)} %stack.24.order, s32[1]{0:T(128)} %bitcast.5.index, bf16[4,384,1280]{2,1,0:T(8,128)(2,1)} %copy-done, bf16[64,2,80,640]{3,2,1,0:T(8,128)(2,1)} %bitcast.30, f32[384,128]{1,0:T(8,128)S(1)} %get-tuple-element.60.cosine, ...), custom_call_target="tpu_custom_call" | custom-call | flops 3271557120 | bytes 10485760 | tf_op jit(solution)/shard_map/attend/pallas_call | solution.py:42
  127.1 1.7 collective-permute-start.18
  128.9 2.7 %collective-permute-start.17 = (bf16[192,640]{1,0:T(8,128)(2,1)S(1)}, bf16[192,640]{1,0:T(8,128)(2,1)S(1)}, u32[]{:S(2)}, u32[]{:S(2)}) collective-permute-start(bf16[192,640]{1,0:T(8,128)(2,1)S(1)} %get-tuple-element.38.top), channel_id=1, source_target_pairs={{0,3},{1,0},{2,1},{3,2},{4,7},{5,4},{6,5},{7,6},{8,11},{9,8},{10,9... | collective-permute-start | bytes 737288 | tf_op jit(solution)/shard_map/ppermute | solution.py:37
  131.6 4.1 %out_own.1 = (f32[384,1280]{1,0:T(8,128)S(1)}, bf16[16,80,640]{2,1,0:T(8,128)(2,1)S(1)}, bf16[16,80,640]{2,1,0:T(8,128)(2,1)S(1)}, bf16[16,80,640]{2,1,0:T(8,128)(2,1)S(1)}) custom-call(s32[5]{0:T(128)S(1)} %stack.24.order, bf16[192,640]{1,0:T(8,128)(2,1)S(1)} %get-tuple-element.38.top, bf16[192,640]{1,0:T(8,128)(2,1)S(1)} %get-tuple-element.39.bottom, ...), custom_call_target="tpu_custom_call" | custom-call | flops 629145600 | bytes 8388608 | tf_op jit(solution)/shard_map/out_own/pallas_call | solution.py:42
  135.8 2.7 %collective-permute-start.20 = (bf16[192,640]{1,0:T(8,128)(2,1)S(1)}, bf16[192,640]{1,0:T(8,128)(2,1)S(1)}, u32[]{:S(2)}, u32[]{:S(2)}) collective-permute-start(bf16[192,640]{1,0:T(8,128)(2,1)S(1)} %collective-permute-done.18.above_bottom), channel_id=1, source_target_pairs={{0,3},{1,0},{2,1},{3,2},{4,7},{5,4},{6,5},{7,6},{8,11},{9,8},{10,9... | collective-permute-start | bytes 737288 | tf_op jit(solution)/shard_map/ppermute | solution.py:37
  138.4 1.6 collective-permute-done.16.below_bottom
  140.0 1.7 out_next.1.total
  141.7 3.3 %collective-permute-done.19.top = bf16[192,640]{1,0:T(8,128)(2,1)S(1)} collective-permute-done((bf16[192,640]{1,0:T(8,128)(2,1)S(1)}, bf16[192,640]{1,0:T(8,128)(2,1)S(1)}, u32[]{:S(2)}, u32[]{:S(2)}) %collective-permute-start.19) | collective-permute-done | bytes 245792 | tf_op jit(solution)/shard_map/ppermute | solution.py:37
  145.0 2.0 %out_last.1 = (bf16[384,1280]{1,0:T(8,128)(2,1)}, f32[4,8,384]{2,1,0:T(8,128)}) custom-call(bf16[384,1280]{1,0:T(8,128)(2,1)S(1)} %copy-done.1, f32[384,1280]{1,0:T(8,128)S(1)} %out_next.1.total, bf16[192,640]{1,0:T(8,128)(2,1)S(1)} %collective-permute-done.19.top, bf16[192,640]{1,0:T(8,128)(2,1)S(1)} %collective-permute-done.20.bottom, ...), custom_call_target="tpu_custom_call" | custom-call | flops 629145600 | bytes 6291456 | tf_op jit(solution)/shard_map/out_last/pallas_call | solution.py:42
  147.0 3.7 %all-to-all-start.2 = ((f32[4,8,384]{2,1,0:T(8,128)}), f32[4,8,384]{2,1,0:T(8,128)S(1)}, u32[]{:S(2)}, u32[]{:S(2)}) async-start(f32[4,8,384]{2,1,0:T(8,128)} %get-tuple-element.47), calls=%async_computation.2 | async-start | bytes 98304 | tf_op jit(solution)/shard_map/all_to_all | solution.py:434
  151.4 3.7 %all-to-all-done.2.stats = f32[4,8,384]{2,1,0:T(8,128)S(1)} async-done(((f32[4,8,384]{2,1,0:T(8,128)}), f32[4,8,384]{2,1,0:T(8,128)S(1)}, u32[]{:S(2)}, u32[]{:S(2)}) %all-to-all-start.2) | async-done | bytes 49184 | tf_op jit(solution)/shard_map/all_to_all | solution.py:434
  156.4 8.0 %all-to-all-start.3 = ((f32[64,1,128]{2,1,0:T(1,128)}), f32[64,1,128]{2,1,0:T(1,128)S(1)}, u32[]{:S(2)}, u32[]{:S(2)}) async-start(f32[64,1,128]{2,1,0:T(1,128)} %bitcast.18), calls=%async_computation.3 | async-start | bytes 65536 | tf_op jit(solution)/shard_map/all_to_all | solution.py:447
  165.0 8.7 %all-to-all-done.3 = f32[64,1,128]{2,1,0:T(1,128)S(1)} async-done(((f32[64,1,128]{2,1,0:T(1,128)}), f32[64,1,128]{2,1,0:T(1,128)S(1)}, u32[]{:S(2)}, u32[]{:S(2)}) %all-to-all-start.3) | async-done | bytes 32800 | tf_op jit(solution)/shard_map/all_to_all | solution.py:447
  (110 shorter events, 28.8 us)
Async XLA Ops:
  7.2 108.2 %all-gather.3.cloned.1.call-start = ((), (), s32[]{:S(2)}) async-start(), calls=%async_computation.4 | async-start | bytes 13312000 | tf_op jit(solution)/shard_map/all_gather | solution.py:356
  7.2 6.1 %collective-permute-start.4 = (bf16[80,640]{1,0:T(8,128)(2,1)}, bf16[80,640]{1,0:T(8,128)(2,1)S(1)}, u32[]{:S(2)}, u32[]{:S(2)}) collective-permute-start(bf16[80,640]{1,0:T(8,128)(2,1)} %bitcast.34), channel_id=1, source_target_pairs={{0,128},{1,192},{2,0},{3,64},{4,132},{5,196},{6,4},{7,68},{8,136},... | collective-permute-start | bytes 307208 | tf_op jit(solution)/shard_map/ppermute | solution.py:352
  14.9 28.5 %collective-permute-start = (bf16[384,1280]{1,0:T(8,128)(2,1)}, bf16[384,1280]{1,0:T(8,128)(2,1)S(1)}, u32[]{:S(2)}, u32[]{:S(2)}) collective-permute-start(bf16[384,1280]{1,0:T(8,128)(2,1)} %tokens.1), channel_id=1, source_target_pairs={{0,1},{1,2},{2,3},{3,0},{4,5},{5,6},{6,7},{7,4},{8,9},{9,10},{10,1... | collective-permute-start | bytes 2949128 | tf_op jit(solution)/shard_map/ppermute | solution.py:37
  18.0 25.4 %collective-permute-start.1 = (bf16[384,1280]{1,0:T(8,128)(2,1)}, bf16[384,1280]{1,0:T(8,128)(2,1)}, u32[]{:S(2)}, u32[]{:S(2)}) collective-permute-start(bf16[384,1280]{1,0:T(8,128)(2,1)} %tokens.1), channel_id=1, source_target_pairs={{0,3},{1,0},{2,1},{3,2},{4,7},{5,4},{6,5},{7,6},{8,11},{9,8},{10,9... | collective-permute-start | bytes 2949128 | tf_op jit(solution)/shard_map/ppermute | solution.py:37
  44.6 17.7 %all-to-all-start.1 = ((bf16[4,8,80,256]{3,2,1,0:T(8,128)(2,1)}), bf16[4,8,80,256]{3,2,1,0:T(8,128)(2,1)S(1)}, u32[]{:S(2)}, u32[]{:S(2)}) async-start(bf16[4,8,80,256]{3,2,1,0:T(8,128)(2,1)} %broadcast_in_dim.64), calls=%async_computation.1 | async-start | bytes 2621440 | tf_op jit(solution)/shard_map/all_to_all | solution.py:281
  48.1 18.8 %copy-start.14 = (f32[640]{0:T(1024)S(1)}, f32[640]{0:T(1024)}, u32[]{:S(2)}) copy-start(f32[640]{0:T(1024)} %param.20) | copy-start | bytes 7684
  48.2 18.9 %copy-start.16 = (f32[128]{0:T(128)S(1)}, f32[128]{0:T(128)}, u32[]{:S(2)}) copy-start(f32[128]{0:T(128)} %param.22) | copy-start | bytes 1540
  48.2 18.9 %copy-start.17 = (f32[128]{0:T(128)S(1)}, f32[128]{0:T(128)}, u32[]{:S(2)}) copy-start(f32[128]{0:T(128)} %param.21) | copy-start | bytes 1540
  48.2 19.9 %copy-start.1 = (bf16[384,1280]{1,0:T(8,128)(2,1)S(1)}, bf16[384,1280]{1,0:T(8,128)(2,1)}, u32[]{:S(2)}) copy-start(bf16[384,1280]{1,0:T(8,128)(2,1)} %tokens.1) | copy-start | bytes 2949124
  48.2 19.9 %copy-start.9 = (f32[5120]{0:T(1024)S(1)}, f32[5120]{0:T(1024)}, u32[]{:S(2)}) copy-start(f32[5120]{0:T(1024)} %param.16) | copy-start | bytes 61444
  48.2 10.5 %collective-permute-start.2 = (bf16[192,1280]{1,0:T(8,128)(2,1)S(1)}, bf16[192,1280]{1,0:T(8,128)(2,1)S(1)}, u32[]{:S(2)}, u32[]{:S(2)}) collective-permute-start(bf16[192,1280]{1,0:T(8,128)(2,1)S(1)} %slice.42), channel_id=1, source_target_pairs={{0,1},{1,2},{2,3},{3,0},{4,5},{5,6},{6,7},{7,4},{8,9},{9,10},{10,1... | collective-permute-start | bytes 1474568 | tf_op jit(solution)/shard_map/ppermute | solution.py:37
  50.0 9.8 %collective-permute-start.3 = (bf16[192,1280]{1,0:T(8,128)(2,1)S(1)}, bf16[192,1280]{1,0:T(8,128)(2,1)S(1)}, u32[]{:S(2)}, u32[]{:S(2)}) collective-permute-start(bf16[192,1280]{1,0:T(8,128)(2,1)S(1)} %slice.43), channel_id=1, source_target_pairs={{0,3},{1,0},{2,1},{3,2},{4,7},{5,4},{6,5},{7,6},{8,11},{9,8},{10,9... | collective-permute-start | bytes 1474568 | tf_op jit(solution)/shard_map/ppermute | solution.py:37
  62.3 8.9 %collective-permute-start.5 = (bf16[4,8,80,256]{3,2,1,0:T(8,128)(2,1)S(1)}, bf16[4,8,80,256]{3,2,1,0:T(8,128)(2,1)}, u32[]{:S(2)}, u32[]{:S(2)}) collective-permute-start(bf16[4,8,80,256]{3,2,1,0:T(8,128)(2,1)S(1)} %all-to-all-done.1.w_own), channel_id=1, source_target_pairs={{0,4},{4,0},{8,12},{12,8},{16,20},{20,16},{24,28},{28,24},{32,36},... | collective-permute-start | bytes 3932168 | tf_op jit(solution)/shard_map/ppermute | solution.py:289
  71.2 23.7 %copy-start.15 = (s32[384]{0:T(512)S(1)}, s32[384]{0:T(512)}, u32[]{:S(2)}) copy-start(s32[384]{0:T(512)} %param.27) | copy-start | bytes 4612
  75.9 39.5 %copy-start.3 = (f32[384,128]{1,0:T(8,128)S(1)}, f32[384,128]{1,0:T(8,128)}, u32[]{:S(2)}) copy-start(f32[384,128]{1,0:T(8,128)} %copy-done.2) | copy-start | bytes 589828
  76.8 3.2 %collective-permute-start.6 = (bf16[384,128]{1,0:T(8,128)(2,1)S(1)}, bf16[384,128]{1,0:T(8,128)(2,1)S(1)}, u32[]{:S(2)}, u32[]{:S(2)}) collective-permute-start(bf16[384,128]{1,0:T(8,128)(2,1)S(1)} %get-tuple-element.35.value), channel_id=1, source_target_pairs={{0,4},{1,5},{2,6},{3,7}} | collective-permute-start | bytes 294920 | tf_op jit(solution)/shard_map/ppermute | solution.py:301
  80.0 8.4 %collective-permute-start.7 = (bf16[384,128]{1,0:T(8,128)(2,1)S(1)}, bf16[384,128]{1,0:T(8,128)(2,1)S(1)}, u32[]{:S(2)}, u32[]{:S(2)}) collective-permute-start(bf16[384,128]{1,0:T(8,128)(2,1)S(1)} %broadcast_select_fusion), channel_id=1, source_target_pairs={{0,64},{4,20},{1,65},{5,21},{2,66},{6,22},{3,67},{7,23}} | collective-permute-start | bytes 294920 | tf_op jit(solution)/shard_map/ppermute | solution.py:317
  82.8 6.4 %collective-permute-start.8 = (bf16[384,128]{1,0:T(8,128)(2,1)S(1)}, bf16[384,128]{1,0:T(8,128)(2,1)S(1)}, u32[]{:S(2)}, u32[]{:S(2)}) collective-permute-start(bf16[384,128]{1,0:T(8,128)(2,1)S(1)} %broadcast_select_fusion), channel_id=1, source_target_pairs={{0,192},{4,52},{1,193},{5,53},{2,194},{6,54},{3,195},{7,55}} | collective-permute-start | bytes 294920 | tf_op jit(solution)/shard_map/ppermute | solution.py:317
  86.6 4.4 %collective-permute-start.9 = (bf16[384,128]{1,0:T(8,128)(2,1)S(1)}, bf16[384,128]{1,0:T(8,128)(2,1)S(1)}, u32[]{:S(2)}, u32[]{:S(2)}) collective-permute-start(bf16[384,128]{1,0:T(8,128)(2,1)S(1)} %broadcast_select_fusion), channel_id=1, source_target_pairs={{0,128},{4,36},{1,129},{5,37},{2,130},{6,38},{3,131},{7,39}} | collective-permute-start | bytes 294920 | tf_op jit(solution)/shard_map/ppermute | solution.py:317
  91.0 5.1 %collective-permute-start.10 = (bf16[384,128]{1,0:T(8,128)(2,1)S(1)}, bf16[384,128]{1,0:T(8,128)(2,1)S(1)}, u32[]{:S(2)}, u32[]{:S(2)}) collective-permute-start(bf16[384,128]{1,0:T(8,128)(2,1)S(1)} %add_select_fusion.1), channel_id=1, source_target_pairs={{0,16},{64,80},{192,208},{128,144},{4,68},{20,84},{52,116},{36,100... | collective-permute-start | bytes 294920 | tf_op jit(solution)/shard_map/ppermute | solution.py:317
  92.3 4.9 %collective-permute-start.11 = (bf16[384,128]{1,0:T(8,128)(2,1)S(1)}, bf16[384,128]{1,0:T(8,128)(2,1)S(1)}, u32[]{:S(2)}, u32[]{:S(2)}) collective-permute-start(bf16[384,128]{1,0:T(8,128)(2,1)S(1)} %add_select_fusion.1), channel_id=1, source_target_pairs={{0,48},{64,112},{192,240},{128,176},{4,196},{20,212},{52,244},{36,... | collective-permute-start | bytes 294920 | tf_op jit(solution)/shard_map/ppermute | solution.py:317
  93.6 5.5 %collective-permute-start.12 = (bf16[384,128]{1,0:T(8,128)(2,1)S(1)}, bf16[384,128]{1,0:T(8,128)(2,1)S(1)}, u32[]{:S(2)}, u32[]{:S(2)}) collective-permute-start(bf16[384,128]{1,0:T(8,128)(2,1)S(1)} %add_select_fusion.1), channel_id=1, source_target_pairs={{0,32},{64,96},{192,224},{128,160},{4,132},{20,148},{52,180},{36,1... | collective-permute-start | bytes 294920 | tf_op jit(solution)/shard_map/ppermute | solution.py:317
  99.1 5.5 %collective-permute-start.13 = (bf16[384,128]{1,0:T(8,128)(2,1)S(1)}, bf16[384,128]{1,0:T(8,128)(2,1)S(1)}, u32[]{:S(2)}, u32[]{:S(2)}) collective-permute-start(bf16[384,128]{1,0:T(8,128)(2,1)S(1)} %add_select_fusion), channel_id=1, source_target_pairs={{0,8},{64,72},{192,200},{128,136},{16,24},{80,88},{208,216},{144,1... | collective-permute-start | bytes 294920 | tf_op jit(solution)/shard_map/ppermute | solution.py:317
  104.6 1.6 collective-permute-start.14
  126.1 9.5 %collective-permute-start.15 = (bf16[192,640]{1,0:T(8,128)(2,1)S(1)}, bf16[192,640]{1,0:T(8,128)(2,1)S(1)}, u32[]{:S(2)}, u32[]{:S(2)}) collective-permute-start(bf16[192,640]{1,0:T(8,128)(2,1)S(1)} %get-tuple-element.38.top), channel_id=1, source_target_pairs={{0,1},{1,2},{2,3},{3,0},{4,5},{5,6},{6,7},{7,4},{8,9},{9,10},{10,1... | collective-permute-start | bytes 737288 | tf_op jit(solution)/shard_map/ppermute | solution.py:37
  127.1 8.6 %collective-permute-start.18 = (bf16[192,640]{1,0:T(8,128)(2,1)S(1)}, bf16[192,640]{1,0:T(8,128)(2,1)S(1)}, u32[]{:S(2)}, u32[]{:S(2)}) collective-permute-start(bf16[192,640]{1,0:T(8,128)(2,1)S(1)} %get-tuple-element.39.bottom), channel_id=1, source_target_pairs={{0,3},{1,0},{2,1},{3,2},{4,7},{5,4},{6,5},{7,6},{8,11},{9,8},{10,9... | collective-permute-start | bytes 737288 | tf_op jit(solution)/shard_map/ppermute | solution.py:37
  128.9 11.1 %collective-permute-start.16 = (bf16[192,640]{1,0:T(8,128)(2,1)S(1)}, bf16[192,640]{1,0:T(8,128)(2,1)S(1)}, u32[]{:S(2)}, u32[]{:S(2)}) collective-permute-start(bf16[192,640]{1,0:T(8,128)(2,1)S(1)} %get-tuple-element.39.bottom), channel_id=1, source_target_pairs={{0,1},{1,2},{2,3},{3,0},{4,5},{5,6},{6,7},{7,4},{8,9},{9,10},{10,1... | collective-permute-start | bytes 737288 | tf_op jit(solution)/shard_map/ppermute | solution.py:37
  128.9 11.1 %collective-permute-start.17 = (bf16[192,640]{1,0:T(8,128)(2,1)S(1)}, bf16[192,640]{1,0:T(8,128)(2,1)S(1)}, u32[]{:S(2)}, u32[]{:S(2)}) collective-permute-start(bf16[192,640]{1,0:T(8,128)(2,1)S(1)} %get-tuple-element.38.top), channel_id=1, source_target_pairs={{0,3},{1,0},{2,1},{3,2},{4,7},{5,4},{6,5},{7,6},{8,11},{9,8},{10,9... | collective-permute-start | bytes 737288 | tf_op jit(solution)/shard_map/ppermute | solution.py:37
  135.6 9.4 %collective-permute-start.19 = (bf16[192,640]{1,0:T(8,128)(2,1)S(1)}, bf16[192,640]{1,0:T(8,128)(2,1)S(1)}, u32[]{:S(2)}, u32[]{:S(2)}) collective-permute-start(bf16[192,640]{1,0:T(8,128)(2,1)S(1)} %collective-permute-done.15.below_top), channel_id=1, source_target_pairs={{0,1},{1,2},{2,3},{3,0},{4,5},{5,6},{6,7},{7,4},{8,9},{9,10},{10,1... | collective-permute-start | bytes 737288 | tf_op jit(solution)/shard_map/ppermute | solution.py:37
  135.8 9.3 %collective-permute-start.20 = (bf16[192,640]{1,0:T(8,128)(2,1)S(1)}, bf16[192,640]{1,0:T(8,128)(2,1)S(1)}, u32[]{:S(2)}, u32[]{:S(2)}) collective-permute-start(bf16[192,640]{1,0:T(8,128)(2,1)S(1)} %collective-permute-done.18.above_bottom), channel_id=1, source_target_pairs={{0,3},{1,0},{2,1},{3,2},{4,7},{5,4},{6,5},{7,6},{8,11},{9,8},{10,9... | collective-permute-start | bytes 737288 | tf_op jit(solution)/shard_map/ppermute | solution.py:37
  147.0 8.1 %all-to-all-start.2 = ((f32[4,8,384]{2,1,0:T(8,128)}), f32[4,8,384]{2,1,0:T(8,128)S(1)}, u32[]{:S(2)}, u32[]{:S(2)}) async-start(f32[4,8,384]{2,1,0:T(8,128)} %get-tuple-element.47), calls=%async_computation.2 | async-start | bytes 98304 | tf_op jit(solution)/shard_map/all_to_all | solution.py:434
  156.4 17.2 %all-to-all-start.3 = ((f32[64,1,128]{2,1,0:T(1,128)}), f32[64,1,128]{2,1,0:T(1,128)S(1)}, u32[]{:S(2)}, u32[]{:S(2)}) async-start(f32[64,1,128]{2,1,0:T(1,128)} %bitcast.18), calls=%async_computation.3 | async-start | bytes 65536 | tf_op jit(solution)/shard_map/all_to_all | solution.py:447
  (11 other events, 44.6 us)
Sparse Core Ops, SparseCore 0:
  15.0 100.3 all-gather.2

commit v6 on v5

--- a/solution.py
+++ b/solution.py
@@ -222,7 +222,7 @@
     resid_out[...] = resid.astype(BF16)
     squares = jnp.sum(resid * resid, axis=-1, keepdims=True)
     products = jnp.sum(resid * gain[...] * head[...], axis=-1, keepdims=True)
-    both = jnp.where(lane == 0, squares, products).T[:8, :]
+    both = jnp.where(lane == 0, squares, products).T[:2, :]
     for at in range(T):
         stats_out[at] = both
 
@@ -426,7 +426,7 @@
         out_last_kernel,
         [tokens, total, far_top, far_bottom, w_far, final_gain[None, :], critic_head[None, :]],
         "vvvvvvv",
-        [jax.ShapeDtypeStruct((ROWS, PIECE), BF16), jax.ShapeDtypeStruct((T, 8, ROWS), F32)],
+        [jax.ShapeDtypeStruct((ROWS, PIECE), BF16), jax.ShapeDtypeStruct((T, 2, ROWS), F32)],
         "out_last",
         flops,
         6 * MIB,

time: 182 us -> 182 us (level)
  no operation moved by 1% of the time
where the time goes in v6:
time: 182 us; the launch traced here: 181 us
  starting transfers between devices  56 us (31%)
  waiting for transfers between devices  47.5 us (26%)
  Pallas kernels  28.3 us (16%)
  blocking collectives  20.6 us (11%)
  between operations  15.2 us (8%)
  local copies, waits for them, and re-layouts  7.16 us (4%)
  other arithmetic  6.4 us (4%)
    pallas_call x9, Pallas kernels, local_call(): pl.pallas_call(kernel, in_specs=[pl.BlockSpec(memory_space=spaces[p]) for...  28.3 us
    all_to_all x1, blocking collectives, gather_by_all_to_all(): return lax.all_to_all(everywhere, axis, 0, 0, axis_index_groups=groups)  20.6 us
    ppermute x10, starting transfers between devices, shift_tp(): lax.ppermute(block, 'tp', [(i, (i + distance) % T) for i in range(T)])  17.6 us
    ppermute x7, starting transfers between devices, broadcast_anchor(): got = lax.ppermute(block, 'ctx', pairs)  13.3 us
    ppermute x10, waiting for transfers between devices, shift_tp(): lax.ppermute(block, 'tp', [(i, (i + distance) % T) for i in range(T)])  12.3 us
    all_gather x1, waiting for transfers between devices, on_device(): weights = lax.all_gather(both, 'ctx')  9.21 us
    all_to_all x1, waiting for transfers between devices, on_device(): records = lax.all_to_all(records, 'ctx', 0, 0, tiled=True)  8.69 us
    all_to_all x1, starting transfers between devices, on_device(): records = lax.all_to_all(records, 'ctx', 0, 0, tiled=True)  7.95 us
  transfers between devices with their start and end apart: 25, of which 17 were waited for; matrix products, arithmetic and copies ran while one was open for 6% of the time, Pallas kernels for 7%

profile of v6, /device:TPU:1, one launch (start us, length us, event | category | flops | bytes accessed | tf_op | source)
XLA Modules:
  0.0 181.1 jit_solution(13151939114946077017)
XLA Ops:
  7.2 3.7 %collective-permute-start.4 = (bf16[80,640]{1,0:T(8,128)(2,1)}, bf16[80,640]{1,0:T(8,128)(2,1)S(1)}, u32[]{:S(2)}, u32[]{:S(2)}) collective-permute-start(bf16[80,640]{1,0:T(8,128)(2,1)} %bitcast.34), channel_id=1, source_target_pairs={{0,128},{1,192},{2,0},{3,64},{4,132},{5,196},{6,4},{7,68},{8,136},... | collective-permute-start | bytes 307208 | tf_op jit(solution)/shard_map/ppermute | solution.py:352
  10.9 2.4 %collective-permute-done.4.first = bf16[80,640]{1,0:T(8,128)(2,1)S(1)} collective-permute-done((bf16[80,640]{1,0:T(8,128)(2,1)}, bf16[80,640]{1,0:T(8,128)(2,1)S(1)}, u32[]{:S(2)}, u32[]{:S(2)}) %collective-permute-start.4) | collective-permute-done | bytes 102432 | tf_op jit(solution)/shard_map/ppermute | solution.py:352
  14.9 3.1 %collective-permute-start = (bf16[384,1280]{1,0:T(8,128)(2,1)}, bf16[384,1280]{1,0:T(8,128)(2,1)S(1)}, u32[]{:S(2)}, u32[]{:S(2)}) collective-permute-start(bf16[384,1280]{1,0:T(8,128)(2,1)} %tokens.1), channel_id=1, source_target_pairs={{0,1},{1,2},{2,3},{3,0},{4,5},{5,6},{6,7},{7,4},{8,9},{9,10},{10,1... | collective-permute-start | bytes 2949128 | tf_op jit(solution)/shard_map/ppermute | solution.py:37
  18.0 3.5 %collective-permute-start.1 = (bf16[384,1280]{1,0:T(8,128)(2,1)}, bf16[384,1280]{1,0:T(8,128)(2,1)}, u32[]{:S(2)}, u32[]{:S(2)}) collective-permute-start(bf16[384,1280]{1,0:T(8,128)(2,1)} %tokens.1), channel_id=1, source_target_pairs={{0,3},{1,0},{2,1},{3,2},{4,7},{5,4},{6,5},{7,6},{8,11},{9,8},{10,9... | collective-permute-start | bytes 2949128 | tf_op jit(solution)/shard_map/ppermute | solution.py:37
  22.3 20.6 %all_to_all.26 = bf16[8,80,256]{2,1,0:T(8,128)(2,1)S(1)} all-to-all(bf16[8,80,256]{2,1,0:T(8,128)(2,1)S(1)} %broadcast_in_dim.63), channel_id=1, replica_groups={{0,8,16,24,32,40,48,56},{4,12,20,28,36,44,52,60},{64,72,80,88,96,104,11..., dimensions={0} | all-to-all | bytes 655360 | tf_op jit(solution)/shard_map/all_to_all | solution.py:281
  44.6 3.5 %all-to-all-start.1 = ((bf16[4,8,80,256]{3,2,1,0:T(8,128)(2,1)}), bf16[4,8,80,256]{3,2,1,0:T(8,128)(2,1)S(1)}, u32[]{:S(2)}, u32[]{:S(2)}) async-start(bf16[4,8,80,256]{3,2,1,0:T(8,128)(2,1)} %broadcast_in_dim.64), calls=%async_computation.1 | async-start | bytes 2621440 | tf_op jit(solution)/shard_map/all_to_all | solution.py:281
  50.0 2.2 %collective-permute-start.3 = (bf16[192,1280]{1,0:T(8,128)(2,1)S(1)}, bf16[192,1280]{1,0:T(8,128)(2,1)S(1)}, u32[]{:S(2)}, u32[]{:S(2)}) collective-permute-start(bf16[192,1280]{1,0:T(8,128)(2,1)S(1)} %slice.43), channel_id=1, source_target_pairs={{0,3},{1,0},{2,1},{3,2},{4,7},{5,4},{6,5},{7,6},{8,11},{9,8},{10,9... | collective-permute-start | bytes 1474568 | tf_op jit(solution)/shard_map/ppermute | solution.py:37
  52.1 6.6 %collective-permute-done.2.first = bf16[192,1280]{1,0:T(8,128)(2,1)S(1)} collective-permute-done((bf16[192,1280]{1,0:T(8,128)(2,1)S(1)}, bf16[192,1280]{1,0:T(8,128)(2,1)S(1)}, u32[]{:S(2)}, u32[]{:S(2)}) %collective-permute-start.2) | collective-permute-done | bytes 491552 | tf_op jit(solution)/shard_map/ppermute | solution.py:37
  60.6 1.7 all-to-all-done.1.w_own
  62.3 4.7 %collective-permute-start.5 = (bf16[4,8,80,256]{3,2,1,0:T(8,128)(2,1)S(1)}, bf16[4,8,80,256]{3,2,1,0:T(8,128)(2,1)}, u32[]{:S(2)}, u32[]{:S(2)}) collective-permute-start(bf16[4,8,80,256]{3,2,1,0:T(8,128)(2,1)S(1)} %all-to-all-done.1.w_own), channel_id=1, source_target_pairs={{0,4},{4,0},{8,12},{12,8},{16,20},{20,16},{24,28},{28,24},{32,36},... | collective-permute-start | bytes 3932168 | tf_op jit(solution)/shard_map/ppermute | solution.py:289
  68.2 2.9 %norm.1.normed = bf16[4,384,1280]{2,1,0:T(8,128)(2,1)S(1)} custom-call(s32[5]{0:T(128)S(1)} %stack.24.order, bf16[384,1280]{1,0:T(8,128)(2,1)S(1)} %copy-done.1, bf16[384,1280]{1,0:T(8,128)(2,1)S(1)} %collective-permute-done.below, bf16[384,1280]{1,0:T(8,128)(2,1)} %collective-permute-done.1.above, bf16[192,1280]{1,0:T(8,128)(2,1)S(1)} %copy-done.5, ...), custom_call_target="tpu_custom_call" | custom-call | flops 11796480 | bytes 7864320 | tf_op jit(solution)/shard_map/norm/pallas_call | solution.py:42
  71.3 4.6 %project_kv.1 = (bf16[384,128]{1,0:T(8,128)(2,1)S(1)}, bf16[384,128]{1,0:T(8,128)(2,1)S(1)}, s32[1,384]{1,0:T(1,128)S(1)}) custom-call(s32[5]{0:T(128)S(1)} %stack.24.order, bf16[4,384,1280]{2,1,0:T(8,128)(2,1)S(1)} %norm.1.normed, bf16[4,8,80,256]{3,2,1,0:T(8,128)(2,1)S(1)} %all-to-all-done.1.w_own, bf16[4,8,80,256]{3,2,1,0:T(8,128)(2,1)} %collective-permute-done.5.w_other, ...), custom_call_target="tpu_custom_call" | custom-call | flops 1006632960 | bytes 6553600 | tf_op jit(solution)/shard_map/project_kv/pallas_call | solution.py:42
  80.0 2.8 %collective-permute-start.7 = (bf16[384,128]{1,0:T(8,128)(2,1)S(1)}, bf16[384,128]{1,0:T(8,128)(2,1)S(1)}, u32[]{:S(2)}, u32[]{:S(2)}) collective-permute-start(bf16[384,128]{1,0:T(8,128)(2,1)S(1)} %broadcast_select_fusion), channel_id=1, source_target_pairs={{0,64},{4,20},{1,65},{5,21},{2,66},{6,22},{3,67},{7,23}} | collective-permute-start | bytes 294920 | tf_op jit(solution)/shard_map/ppermute | solution.py:317
  82.8 3.7 %collective-permute-start.8 = (bf16[384,128]{1,0:T(8,128)(2,1)S(1)}, bf16[384,128]{1,0:T(8,128)(2,1)S(1)}, u32[]{:S(2)}, u32[]{:S(2)}) collective-permute-start(bf16[384,128]{1,0:T(8,128)(2,1)S(1)} %broadcast_select_fusion), channel_id=1, source_target_pairs={{0,192},{4,52},{1,193},{5,53},{2,194},{6,54},{3,195},{7,55}} | collective-permute-start | bytes 294920 | tf_op jit(solution)/shard_map/ppermute | solution.py:317
  86.6 1.6 collective-permute-start.9
  89.2 1.8 collective-permute-done.9
  97.2 1.9 %collective-permute-done.12 = bf16[384,128]{1,0:T(8,128)(2,1)S(1)} collective-permute-done((bf16[384,128]{1,0:T(8,128)(2,1)S(1)}, bf16[384,128]{1,0:T(8,128)(2,1)S(1)}, u32[]{:S(2)}, u32[]{:S(2)}) %collective-permute-start.12) | collective-permute-done | bytes 98336 | tf_op jit(solution)/shard_map/ppermute | solution.py:317
  102.3 2.3 %collective-permute-done.13 = bf16[384,128]{1,0:T(8,128)(2,1)S(1)} collective-permute-done((bf16[384,128]{1,0:T(8,128)(2,1)S(1)}, bf16[384,128]{1,0:T(8,128)(2,1)S(1)}, u32[]{:S(2)}, u32[]{:S(2)}) %collective-permute-start.13) | collective-permute-done | bytes 98336 | tf_op jit(solution)/shard_map/ppermute | solution.py:317
  106.2 9.2 %all-gather.3.cloned.1.call-done = bf16[128,80,640]{2,1,0:T(8,128)(2,1)} async-done(((bf16[2,80,640]{2,1,0:T(8,128)(2,1)}), bf16[128,80,640]{2,1,0:T(8,128)(2,1)}) %all-gather.3.cloned.1.call-update) | async-done | bytes 13107216 | tf_op jit(solution)/shard_map/all_gather | solution.py:356
  115.4 10.7 %attend.1 = (bf16[192,640]{1,0:T(8,128)(2,1)S(1)}, bf16[192,640]{1,0:T(8,128)(2,1)S(1)}) custom-call(s32[5]{0:T(128)S(1)} %stack.24.order, s32[1]{0:T(128)} %bitcast.5.index, bf16[4,384,1280]{2,1,0:T(8,128)(2,1)} %copy-done, bf16[64,2,80,640]{3,2,1,0:T(8,128)(2,1)} %bitcast.30, f32[384,128]{1,0:T(8,128)S(1)} %get-tuple-element.60.cosine, ...), custom_call_target="tpu_custom_call" | custom-call | flops 3271557120 | bytes 10485760 | tf_op jit(solution)/shard_map/attend/pallas_call | solution.py:42
  127.1 1.7 collective-permute-start.18
  128.9 2.7 %collective-permute-start.17 = (bf16[192,640]{1,0:T(8,128)(2,1)S(1)}, bf16[192,640]{1,0:T(8,128)(2,1)S(1)}, u32[]{:S(2)}, u32[]{:S(2)}) collective-permute-start(bf16[192,640]{1,0:T(8,128)(2,1)S(1)} %get-tuple-element.38.top), channel_id=1, source_target_pairs={{0,3},{1,0},{2,1},{3,2},{4,7},{5,4},{6,5},{7,6},{8,11},{9,8},{10,9... | collective-permute-start | bytes 737288 | tf_op jit(solution)/shard_map/ppermute | solution.py:37
  131.6 4.1 %out_own.1 = (f32[384,1280]{1,0:T(8,128)S(1)}, bf16[16,80,640]{2,1,0:T(8,128)(2,1)S(1)}, bf16[16,80,640]{2,1,0:T(8,128)(2,1)S(1)}, bf16[16,80,640]{2,1,0:T(8,128)(2,1)S(1)}) custom-call(s32[5]{0:T(128)S(1)} %stack.24.order, bf16[192,640]{1,0:T(8,128)(2,1)S(1)} %get-tuple-element.38.top, bf16[192,640]{1,0:T(8,128)(2,1)S(1)} %get-tuple-element.39.bottom, ...), custom_call_target="tpu_custom_call" | custom-call | flops 629145600 | bytes 8388608 | tf_op jit(solution)/shard_map/out_own/pallas_call | solution.py:42
  135.8 2.7 %collective-permute-start.20 = (bf16[192,640]{1,0:T(8,128)(2,1)S(1)}, bf16[192,640]{1,0:T(8,128)(2,1)S(1)}, u32[]{:S(2)}, u32[]{:S(2)}) collective-permute-start(bf16[192,640]{1,0:T(8,128)(2,1)S(1)} %collective-permute-done.18.above_bottom), channel_id=1, source_target_pairs={{0,3},{1,0},{2,1},{3,2},{4,7},{5,4},{6,5},{7,6},{8,11},{9,8},{10,9... | collective-permute-start | bytes 737288 | tf_op jit(solution)/shard_map/ppermute | solution.py:37
  138.4 1.6 collective-permute-done.16.below_bottom
  140.0 1.7 out_next.1.total
  141.7 3.3 %collective-permute-done.19.top = bf16[192,640]{1,0:T(8,128)(2,1)S(1)} collective-permute-done((bf16[192,640]{1,0:T(8,128)(2,1)S(1)}, bf16[192,640]{1,0:T(8,128)(2,1)S(1)}, u32[]{:S(2)}, u32[]{:S(2)}) %collective-permute-start.19) | collective-permute-done | bytes 245792 | tf_op jit(solution)/shard_map/ppermute | solution.py:37
  145.0 2.0 %out_last.1 = (bf16[384,1280]{1,0:T(8,128)(2,1)}, f32[4,2,384]{2,1,0:T(2,128)}) custom-call(bf16[384,1280]{1,0:T(8,128)(2,1)S(1)} %copy-done.1, f32[384,1280]{1,0:T(8,128)S(1)} %out_next.1.total, bf16[192,640]{1,0:T(8,128)(2,1)S(1)} %collective-permute-done.19.top, bf16[192,640]{1,0:T(8,128)(2,1)S(1)} %collective-permute-done.20.bottom, ...), custom_call_target="tpu_custom_call" | custom-call | flops 629145600 | bytes 6291456 | tf_op jit(solution)/shard_map/out_last/pallas_call | solution.py:42
  147.0 3.7 %all-to-all-start.2 = ((f32[4,2,384]{2,1,0:T(2,128)}), f32[4,2,384]{2,1,0:T(2,128)S(1)}, u32[]{:S(2)}, u32[]{:S(2)}) async-start(f32[4,2,384]{2,1,0:T(2,128)} %get-tuple-element.47), calls=%async_computation.2 | async-start | bytes 24576 | tf_op jit(solution)/shard_map/all_to_all | solution.py:434
  151.4 3.5 %all-to-all-done.2.stats = f32[4,2,384]{2,1,0:T(2,128)S(1)} async-done(((f32[4,2,384]{2,1,0:T(2,128)}), f32[4,2,384]{2,1,0:T(2,128)S(1)}, u32[]{:S(2)}, u32[]{:S(2)}) %all-to-all-start.2) | async-done | bytes 12320 | tf_op jit(solution)/shard_map/all_to_all | solution.py:434
  156.2 8.0 %all-to-all-start.3 = ((f32[64,1,128]{2,1,0:T(1,128)}), f32[64,1,128]{2,1,0:T(1,128)S(1)}, u32[]{:S(2)}, u32[]{:S(2)}) async-start(f32[64,1,128]{2,1,0:T(1,128)} %bitcast.18), calls=%async_computation.3 | async-start | bytes 65536 | tf_op jit(solution)/shard_map/all_to_all | solution.py:447
  164.8 8.7 %all-to-all-done.3 = f32[64,1,128]{2,1,0:T(1,128)S(1)} async-done(((f32[64,1,128]{2,1,0:T(1,128)}), f32[64,1,128]{2,1,0:T(1,128)S(1)}, u32[]{:S(2)}, u32[]{:S(2)}) %all-to-all-start.3) | async-done | bytes 32800 | tf_op jit(solution)/shard_map/all_to_all | solution.py:447
  (110 shorter events, 28.8 us)
Async XLA Ops:
  7.2 108.2 %all-gather.3.cloned.1.call-start = ((), (), s32[]{:S(2)}) async-start(), calls=%async_computation.4 | async-start | bytes 13312000 | tf_op jit(solution)/shard_map/all_gather | solution.py:356
  7.2 6.1 %collective-permute-start.4 = (bf16[80,640]{1,0:T(8,128)(2,1)}, bf16[80,640]{1,0:T(8,128)(2,1)S(1)}, u32[]{:S(2)}, u32[]{:S(2)}) collective-permute-start(bf16[80,640]{1,0:T(8,128)(2,1)} %bitcast.34), channel_id=1, source_target_pairs={{0,128},{1,192},{2,0},{3,64},{4,132},{5,196},{6,4},{7,68},{8,136},... | collective-permute-start | bytes 307208 | tf_op jit(solution)/shard_map/ppermute | solution.py:352
  14.9 28.5 %collective-permute-start = (bf16[384,1280]{1,0:T(8,128)(2,1)}, bf16[384,1280]{1,0:T(8,128)(2,1)S(1)}, u32[]{:S(2)}, u32[]{:S(2)}) collective-permute-start(bf16[384,1280]{1,0:T(8,128)(2,1)} %tokens.1), channel_id=1, source_target_pairs={{0,1},{1,2},{2,3},{3,0},{4,5},{5,6},{6,7},{7,4},{8,9},{9,10},{10,1... | collective-permute-start | bytes 2949128 | tf_op jit(solution)/shard_map/ppermute | solution.py:37
  18.0 25.4 %collective-permute-start.1 = (bf16[384,1280]{1,0:T(8,128)(2,1)}, bf16[384,1280]{1,0:T(8,128)(2,1)}, u32[]{:S(2)}, u32[]{:S(2)}) collective-permute-start(bf16[384,1280]{1,0:T(8,128)(2,1)} %tokens.1), channel_id=1, source_target_pairs={{0,3},{1,0},{2,1},{3,2},{4,7},{5,4},{6,5},{7,6},{8,11},{9,8},{10,9... | collective-permute-start | bytes 2949128 | tf_op jit(solution)/shard_map/ppermute | solution.py:37
  44.6 17.7 %all-to-all-start.1 = ((bf16[4,8,80,256]{3,2,1,0:T(8,128)(2,1)}), bf16[4,8,80,256]{3,2,1,0:T(8,128)(2,1)S(1)}, u32[]{:S(2)}, u32[]{:S(2)}) async-start(bf16[4,8,80,256]{3,2,1,0:T(8,128)(2,1)} %broadcast_in_dim.64), calls=%async_computation.1 | async-start | bytes 2621440 | tf_op jit(solution)/shard_map/all_to_all | solution.py:281
  48.1 18.8 %copy-start.14 = (f32[640]{0:T(1024)S(1)}, f32[640]{0:T(1024)}, u32[]{:S(2)}) copy-start(f32[640]{0:T(1024)} %param.20) | copy-start | bytes 7684
  48.2 18.9 %copy-start.16 = (f32[128]{0:T(128)S(1)}, f32[128]{0:T(128)}, u32[]{:S(2)}) copy-start(f32[128]{0:T(128)} %param.22) | copy-start | bytes 1540
  48.2 18.9 %copy-start.17 = (f32[128]{0:T(128)S(1)}, f32[128]{0:T(128)}, u32[]{:S(2)}) copy-start(f32[128]{0:T(128)} %param.21) | copy-start | bytes 1540
  48.2 19.9 %copy-start.1 = (bf16[384,1280]{1,0:T(8,128)(2,1)S(1)}, bf16[384,1280]{1,0:T(8,128)(2,1)}, u32[]{:S(2)}) copy-start(bf16[384,1280]{1,0:T(8,128)(2,1)} %tokens.1) | copy-start | bytes 2949124
  48.2 19.9 %copy-start.9 = (f32[5120]{0:T(1024)S(1)}, f32[5120]{0:T(1024)}, u32[]{:S(2)}) copy-start(f32[5120]{0:T(1024)} %param.16) | copy-start | bytes 61444
  48.2 10.5 %collective-permute-start.2 = (bf16[192,1280]{1,0:T(8,128)(2,1)S(1)}, bf16[192,1280]{1,0:T(8,128)(2,1)S(1)}, u32[]{:S(2)}, u32[]{:S(2)}) collective-permute-start(bf16[192,1280]{1,0:T(8,128)(2,1)S(1)} %slice.42), channel_id=1, source_target_pairs={{0,1},{1,2},{2,3},{3,0},{4,5},{5,6},{6,7},{7,4},{8,9},{9,10},{10,1... | collective-permute-start | bytes 1474568 | tf_op jit(solution)/shard_map/ppermute | solution.py:37
  50.0 9.8 %collective-permute-start.3 = (bf16[192,1280]{1,0:T(8,128)(2,1)S(1)}, bf16[192,1280]{1,0:T(8,128)(2,1)S(1)}, u32[]{:S(2)}, u32[]{:S(2)}) collective-permute-start(bf16[192,1280]{1,0:T(8,128)(2,1)S(1)} %slice.43), channel_id=1, source_target_pairs={{0,3},{1,0},{2,1},{3,2},{4,7},{5,4},{6,5},{7,6},{8,11},{9,8},{10,9... | collective-permute-start | bytes 1474568 | tf_op jit(solution)/shard_map/ppermute | solution.py:37
  62.3 8.9 %collective-permute-start.5 = (bf16[4,8,80,256]{3,2,1,0:T(8,128)(2,1)S(1)}, bf16[4,8,80,256]{3,2,1,0:T(8,128)(2,1)}, u32[]{:S(2)}, u32[]{:S(2)}) collective-permute-start(bf16[4,8,80,256]{3,2,1,0:T(8,128)(2,1)S(1)} %all-to-all-done.1.w_own), channel_id=1, source_target_pairs={{0,4},{4,0},{8,12},{12,8},{16,20},{20,16},{24,28},{28,24},{32,36},... | collective-permute-start | bytes 3932168 | tf_op jit(solution)/shard_map/ppermute | solution.py:289
  71.2 23.7 %copy-start.15 = (s32[384]{0:T(512)S(1)}, s32[384]{0:T(512)}, u32[]{:S(2)}) copy-start(s32[384]{0:T(512)} %param.27) | copy-start | bytes 4612
  75.9 39.5 %copy-start.3 = (f32[384,128]{1,0:T(8,128)S(1)}, f32[384,128]{1,0:T(8,128)}, u32[]{:S(2)}) copy-start(f32[384,128]{1,0:T(8,128)} %copy-done.2) | copy-start | bytes 589828
  76.8 3.2 %collective-permute-start.6 = (bf16[384,128]{1,0:T(8,128)(2,1)S(1)}, bf16[384,128]{1,0:T(8,128)(2,1)S(1)}, u32[]{:S(2)}, u32[]{:S(2)}) collective-permute-start(bf16[384,128]{1,0:T(8,128)(2,1)S(1)} %get-tuple-element.35.value), channel_id=1, source_target_pairs={{0,4},{1,5},{2,6},{3,7}} | collective-permute-start | bytes 294920 | tf_op jit(solution)/shard_map/ppermute | solution.py:301
  80.0 8.4 %collective-permute-start.7 = (bf16[384,128]{1,0:T(8,128)(2,1)S(1)}, bf16[384,128]{1,0:T(8,128)(2,1)S(1)}, u32[]{:S(2)}, u32[]{:S(2)}) collective-permute-start(bf16[384,128]{1,0:T(8,128)(2,1)S(1)} %broadcast_select_fusion), channel_id=1, source_target_pairs={{0,64},{4,20},{1,65},{5,21},{2,66},{6,22},{3,67},{7,23}} | collective-permute-start | bytes 294920 | tf_op jit(solution)/shard_map/ppermute | solution.py:317
  82.8 6.4 %collective-permute-start.8 = (bf16[384,128]{1,0:T(8,128)(2,1)S(1)}, bf16[384,128]{1,0:T(8,128)(2,1)S(1)}, u32[]{:S(2)}, u32[]{:S(2)}) collective-permute-start(bf16[384,128]{1,0:T(8,128)(2,1)S(1)} %broadcast_select_fusion), channel_id=1, source_target_pairs={{0,192},{4,52},{1,193},{5,53},{2,194},{6,54},{3,195},{7,55}} | collective-permute-start | bytes 294920 | tf_op jit(solution)/shard_map/ppermute | solution.py:317
  86.6 4.4 %collective-permute-start.9 = (bf16[384,128]{1,0:T(8,128)(2,1)S(1)}, bf16[384,128]{1,0:T(8,128)(2,1)S(1)}, u32[]{:S(2)}, u32[]{:S(2)}) collective-permute-start(bf16[384,128]{1,0:T(8,128)(2,1)S(1)} %broadcast_select_fusion), channel_id=1, source_target_pairs={{0,128},{4,36},{1,129},{5,37},{2,130},{6,38},{3,131},{7,39}} | collective-permute-start | bytes 294920 | tf_op jit(solution)/shard_map/ppermute | solution.py:317
  91.0 5.1 %collective-permute-start.10 = (bf16[384,128]{1,0:T(8,128)(2,1)S(1)}, bf16[384,128]{1,0:T(8,128)(2,1)S(1)}, u32[]{:S(2)}, u32[]{:S(2)}) collective-permute-start(bf16[384,128]{1,0:T(8,128)(2,1)S(1)} %add_select_fusion.1), channel_id=1, source_target_pairs={{0,16},{64,80},{192,208},{128,144},{4,68},{20,84},{52,116},{36,100... | collective-permute-start | bytes 294920 | tf_op jit(solution)/shard_map/ppermute | solution.py:317
  92.3 4.9 %collective-permute-start.11 = (bf16[384,128]{1,0:T(8,128)(2,1)S(1)}, bf16[384,128]{1,0:T(8,128)(2,1)S(1)}, u32[]{:S(2)}, u32[]{:S(2)}) collective-permute-start(bf16[384,128]{1,0:T(8,128)(2,1)S(1)} %add_select_fusion.1), channel_id=1, source_target_pairs={{0,48},{64,112},{192,240},{128,176},{4,196},{20,212},{52,244},{36,... | collective-permute-start | bytes 294920 | tf_op jit(solution)/shard_map/ppermute | solution.py:317
  93.6 5.5 %collective-permute-start.12 = (bf16[384,128]{1,0:T(8,128)(2,1)S(1)}, bf16[384,128]{1,0:T(8,128)(2,1)S(1)}, u32[]{:S(2)}, u32[]{:S(2)}) collective-permute-start(bf16[384,128]{1,0:T(8,128)(2,1)S(1)} %add_select_fusion.1), channel_id=1, source_target_pairs={{0,32},{64,96},{192,224},{128,160},{4,132},{20,148},{52,180},{36,1... | collective-permute-start | bytes 294920 | tf_op jit(solution)/shard_map/ppermute | solution.py:317
  99.1 5.5 %collective-permute-start.13 = (bf16[384,128]{1,0:T(8,128)(2,1)S(1)}, bf16[384,128]{1,0:T(8,128)(2,1)S(1)}, u32[]{:S(2)}, u32[]{:S(2)}) collective-permute-start(bf16[384,128]{1,0:T(8,128)(2,1)S(1)} %add_select_fusion), channel_id=1, source_target_pairs={{0,8},{64,72},{192,200},{128,136},{16,24},{80,88},{208,216},{144,1... | collective-permute-start | bytes 294920 | tf_op jit(solution)/shard_map/ppermute | solution.py:317
  104.6 1.6 collective-permute-start.14
  126.1 9.5 %collective-permute-start.15 = (bf16[192,640]{1,0:T(8,128)(2,1)S(1)}, bf16[192,640]{1,0:T(8,128)(2,1)S(1)}, u32[]{:S(2)}, u32[]{:S(2)}) collective-permute-start(bf16[192,640]{1,0:T(8,128)(2,1)S(1)} %get-tuple-element.38.top), channel_id=1, source_target_pairs={{0,1},{1,2},{2,3},{3,0},{4,5},{5,6},{6,7},{7,4},{8,9},{9,10},{10,1... | collective-permute-start | bytes 737288 | tf_op jit(solution)/shard_map/ppermute | solution.py:37
  127.1 8.6 %collective-permute-start.18 = (bf16[192,640]{1,0:T(8,128)(2,1)S(1)}, bf16[192,640]{1,0:T(8,128)(2,1)S(1)}, u32[]{:S(2)}, u32[]{:S(2)}) collective-permute-start(bf16[192,640]{1,0:T(8,128)(2,1)S(1)} %get-tuple-element.39.bottom), channel_id=1, source_target_pairs={{0,3},{1,0},{2,1},{3,2},{4,7},{5,4},{6,5},{7,6},{8,11},{9,8},{10,9... | collective-permute-start | bytes 737288 | tf_op jit(solution)/shard_map/ppermute | solution.py:37
  128.9 11.1 %collective-permute-start.16 = (bf16[192,640]{1,0:T(8,128)(2,1)S(1)}, bf16[192,640]{1,0:T(8,128)(2,1)S(1)}, u32[]{:S(2)}, u32[]{:S(2)}) collective-permute-start(bf16[192,640]{1,0:T(8,128)(2,1)S(1)} %get-tuple-element.39.bottom), channel_id=1, source_target_pairs={{0,1},{1,2},{2,3},{3,0},{4,5},{5,6},{6,7},{7,4},{8,9},{9,10},{10,1... | collective-permute-start | bytes 737288 | tf_op jit(solution)/shard_map/ppermute | solution.py:37
  128.9 11.1 %collective-permute-start.17 = (bf16[192,640]{1,0:T(8,128)(2,1)S(1)}, bf16[192,640]{1,0:T(8,128)(2,1)S(1)}, u32[]{:S(2)}, u32[]{:S(2)}) collective-permute-start(bf16[192,640]{1,0:T(8,128)(2,1)S(1)} %get-tuple-element.38.top), channel_id=1, source_target_pairs={{0,3},{1,0},{2,1},{3,2},{4,7},{5,4},{6,5},{7,6},{8,11},{9,8},{10,9... | collective-permute-start | bytes 737288 | tf_op jit(solution)/shard_map/ppermute | solution.py:37
  135.6 9.4 %collective-permute-start.19 = (bf16[192,640]{1,0:T(8,128)(2,1)S(1)}, bf16[192,640]{1,0:T(8,128)(2,1)S(1)}, u32[]{:S(2)}, u32[]{:S(2)}) collective-permute-start(bf16[192,640]{1,0:T(8,128)(2,1)S(1)} %collective-permute-done.15.below_top), channel_id=1, source_target_pairs={{0,1},{1,2},{2,3},{3,0},{4,5},{5,6},{6,7},{7,4},{8,9},{9,10},{10,1... | collective-permute-start | bytes 737288 | tf_op jit(solution)/shard_map/ppermute | solution.py:37
  135.8 9.3 %collective-permute-start.20 = (bf16[192,640]{1,0:T(8,128)(2,1)S(1)}, bf16[192,640]{1,0:T(8,128)(2,1)S(1)}, u32[]{:S(2)}, u32[]{:S(2)}) collective-permute-start(bf16[192,640]{1,0:T(8,128)(2,1)S(1)} %collective-permute-done.18.above_bottom), channel_id=1, source_target_pairs={{0,3},{1,0},{2,1},{3,2},{4,7},{5,4},{6,5},{7,6},{8,11},{9,8},{10,9... | collective-permute-start | bytes 737288 | tf_op jit(solution)/shard_map/ppermute | solution.py:37
  147.0 7.9 %all-to-all-start.2 = ((f32[4,2,384]{2,1,0:T(2,128)}), f32[4,2,384]{2,1,0:T(2,128)S(1)}, u32[]{:S(2)}, u32[]{:S(2)}) async-start(f32[4,2,384]{2,1,0:T(2,128)} %get-tuple-element.47), calls=%async_computation.2 | async-start | bytes 24576 | tf_op jit(solution)/shard_map/all_to_all | solution.py:434
  156.2 17.2 %all-to-all-start.3 = ((f32[64,1,128]{2,1,0:T(1,128)}), f32[64,1,128]{2,1,0:T(1,128)S(1)}, u32[]{:S(2)}, u32[]{:S(2)}) async-start(f32[64,1,128]{2,1,0:T(1,128)} %bitcast.18), calls=%async_computation.3 | async-start | bytes 65536 | tf_op jit(solution)/shard_map/all_to_all | solution.py:447
  (11 other events, 44.6 us)
Sparse Core Ops, SparseCore 0:
  15.0 100.3 all-gather.2
